TPU v7x, 32 devices: a whole 2x2x4 slice. The times are simulated.
32 devices in a mesh: group: 4 (over y, x), member: 8 (over z, core).
Axes of the slice: x: 2, y: 2, z: 4, core: 2. Of those that a mesh axis runs over, the one named last changes fastest.
Arguments:
- points: bfloat16 [8192, 768], P(('group', 'member')), may hold values from -9 to 9
- centroids: bfloat16 [8192, 768], P('group'), may hold values from -5 to 5
- dest_group: int32 [8192, 1], P(('group', 'member')), may hold values from 0 to 3; in each aligned block of 256 rows (0 to 255, 256 to 511, ...) at most 64 rows name the same one
Outputs:
- refined: bfloat16 [8192, 768], P(('group', 'member'))
Inputs may be any that keep to these rules, and one draw needn't show every extreme that they name: `dest_group`: among the 256 rows of one device, at most 64 name the same group, a bound that some block reaches of them.
All inputs are finite; a program needn't handle non-finite values.
Results may differ from a plain program's by a relative error of at most 0.0025.
Values may be sent and summed in bfloat16 or wider, within the bound.
No kernel may reach another device: no remote copies, remote signals or barrier semaphores. Data moves between devices by JAX's collectives and lax.ppermute only.
A program may use at most 64 MiB of HBM per device.

v0:
```python
import jax
import jax.numpy as jnp
from jax import lax
from jax.sharding import PartitionSpec as P

score_scale = 0.15


def local(points, centroids, dest_group):
    group_count = lax.axis_size("group")
    member_count = lax.axis_size("member")
    point_rows = points.shape[0]
    capacity = point_rows // 4
    feature_dim = points.shape[1]
    fine_count = centroids.shape[0]
    destination = dest_group[:, 0]
    in_group = (destination[:, None] == jnp.arange(group_count, dtype=jnp.int32)[None, :]).astype(
        jnp.int32
    )
    earlier = jnp.cumsum(in_group, axis=0) - in_group
    own_rank = jnp.sum(earlier * in_group, axis=1)
    slot_index = destination * capacity + own_rank
    placement = (
        jnp.arange(group_count * capacity, dtype=jnp.int32)[:, None] == slot_index[None, :]
    ).astype(jnp.bfloat16)
    packed = jnp.dot(placement, points, preferred_element_type=jnp.float32).astype(jnp.bfloat16)
    packed = packed.reshape(group_count, capacity, feature_dim)
    slot_flags = jnp.dot(
        placement, jnp.ones((point_rows, 1), jnp.bfloat16), preferred_element_type=jnp.float32
    )
    slot_flags = slot_flags.astype(jnp.bfloat16).reshape(group_count, capacity, 1)
    centroid_f = centroids.astype(jnp.float32)
    centroid_norms = jnp.sum(centroid_f * centroid_f, axis=1)
    arrived, marks = (
        lax.all_to_all(packed, "group", split_axis=0, concat_axis=0, tiled=True),
        lax.all_to_all(slot_flags, "group", split_axis=0, concat_axis=0, tiled=True),
    )
    rows = arrived.reshape(-1, feature_dim)
    scores = score_scale * (
        jnp.dot(rows, centroids.T, preferred_element_type=jnp.float32)
        - 0.5 * centroid_norms[None, :]
    )
    weights = jax.nn.softmax(scores, axis=-1) * marks.reshape(-1, 1).astype(jnp.float32)
    responsibility = weights.astype(jnp.bfloat16).reshape(
        arrived.shape[0], arrived.shape[1], fine_count
    )
    all_rows = arrived.reshape(-1, feature_dim)
    all_weights = responsibility.reshape(-1, fine_count)
    weighted = jnp.dot(all_weights.T, all_rows, preferred_element_type=jnp.float32)
    soft_counts = jnp.dot(
        jnp.ones((1, all_weights.shape[0]), jnp.bfloat16),
        all_weights,
        preferred_element_type=jnp.float32,
    )[0]
    member_index = lax.axis_index("member")
    tile_sums, tile_counts = (
        lax.psum_scatter(weighted, "member", scatter_dimension=0, tiled=True),
        lax.psum_scatter(soft_counts, "member", scatter_dimension=0, tiled=True),
    )
    tile_rows = fine_count // member_count
    old_tile = lax.dynamic_slice_in_dim(centroid_f, member_index * tile_rows, tile_rows, 0)
    refined = ((tile_sums + old_tile) / (tile_counts + 1.0)[:, None]).astype(jnp.bfloat16)
    return refined


def solution(mesh):
    return jax.shard_map(
        local,
        mesh=mesh,
        in_specs=(P(("group", "member"), None), P("group", None), P(("group", "member"), None)),
        out_specs=P(("group", "member"), None),
        check_vma=False,
    )
```

profile of v0, /device:TPU:0, one launch (start us, length us, event | category | flops | bytes accessed | tf_op | source)
XLA Modules:
  0.0 118.7 jit_solution(6921389028984356215)
XLA Ops:
  6.5 0.0 copy-start
  6.5 0.7 compare_convert_fusion
  7.3 1.2 %reduce-window.6 = s32[4,2,128]{2,1,0:T(2,128)S(1)} reduce-window(s32[4,2,128]{2,1,0:T(2,128)S(1)} %compare_convert_fusion, s32[]{:T(128)} %constant.12.clone.1), window={size=1x1x128 pad=0_0x0_0x127_0}, to_apply=%region_0.0 | reduce-window | flops 130048 | bytes 8196 | tf_op jit(solution)/shard_map/reduce-window
  8.5 0.1 slice.8
  8.6 0.1 copy.8
  8.7 0.1 copy.9
  8.8 0.1 add_bitcast_fusion
  8.9 0.7 fusion.7
  9.6 0.7 multiply_add_fusion
  10.3 0.2 fusion.2
  10.4 0.7 reshape.67
  11.1 5.2 %all-to-all-start.1 = ((bf16[4,64,1]{1,2,0:T(2,128)(2,1)}), bf16[4,64,1]{1,2,0:T(2,128)(2,1)S(1)}, u32[]{:S(2)}, u32[]{:S(2)}) async-start(bf16[4,64,1]{1,2,0:T(2,128)(2,1)} %reshape.67), calls=%async_computation.1 | async-start | bytes 4096 | tf_op jit(solution)/shard_map/all_to_all | solution.py:36
  16.3 0.0 copy-start.1
  16.3 2.7 %multiply_reduce_fusion = f32[2048]{0:T(1024)S(1)} fusion(bf16[2048,768]{1,0:T(8,128)(2,1)} %param.4), kind=kLoop, calls=%fused_computation | loop fusion | flops 4716544 | bytes 3153920 | tf_op jit(solution)/shard_map/reduce_sum | solution.py:33
  19.0 0.0 copy-done
  19.0 1.0 convolution_convert_fusion
  20.1 0.7 all-to-all-done.1
  20.8 0.0 copy-start.2
  20.8 4.1 %all-to-all-start = ((bf16[4,64,768]{2,1,0:T(8,128)(2,1)}), bf16[4,64,768]{2,1,0:T(8,128)(2,1)}, u32[]{:S(2)}, u32[]{:S(2)}) async-start(bf16[4,64,768]{2,1,0:T(8,128)(2,1)} %bitcast.32), calls=%async_computation | async-start | bytes 786432 | tf_op jit(solution)/shard_map/all_to_all | solution.py:35
  24.9 0.0 copy-done.2
  24.9 0.0 reduce-scatter.2.cloned.1.call-start
  25.0 0.7 convert_reduce_fusion
  25.7 0.1 reshape.62
  25.8 5.1 %all-to-all-done = bf16[4,64,768]{2,1,0:T(8,128)(2,1)} async-done(((bf16[4,64,768]{2,1,0:T(8,128)(2,1)}), bf16[4,64,768]{2,1,0:T(8,128)(2,1)}, u32[]{:S(2)}, u32[]{:S(2)}) %all-to-all-start) | async-done | bytes 393248 | tf_op jit(solution)/shard_map/all_to_all | solution.py:35
  30.8 0.0 copy-done.1
  30.8 2.1 %fusion.13 = (f32[256]{0:T(256)S(1)}, f32[256,2048]{1,0:T(8,128)S(1)}) fusion(f32[2048]{0:T(1024)S(1)} %broadcast_multiply_fusion, bf16[256,768]{1,0:T(8,128)(2,1)} %bitcast.5, bf16[2048,768]{1,0:T(8,128)(2,1)S(1)} %copy-done.1), kind=kOutput, calls=%fused_computation.28 | convolution fusion | flops 806878976 | bytes 5645312 | tf_op jit(solution)/shard_map/dot_general | solution.py:40
  32.9 0.4 fusion.1
  33.4 0.6 multiply_convert_fusion
  34.0 4.7 %fusion.14 = f32[2048,768]{1,0:T(8,128)} fusion(bf16[256,2048]{1,0:T(8,128)(2,1)S(1)} %multiply_convert_fusion, bf16[256,768]{1,0:T(8,128)(2,1)} %bitcast.5), kind=kOutput, calls=%fused_computation.29 | convolution fusion | flops 805306368 | bytes 7733248 | tf_op jit(solution)/shard_map/dot_general | solution.py:49
  38.7 0.0 reduce-scatter.2.cloned.1.call-update
  38.7 0.0 copy-start.3
  38.7 5.0 %convert_element_type.38 = f32[2048,768]{1,0:T(8,128)} convert(bf16[2048,768]{1,0:T(8,128)(2,1)} %param.4) | non-fusion elementwise | flops 1572864 | bytes 9437184 | tf_op jit(solution)/shard_map/convert_element_type | solution.py:32
  43.7 0.0 copy-done.3
  43.7 0.6 dynamic-slice
  45.0 0.2 fusion.8
  45.2 15.8 %all-reduce = f32[2048]{0:T(1024)S(1)} all-reduce(f32[2048]{0:T(1024)S(1)} %bitcast.33), channel_id=3, replica_groups=mesh['group'=4,'member'=8] {'member'}, use_global_device_ids=true, to_apply=%region_7.8.clone | all-reduce | flops 2048 | bytes 16384
  61.0 0.1 dynamic-slice_add_fusion
  61.1 48.5 %reduce-scatter.2.cloned.1.call-done = f32[256,768]{1,0:T(8,128)} async-done(((f32[2048,768]{1,0:T(8,128)}), f32[256,768]{1,0:T(8,128)}) %reduce-scatter.2.cloned.1.call-update) | async-done | bytes 786448 | tf_op jit(solution)/shard_map/reduce_scatter | solution.py:57
  109.6 2.3 %divide_convert_fusion = bf16[256,768]{1,0:T(8,128)(2,1)} fusion(f32[256,768]{1,0:T(8,128)} %reduce-scatter.2.cloned.1.call-done, f32[2048,768]{1,0:T(8,128)} %convert_element_type.38, s32[]{:T(128)S(6)} %select_n.3, f32[256]{0:T(256)S(1)} %dynamic-slice_add_fusion), kind=kLoop, calls=%fused_computation.7 | loop fusion | flops 589824 | bytes 1967108 | tf_op jit(solution)/shard_map/convert_element_type | solution.py:62
  (4 shorter events, 0.1 us)
Async XLA Ops:
  6.5 12.5 %copy-start = (bf16[256,768]{1,0:T(8,128)(2,1)S(1)}, bf16[256,768]{1,0:T(8,128)(2,1)}, u32[]{:S(2)}) copy-start(bf16[256,768]{1,0:T(8,128)(2,1)} %param.3) | copy-start | bytes 1179652
  11.1 9.7 %all-to-all-start.1 = ((bf16[4,64,1]{1,2,0:T(2,128)(2,1)}), bf16[4,64,1]{1,2,0:T(2,128)(2,1)S(1)}, u32[]{:S(2)}, u32[]{:S(2)}) async-start(bf16[4,64,1]{1,2,0:T(2,128)(2,1)} %reshape.67), calls=%async_computation.1 | async-start | bytes 4096 | tf_op jit(solution)/shard_map/all_to_all | solution.py:36
  16.3 14.5 %copy-start.1 = (bf16[2048,768]{1,0:T(8,128)(2,1)S(1)}, bf16[2048,768]{1,0:T(8,128)(2,1)}, u32[]{:S(2)}) copy-start(bf16[2048,768]{1,0:T(8,128)(2,1)} %param.4) | copy-start | bytes 9437188
  20.8 4.1 %copy-start.2 = (bf16[4,64,1]{1,2,0:T(2,128)(2,1)}, bf16[4,64,1]{1,2,0:T(2,128)(2,1)S(1)}, u32[]{:S(2)}) copy-start(bf16[4,64,1]{1,2,0:T(2,128)(2,1)S(1)} %all-to-all-done.1) | copy-start | bytes 1540
  20.8 10.0 %all-to-all-start = ((bf16[4,64,768]{2,1,0:T(8,128)(2,1)}), bf16[4,64,768]{2,1,0:T(8,128)(2,1)}, u32[]{:S(2)}, u32[]{:S(2)}) async-start(bf16[4,64,768]{2,1,0:T(8,128)(2,1)} %bitcast.32), calls=%async_computation | async-start | bytes 786432 | tf_op jit(solution)/shard_map/all_to_all | solution.py:35
  24.9 84.7 %reduce-scatter.2.cloned.1.call-start = ((), (), s32[]{:S(2)}) async-start(), calls=%async_computation.3 | async-start | bytes 7077888 | tf_op jit(solution)/shard_map/reduce_scatter | solution.py:57
  38.7 5.1 %copy-start.3 = (u32[32]{0:T(128)S(1)}, u32[32]{0:T(128)}, u32[]{:S(2)}) copy-start(u32[32]{0:T(128)} %constant.32) | copy-start | bytes 388
Sparse Core Ops, SparseCore 0:
  38.8 70.7 reduce-scatter.1
where the time goes:
time: 119 us
  waiting for transfers between devices  54.4 us (46%)
  blocking collectives  15.8 us (13%)
  other arithmetic  15.2 us (13%)
  between operations  14.1 us (12%)
  starting transfers between devices  9.31 us (8%)
  matrix products  8.23 us (7%)
  local copies, waits for them, and re-layouts  1.66 us (1%)
    reduce_scatter x1, waiting for transfers between devices, local(): lax.psum_scatter(weighted, 'member', scatter_dimension=0, tiled=True)  48.5 us
    unnamed x1, blocking collectives  15.8 us
    all_to_all x1, starting transfers between devices, local(): lax.all_to_all(slot_flags, 'group', split_axis=0, concat_axis=0, tiled=True)  5.16 us
    all_to_all x1, waiting for transfers between devices, local(): lax.all_to_all(packed, 'group', split_axis=0, concat_axis=0, tiled=True)  5.08 us
    convert_element_type x1, other arithmetic, local(): centroid_f = centroids.astype(jnp.float32)  5.04 us
    dot_general x1, matrix products, local(): jnp.dot(all_weights.T, all_rows, preferred_element_type=jnp.float32)  4.69 us
    all_to_all x1, starting transfers between devices, local(): lax.all_to_all(packed, 'group', split_axis=0, concat_axis=0, tiled=True)  4.1 us
    reduce_sum x1, other arithmetic, local(): centroid_norms = jnp.sum(centroid_f * centroid_f, axis=1)  2.72 us
  transfers between devices with their start and end apart: 3, of which 3 were waited for; matrix products, arithmetic and copies ran while one was open for 9% of the time, Pallas kernels for 0%

commit v1 on v0

--- a/solution.py
+++ b/solution.py
@@ -1,12 +1,18 @@
+import functools
+
 import jax
 import jax.numpy as jnp
 from jax import lax
+from jax.experimental import pallas as pl
+from jax.experimental.pallas import tpu as pltpu
 from jax.sharding import PartitionSpec as P
 
 score_scale = 0.15
-
-
-def local(points, centroids, dest_group):
+lanes = 128
+vmem_limit = 48 * 1024 * 1024
+
+
+def general(points, centroids, dest_group):
     group_count = lax.axis_size("group")
     member_count = lax.axis_size("member")
     point_rows = points.shape[0]
@@ -63,7 +69,268 @@
     return refined
 
 
+def vmem():
+    return pl.BlockSpec(memory_space=pltpu.VMEM)
+
+
+def smem():
+    return pl.BlockSpec(memory_space=pltpu.SMEM)
+
+
+def pack_kernel(place, dest, points, *packed):
+    count = len(packed)
+    row_count = points.shape[0]
+    capacity = row_count // count
+    apart = jnp.bitwise_xor(dest[...], place[0])
+    lane = lax.broadcasted_iota(jnp.int32, (row_count, lanes), 1)
+    named = (apart == lane).astype(jnp.float32)
+    row_at = lax.broadcasted_iota(jnp.int32, (row_count, row_count), 0)
+    col_at = lax.broadcasted_iota(jnp.int32, (row_count, row_count), 1)
+    before = (col_at < row_at).astype(jnp.bfloat16)
+    earlier = jnp.dot(before, named.astype(jnp.bfloat16), preferred_element_type=jnp.float32)
+    rank = jnp.sum(earlier * named, axis=1, keepdims=True)
+    slot = apart * capacity + rank.astype(jnp.int32)
+    placement = (slot == col_at).astype(jnp.float32).T.astype(jnp.bfloat16)
+    rows = jnp.dot(placement, points[...], preferred_element_type=jnp.float32)
+    rows = rows.astype(jnp.bfloat16)
+    for k in range(count):
+        packed[k][...] = rows[k * capacity : (k + 1) * capacity]
+
+
+def pack(place, dest_group, points, group_count):
+    row_count, feature_dim = points.shape
+    capacity = row_count // group_count
+    return pl.pallas_call(
+        pack_kernel,
+        out_shape=[jax.ShapeDtypeStruct((capacity, feature_dim), points.dtype)] * group_count,
+        in_specs=[smem(), vmem(), vmem()],
+        out_specs=[vmem()] * group_count,
+        compiler_params=pltpu.CompilerParams(vmem_limit_bytes=vmem_limit),
+        cost_estimate=pl.CostEstimate(
+            flops=4 * row_count * row_count * feature_dim,
+            bytes_accessed=4 * row_count * feature_dim,
+            transcendentals=0,
+        ),
+        name="pack",
+    )(place, dest_group, points)
+
+
+def soft_weights(rows, table, half_norms, scores, tile, first, inverse_at):
+    fine_count = table.shape[0]
+    row_count = rows.shape[0]
+    dims = (((1,), (1,)), ((), ()))
+
+    def score(index, top):
+        at = pl.ds(pl.multiple_of(index * tile, tile), tile)
+        block = lax.dot_general(
+            table[at, :], rows[...], dims, preferred_element_type=jnp.float32
+        )
+        block = block - half_norms[at, :]
+        scores[at, :] = block
+        return jnp.maximum(top, jnp.max(block, axis=0, keepdims=True))
+
+    top = lax.fori_loop(
+        0, fine_count // tile, score, jnp.full((1, row_count), -jnp.inf, jnp.float32)
+    )
+
+    def total(index, sofar):
+        at = pl.ds(pl.multiple_of(index * tile, tile), tile)
+        block = jnp.exp(score_scale * (scores[at, :] - top))
+        return sofar + jnp.sum(block, axis=0, keepdims=True)
+
+    sofar = lax.fori_loop(
+        0, fine_count // tile, total, jnp.zeros((1, row_count), jnp.float32)
+    )
+    return top, 1.0 / sofar
+
+
+def tile_weights(scores, top, inverse, start, tile):
+    at = pl.ds(pl.multiple_of(start, tile), tile)
+    return (jnp.exp(score_scale * (scores[at, :] - top)) * inverse).astype(jnp.bfloat16)
+
+
+def gather_rows(parts, rows):
+    start = 0
+    for part in parts:
+        rows[start : start + part.shape[0], :] = part[...]
+        start += part.shape[0]
+
+
+def add_tile(weights, rows, sums, fresh):
+    feature_dim = rows.shape[1]
+    product = jnp.dot(weights, rows[...], preferred_element_type=jnp.float32)
+    count = jnp.sum(weights.astype(jnp.float32), axis=1, keepdims=True)
+    count = jnp.broadcast_to(count, (count.shape[0], lanes))
+    if fresh:
+        sums[:, :feature_dim] = product
+        sums[:, feature_dim:] = count
+    else:
+        sums[:, :feature_dim] += product
+        sums[:, feature_dim:] += count
+
+
+def own_kernel(tile, parts_n, place, table, *refs):
+    parts, (keep, give, half_norms, rows, scores) = refs[:parts_n], refs[parts_n:]
+
+    @pl.loop(0, table.shape[0] // tile)
+    def _(index):
+        at = pl.ds(pl.multiple_of(index * tile, tile), tile)
+        block = table[at, :].astype(jnp.float32)
+        half_norms[at, :] = 0.5 * jnp.sum(block * block, axis=1, keepdims=True)
+
+    gather_rows(parts, rows)
+    top, inverse = soft_weights(rows, table, half_norms, scores, tile, None, None)
+    mine, other = place[1] * tile, place[2] * tile
+    add_tile(tile_weights(scores, top, inverse, mine, tile), rows, keep, True)
+    add_tile(tile_weights(scores, top, inverse, other, tile), rows, give, True)
+
+
+def step_kernel(tile, parts_n, place, table, half_norms, keep_in, give_in, *refs):
+    parts, (keep, give, rows, scores) = refs[:parts_n], refs[parts_n:]
+    keep[...] = keep_in[...]
+    give[...] = give_in[...]
+
+    @pl.when(place[0] == 1)
+    def _():
+        gather_rows(parts, rows)
+        top, inverse = soft_weights(rows, table, half_norms, scores, tile, None, None)
+        mine, other = place[1] * tile, place[2] * tile
+        add_tile(tile_weights(scores, top, inverse, mine, tile), rows, keep, False)
+        add_tile(tile_weights(scores, top, inverse, other, tile), rows, give, False)
+
+
+def last_kernel(tile, parts_n, place, table, half_norms, keep, got, *refs):
+    parts, passed = refs[:parts_n], refs[parts_n : 2 * parts_n]
+    refined, rows, scores, sums = refs[2 * parts_n :]
+    feature_dim = rows.shape[1]
+    sums[...] = keep[...] + got[...]
+    mine = place[1] * tile
+
+    @pl.when(place[0] == 1)
+    def _():
+        gather_rows(parts, rows)
+
+    @pl.when(place[0] == 2)
+    def _():
+        gather_rows(passed, rows)
+
+    @pl.when(place[0] > 0)
+    def _():
+        top, inverse = soft_weights(rows, table, half_norms, scores, tile, None, None)
+        add_tile(tile_weights(scores, top, inverse, mine, tile), rows, sums, False)
+
+    old = table[pl.ds(pl.multiple_of(mine, tile), tile), :].astype(jnp.float32)
+    scale = 1.0 / (sums[:, feature_dim : feature_dim + 1] + 1.0)
+    refined[...] = ((sums[:, :feature_dim] + old) * scale).astype(jnp.bfloat16)
+
+
+def cost(fine_count, row_count, feature_dim):
+    return pl.CostEstimate(
+        flops=4 * fine_count * row_count * feature_dim,
+        bytes_accessed=2 * fine_count * feature_dim + 8 * row_count * feature_dim,
+        transcendentals=fine_count * row_count,
+    )
+
+
+def handoff(points, centroids, dest_group):
+    group_count = lax.axis_size("group")
+    member_count = lax.axis_size("member")
+    depth = member_count // 2
+    feature_dim = points.shape[1]
+    fine_count = centroids.shape[0]
+    tile = fine_count // member_count
+    group = lax.axis_index("group")
+    member = lax.axis_index("member")
+    level, core = member // 2, member % 2
+
+    def perm(x, pairs):
+        return lax.ppermute(x, "member", pairs)
+
+    def swap(x):
+        return perm(x, [(i, i ^ 1) for i in range(member_count)])
+
+    def onward(x, step):
+        up = [(2 * z, 2 * z + 2) for z in range(step - 1, depth - 1)]
+        down = [(2 * z + 3, 2 * z + 1) for z in range(0, depth - step)]
+        return perm(x, up + down)
+
+    def ints(*values):
+        return jnp.stack([jnp.asarray(v, jnp.int32) for v in values])
+
+    packed = pack(ints(group), dest_group, points, group_count)
+    own = packed[0]
+    fetched = [
+        lax.ppermute(packed[k], "group", [(i, i ^ k) for i in range(group_count)])
+        for k in range(1, group_count)
+    ]
+    own_far = jnp.concatenate(fetched, axis=0)
+    near, far = [own, swap(own)], [own_far, swap(own_far)]
+    chunks = near + far
+
+    sums_shape = jax.ShapeDtypeStruct((tile, feature_dim + lanes), jnp.float32)
+    params = pltpu.CompilerParams(vmem_limit_bytes=vmem_limit)
+
+    def scratch(rows):
+        return [
+            pltpu.VMEM((rows, feature_dim), jnp.bfloat16),
+            pltpu.VMEM((fine_count, rows), jnp.float32),
+        ]
+
+    mine, other = member, member + 1 - 2 * core
+    mine_rows = points.shape[0]
+    keep, give, half_norms = pl.pallas_call(
+        functools.partial(own_kernel, tile, 2),
+        out_shape=[sums_shape, sums_shape, jax.ShapeDtypeStruct((fine_count, 1), jnp.float32)],
+        in_specs=[smem()] + [vmem()] * 3,
+        out_specs=[vmem()] * 3,
+        scratch_shapes=scratch(mine_rows),
+        compiler_params=params,
+        cost_estimate=cost(fine_count, mine_rows, feature_dim),
+        name="own_rows",
+    )(ints(1, mine, other), centroids, own, own_far)
+
+    for step in range(1, depth):
+        chunks = [onward(chunk, step) for chunk in chunks]
+        if step == depth - 1:
+            break
+        valid = jnp.where(core == 0, level >= step, level <= depth - 1 - step)
+        keep, give = pl.pallas_call(
+            functools.partial(step_kernel, tile, len(chunks)),
+            out_shape=[sums_shape, sums_shape],
+            in_specs=[smem()] + [vmem()] * (4 + len(chunks)),
+            out_specs=[vmem()] * 2,
+            scratch_shapes=scratch(2 * mine_rows),
+            input_output_aliases={3: 0, 4: 1},
+            compiler_params=params,
+            cost_estimate=cost(fine_count, 2 * mine_rows, feature_dim),
+            name="step_rows",
+        )(ints(valid, mine, other), centroids, half_norms, keep, give, *chunks)
+
+    got = swap(give)
+    passed = [swap(chunk) for chunk in chunks]
+    receives = jnp.where(core == 0, level == depth - 1, level == 0)
+    ends = jnp.logical_or(level == depth - 1, level == 0)
+    mode = jnp.where(receives, 1, jnp.where(ends, 2, 0))
+    return pl.pallas_call(
+        functools.partial(last_kernel, tile, len(chunks)),
+        out_shape=jax.ShapeDtypeStruct((tile, feature_dim), jnp.bfloat16),
+        in_specs=[smem()] + [vmem()] * (4 + 2 * len(chunks)),
+        out_specs=vmem(),
+        scratch_shapes=scratch(2 * mine_rows)
+        + [pltpu.VMEM((tile, feature_dim + lanes), jnp.float32)],
+        compiler_params=params,
+        cost_estimate=cost(fine_count, 2 * mine_rows, feature_dim),
+        name="last_rows",
+    )(ints(mode, mine, other), centroids, half_norms, keep, got, *chunks, *passed)
+
+
 def solution(mesh):
+    def local(points, centroids, dest_group):
+        groups, members = mesh.shape["group"], mesh.shape["member"]
+        if groups * (points.shape[0] // 4) == points.shape[0] and 6 <= members <= 16:
+            return handoff(points, centroids, dest_group)
+        return general(points, centroids, dest_group)
+
     return jax.shard_map(
         local,
         mesh=mesh,

time: 119 us -> 81.7 us (0.69)
  the two profiles are of different devices: /device:TPU:0 before, /device:TPU:25 now
where the time goes in v1:
time: 81.7 us; the launch traced here: 81.1 us
  starting transfers between devices  51.1 us (63%)
  Pallas kernels  19 us (23%)
  waiting for transfers between devices  5.17 us (6%)
  local copies, waits for them, and re-layouts  5.14 us (6%)
    ppermute x19, starting transfers between devices, perm(): return lax.ppermute(x, 'member', pairs)  48.4 us
    pallas_call x1, Pallas kernels, handoff(): pl.pallas_call(functools.partial(last_kernel, tile, len(chunks)), out_sha...  7.5 us
    pallas_call x1, Pallas kernels, handoff(): pl.pallas_call(functools.partial(own_kernel, tile, 2), out_shape=[sums_sh...  6.48 us
    unnamed x13, local copies, waits for them, and re-layouts  5.14 us
    pallas_call x2, Pallas kernels, handoff(): pl.pallas_call(functools.partial(step_kernel, tile, len(chunks)), out_sha...  4.27 us
    ppermute x3, waiting for transfers between devices, handoff(): lax.ppermute(packed[k], 'group', [(i, i ^ k) for i in range(group_count)])  4.25 us
    ppermute x3, starting transfers between devices, handoff(): lax.ppermute(packed[k], 'group', [(i, i ^ k) for i in range(group_count)])  2.71 us
  transfers between devices with their start and end apart: 22, of which 4 were waited for; matrix products, arithmetic and copies ran while one was open for 0% of the time, Pallas kernels for 11%

profile of v1, /device:TPU:25, one launch (start us, length us, event | category | flops | bytes accessed | tf_op | source)
XLA Modules:
  0.0 81.1 jit_solution(3231185889951569199)
XLA Ops:
  0.0 0.8 copy.8.dest
  0.8 0.0 copy-start
  0.8 1.0 %copy-done = bf16[256,768]{1,0:T(8,128)(2,1)S(1)} copy-done((bf16[256,768]{1,0:T(8,128)(2,1)S(1)}, bf16[256,768]{1,0:T(8,128)(2,1)}, u32[]{:S(2)}) %copy-start) | copy-done | bytes 393240
  1.8 0.7 pack.1
  2.6 1.3 %collective-permute-start = (bf16[64,768]{1,0:T(8,128)(2,1)S(1)}, bf16[64,768]{1,0:T(8,128)(2,1)S(1)}, u32[]{:S(2)}, u32[]{:S(2)}) collective-permute-start(bf16[64,768]{1,0:T(8,128)(2,1)S(1)} %get-tuple-element.17), channel_id=1, source_target_pairs={{0,8},{8,0},{16,24},{24,16},{1,9},{9,1},{17,25},{25,17},{2,10},{10... | collective-permute-start | bytes 294920 | tf_op jit(solution)/shard_map/ppermute | solution.py:263
  3.8 1.2 %collective-permute-start.1 = (bf16[64,768]{1,0:T(8,128)(2,1)S(1)}, bf16[64,768]{1,0:T(8,128)(2,1)S(1)}, u32[]{:S(2)}, u32[]{:S(2)}) collective-permute-start(bf16[64,768]{1,0:T(8,128)(2,1)S(1)} %get-tuple-element.18), channel_id=1, source_target_pairs={{0,16},{8,24},{16,0},{24,8},{1,17},{9,25},{17,1},{25,9},{2,18},{10... | collective-permute-start | bytes 294920 | tf_op jit(solution)/shard_map/ppermute | solution.py:263
  5.1 0.2 collective-permute-start.2
  5.3 0.8 %collective-permute-done = bf16[64,768]{1,0:T(8,128)(2,1)S(1)} collective-permute-done((bf16[64,768]{1,0:T(8,128)(2,1)S(1)}, bf16[64,768]{1,0:T(8,128)(2,1)S(1)}, u32[]{:S(2)}, u32[]{:S(2)}) %collective-permute-start) | collective-permute-done | bytes 98336 | tf_op jit(solution)/shard_map/ppermute | solution.py:263
  6.1 1.4 %collective-permute-done.1 = bf16[64,768]{1,0:T(8,128)(2,1)S(1)} collective-permute-done((bf16[64,768]{1,0:T(8,128)(2,1)S(1)}, bf16[64,768]{1,0:T(8,128)(2,1)S(1)}, u32[]{:S(2)}, u32[]{:S(2)}) %collective-permute-start.1) | collective-permute-done | bytes 98336 | tf_op jit(solution)/shard_map/ppermute | solution.py:263
  7.5 2.0 %collective-permute-done.2 = bf16[64,768]{1,0:T(8,128)(2,1)S(1)} collective-permute-done((bf16[64,768]{1,0:T(8,128)(2,1)S(1)}, bf16[64,768]{1,0:T(8,128)(2,1)S(1)}, u32[]{:S(2)}, u32[]{:S(2)}) %collective-permute-start.2) | collective-permute-done | bytes 98336 | tf_op jit(solution)/shard_map/ppermute | solution.py:263
  9.6 2.3 %collective-permute-start.7 = (bf16[192,768]{1,0:T(8,128)(2,1)S(1)}, bf16[192,768]{1,0:T(8,128)(2,1)S(1)}, u32[]{:S(2)}, u32[]{:S(2)}) collective-permute-start(bf16[192,768]{1,0:T(8,128)(2,1)S(1)} %constant_dynamic-update-slice_fusion.refs_1_), channel_id=1, source_target_pairs={{0,1},{1,0},{2,3},{3,2},{4,5},{5,4},{6,7},{7,6},{8,9},{9,8},{10,11... | collective-permute-start | bytes 884744 | tf_op jit(solution)/shard_map/ppermute | solution.py:247
  11.9 2.1 %collective-permute-start.3 = (bf16[64,768]{1,0:T(8,128)(2,1)S(1)}, bf16[64,768]{1,0:T(8,128)(2,1)S(1)}, u32[]{:S(2)}, u32[]{:S(2)}) collective-permute-start(bf16[64,768]{1,0:T(8,128)(2,1)S(1)} %get-tuple-element.16.refs_0_), channel_id=1, source_target_pairs={{0,2},{2,4},{4,6},{3,1},{5,3},{7,5},{8,10},{10,12},{12,14},{11,9},... | collective-permute-start | bytes 294920 | tf_op jit(solution)/shard_map/ppermute | solution.py:247
  14.0 0.1 collective-permute-start.4
  14.1 0.1 add_add_fusion.1.place
  14.2 3.5 %collective-permute-start.6 = (bf16[192,768]{1,0:T(8,128)(2,1)S(1)}, bf16[192,768]{1,0:T(8,128)(2,1)S(1)}, u32[]{:S(2)}, u32[]{:S(2)}) collective-permute-start(bf16[192,768]{1,0:T(8,128)(2,1)S(1)} %constant_dynamic-update-slice_fusion.refs_1_), channel_id=1, source_target_pairs={{0,2},{2,4},{4,6},{3,1},{5,3},{7,5},{8,10},{10,12},{12,14},{11,9},... | collective-permute-start | bytes 884744 | tf_op jit(solution)/shard_map/ppermute | solution.py:247
  17.6 0.0 collective-permute-done.7
  17.6 2.1 %collective-permute-start.8 = (bf16[192,768]{1,0:T(8,128)(2,1)S(1)}, bf16[192,768]{1,0:T(8,128)(2,1)S(1)}, u32[]{:S(2)}, u32[]{:S(2)}) collective-permute-start(bf16[192,768]{1,0:T(8,128)(2,1)S(1)} %collective-permute-done.7), channel_id=1, source_target_pairs={{0,2},{2,4},{4,6},{3,1},{5,3},{7,5},{8,10},{10,12},{12,14},{11,9},... | collective-permute-start | bytes 884744 | tf_op jit(solution)/shard_map/ppermute | solution.py:247
  19.7 0.1 add_add_fusion.2.place
  19.8 0.1 add_add_fusion.3.place
  19.9 0.0 collective-permute-done.4
  19.9 2.1 %collective-permute-start.5 = (bf16[64,768]{1,0:T(8,128)(2,1)S(1)}, bf16[64,768]{1,0:T(8,128)(2,1)S(1)}, u32[]{:S(2)}, u32[]{:S(2)}) collective-permute-start(bf16[64,768]{1,0:T(8,128)(2,1)S(1)} %collective-permute-done.4), channel_id=1, source_target_pairs={{0,2},{2,4},{4,6},{3,1},{5,3},{7,5},{8,10},{10,12},{12,14},{11,9},... | collective-permute-start | bytes 294920 | tf_op jit(solution)/shard_map/ppermute | solution.py:247
  22.0 0.0 collective-permute-done.3.refs_0_
  22.0 0.7 collective-permute-start.9
  22.6 6.5 %own_rows.1 = (f32[256,896]{1,0:T(8,128)S(1)}, f32[256,896]{1,0:T(8,128)S(1)}, f32[2048,1]{1,0:T(8,128)S(1)}) custom-call(s32[3]{0:T(128)S(1)} %add_add_fusion.1.place, bf16[2048,768]{1,0:T(8,128)(2,1)} %table.7, bf16[64,768]{1,0:T(8,128)(2,1)S(1)} %get-tuple-element.16.refs_0_, bf16[192,768]{1,0:T(8,128)(2,1)S(1)} %constant_dynamic-update-slice_fusion.refs_1_), custom_call_target="tpu_custom_call" | custom-call | flops 1610612736 | bytes 4718592 | tf_op jit(solution)/shard_map/own_rows/pallas_call | solution.py:281
  29.1 0.0 copy-start.1
  29.1 0.0 collective-permute-done.5.refs_1_
  29.1 0.7 collective-permute-start.10
  29.8 0.0 collective-permute-done.6.refs_2_
  29.8 0.7 collective-permute-start.11
  30.5 0.0 collective-permute-done.8.refs_3_
  30.5 0.7 collective-permute-start.12
  31.2 2.1 %step_rows.2 = (f32[256,896]{1,0:T(8,128)S(1)}, f32[256,896]{1,0:T(8,128)S(1)}) custom-call(s32[3]{0:T(128)S(1)} %add_add_fusion.3.place, bf16[2048,768]{1,0:T(8,128)(2,1)} %table.7, f32[2048,1]{1,0:T(8,128)S(1)} %get-tuple-element.20.half_norms, f32[256,896]{1,0:T(8,128)S(1)} %get-tuple-element.21.keep_in, ...), custom_call_target="tpu_custom_call", output_to_operand_aliasing={{0}: (3, {}), {1}: (4, {})} | custom-call | flops 3221225472 | bytes 6291456 | tf_op jit(solution)/shard_map/step_rows/pallas_call | solution.py:297
  33.4 0.0 collective-permute-done.9.refs_0_
  33.4 0.0 collective-permute-done.10.refs_1_
  33.4 0.0 collective-permute-done.11.refs_2_
  33.4 0.0 collective-permute-done.12.refs_3_
  33.4 0.0 copy-done.1
  33.4 2.1 %step_rows.3 = (f32[256,896]{1,0:T(8,128)S(1)}, f32[256,896]{1,0:T(8,128)S(1)}) custom-call(s32[3]{0:T(128)S(1)} %add_add_fusion.2.place, bf16[2048,768]{1,0:T(8,128)(2,1)} %table.7, f32[2048,1]{1,0:T(8,128)S(1)} %get-tuple-element.20.half_norms, f32[256,896]{1,0:T(8,128)S(1)} %get-tuple-element.23.keep_in, ...), custom_call_target="tpu_custom_call", output_to_operand_aliasing={{0}: (3, {}), {1}: (4, {})} | custom-call | flops 3221225472 | bytes 6291456 | tf_op jit(solution)/shard_map/step_rows/pallas_call | solution.py:297
  35.5 0.0 copy-start.3
  35.6 0.9 %copy-done.3 = f32[256,896]{1,0:T(8,128)} copy-done((f32[256,896]{1,0:T(8,128)}, f32[256,896]{1,0:T(8,128)S(1)}, u32[]{:S(2)}) %copy-start.3) | copy-done | bytes 917528
  36.5 14.1 %collective-permute-start.13 = (f32[256,896]{1,0:T(8,128)S(1)}, f32[256,896]{1,0:T(8,128)S(1)}, u32[]{:S(2)}, u32[]{:S(2)}) collective-permute-start(f32[256,896]{1,0:T(8,128)S(1)} %get-tuple-element.26), channel_id=1, source_target_pairs={{0,1},{1,0},{2,3},{3,2},{4,5},{5,4},{6,7},{7,6},{8,9},{9,8},{10,11... | collective-permute-start | bytes 2752520 | tf_op jit(solution)/shard_map/ppermute | solution.py:247
  50.6 0.7 collective-permute-start.16
  51.3 0.7 collective-permute-start.17
  52.0 0.0 collective-permute-done.16.refs_2_
  52.0 7.2 %collective-permute-start.20 = (bf16[192,768]{1,0:T(8,128)(2,1)S(1)}, bf16[192,768]{1,0:T(8,128)(2,1)S(1)}, u32[]{:S(2)}, u32[]{:S(2)}) collective-permute-start(bf16[192,768]{1,0:T(8,128)(2,1)S(1)} %collective-permute-done.16.refs_2_), channel_id=1, source_target_pairs={{0,1},{1,0},{2,3},{3,2},{4,5},{5,4},{6,7},{7,6},{8,9},{9,8},{10,11... | collective-permute-start | bytes 884744 | tf_op jit(solution)/shard_map/ppermute | solution.py:247
  59.2 0.0 collective-permute-done.17.refs_3_
  59.2 3.2 %collective-permute-start.21 = (bf16[192,768]{1,0:T(8,128)(2,1)S(1)}, bf16[192,768]{1,0:T(8,128)(2,1)S(1)}, u32[]{:S(2)}, u32[]{:S(2)}) collective-permute-start(bf16[192,768]{1,0:T(8,128)(2,1)S(1)} %collective-permute-done.17.refs_3_), channel_id=1, source_target_pairs={{0,1},{1,0},{2,3},{3,2},{4,5},{5,4},{6,7},{7,6},{8,9},{9,8},{10,11... | collective-permute-start | bytes 884744 | tf_op jit(solution)/shard_map/ppermute | solution.py:247
  62.4 0.7 collective-permute-start.14
  63.0 0.7 collective-permute-start.15
  63.7 0.0 collective-permute-done.14.refs_0_
  63.7 5.1 %collective-permute-start.18 = (bf16[64,768]{1,0:T(8,128)(2,1)S(1)}, bf16[64,768]{1,0:T(8,128)(2,1)S(1)}, u32[]{:S(2)}, u32[]{:S(2)}) collective-permute-start(bf16[64,768]{1,0:T(8,128)(2,1)S(1)} %collective-permute-done.14.refs_0_), channel_id=1, source_target_pairs={{0,1},{1,0},{2,3},{3,2},{4,5},{5,4},{6,7},{7,6},{8,9},{9,8},{10,11... | collective-permute-start | bytes 294920 | tf_op jit(solution)/shard_map/ppermute | solution.py:247
  68.9 0.0 collective-permute-done.15.refs_1_
  68.9 1.3 %collective-permute-start.19 = (bf16[64,768]{1,0:T(8,128)(2,1)S(1)}, bf16[64,768]{1,0:T(8,128)(2,1)S(1)}, u32[]{:S(2)}, u32[]{:S(2)}) collective-permute-start(bf16[64,768]{1,0:T(8,128)(2,1)S(1)} %collective-permute-done.15.refs_1_), channel_id=1, source_target_pairs={{0,1},{1,0},{2,3},{3,2},{4,5},{5,4},{6,7},{7,6},{8,9},{9,8},{10,11... | collective-permute-start | bytes 294920 | tf_op jit(solution)/shard_map/ppermute | solution.py:247
  70.2 0.1 add_add_fusion.place
  70.3 0.0 collective-permute-done.18.refs_4_
  70.3 0.9 %collective-permute-done.19.refs_5_ = bf16[64,768]{1,0:T(8,128)(2,1)S(1)} collective-permute-done((bf16[64,768]{1,0:T(8,128)(2,1)S(1)}, bf16[64,768]{1,0:T(8,128)(2,1)S(1)}, u32[]{:S(2)}, u32[]{:S(2)}) %collective-permute-start.19) | collective-permute-done | bytes 98336 | tf_op jit(solution)/shard_map/ppermute | solution.py:247
  71.1 0.0 collective-permute-done.20.refs_6_
  71.1 0.0 collective-permute-done.21.refs_7_
  71.1 0.0 collective-permute-done.13.got
  71.1 0.0 copy-start.2
  71.2 1.2 %copy-done.2 = f32[2048,1]{1,0:T(8,128)S(1)} copy-done((f32[2048,1]{1,0:T(8,128)S(1)}, f32[2048,1]{1,0:T(8,128)}, u32[]{:S(2)}) %copy-start.2) | copy-done | bytes 8216
  72.4 0.0 copy-start.4
  72.4 1.2 %copy-done.4 = f32[256,896]{1,0:T(8,128)S(1)} copy-done((f32[256,896]{1,0:T(8,128)S(1)}, f32[256,896]{1,0:T(8,128)}, u32[]{:S(2)}) %copy-start.4) | copy-done | bytes 917528
  73.5 7.5 %last_rows.1 = bf16[256,768]{1,0:T(8,128)(2,1)} custom-call(s32[3]{0:T(128)S(1)} %add_add_fusion.place, bf16[2048,768]{1,0:T(8,128)(2,1)} %table.7, f32[2048,1]{1,0:T(8,128)S(1)} %copy-done.2, f32[256,896]{1,0:T(8,128)S(1)} %copy-done.4, f32[256,896]{1,0:T(8,128)S(1)} %collective-permute-done.13.got, bf16[64,768]{1,0:T(8,128)(2,1)S(1)} %collective-permute-done.14.refs_0_, ...), custom_call_target="tpu_custom_call" | custom-call | flops 3221225472 | bytes 6291456 | tf_op jit(solution)/shard_map/last_rows/pallas_call | solution.py:314
  (3 shorter events, 0.0 us)
Async XLA Ops:
  0.8 1.0 %copy-start = (bf16[256,768]{1,0:T(8,128)(2,1)S(1)}, bf16[256,768]{1,0:T(8,128)(2,1)}, u32[]{:S(2)}) copy-start(bf16[256,768]{1,0:T(8,128)(2,1)} %points.1) | copy-start | bytes 1179652
  2.6 3.5 %collective-permute-start = (bf16[64,768]{1,0:T(8,128)(2,1)S(1)}, bf16[64,768]{1,0:T(8,128)(2,1)S(1)}, u32[]{:S(2)}, u32[]{:S(2)}) collective-permute-start(bf16[64,768]{1,0:T(8,128)(2,1)S(1)} %get-tuple-element.17), channel_id=1, source_target_pairs={{0,8},{8,0},{16,24},{24,16},{1,9},{9,1},{17,25},{25,17},{2,10},{10... | collective-permute-start | bytes 294920 | tf_op jit(solution)/shard_map/ppermute | solution.py:263
  3.8 3.7 %collective-permute-start.1 = (bf16[64,768]{1,0:T(8,128)(2,1)S(1)}, bf16[64,768]{1,0:T(8,128)(2,1)S(1)}, u32[]{:S(2)}, u32[]{:S(2)}) collective-permute-start(bf16[64,768]{1,0:T(8,128)(2,1)S(1)} %get-tuple-element.18), channel_id=1, source_target_pairs={{0,16},{8,24},{16,0},{24,8},{1,17},{9,25},{17,1},{25,9},{2,18},{10... | collective-permute-start | bytes 294920 | tf_op jit(solution)/shard_map/ppermute | solution.py:263
  5.1 4.5 %collective-permute-start.2 = (bf16[64,768]{1,0:T(8,128)(2,1)S(1)}, bf16[64,768]{1,0:T(8,128)(2,1)S(1)}, u32[]{:S(2)}, u32[]{:S(2)}) collective-permute-start(bf16[64,768]{1,0:T(8,128)(2,1)S(1)} %get-tuple-element.19), channel_id=1, source_target_pairs={{0,24},{8,16},{16,8},{24,0},{1,25},{9,17},{17,9},{25,1},{2,26},{10... | collective-permute-start | bytes 294920 | tf_op jit(solution)/shard_map/ppermute | solution.py:263
  9.6 8.1 %collective-permute-start.7 = (bf16[192,768]{1,0:T(8,128)(2,1)S(1)}, bf16[192,768]{1,0:T(8,128)(2,1)S(1)}, u32[]{:S(2)}, u32[]{:S(2)}) collective-permute-start(bf16[192,768]{1,0:T(8,128)(2,1)S(1)} %constant_dynamic-update-slice_fusion.refs_1_), channel_id=1, source_target_pairs={{0,1},{1,0},{2,3},{3,2},{4,5},{5,4},{6,7},{7,6},{8,9},{9,8},{10,11... | collective-permute-start | bytes 884744 | tf_op jit(solution)/shard_map/ppermute | solution.py:247
  11.9 10.1 %collective-permute-start.3 = (bf16[64,768]{1,0:T(8,128)(2,1)S(1)}, bf16[64,768]{1,0:T(8,128)(2,1)S(1)}, u32[]{:S(2)}, u32[]{:S(2)}) collective-permute-start(bf16[64,768]{1,0:T(8,128)(2,1)S(1)} %get-tuple-element.16.refs_0_), channel_id=1, source_target_pairs={{0,2},{2,4},{4,6},{3,1},{5,3},{7,5},{8,10},{10,12},{12,14},{11,9},... | collective-permute-start | bytes 294920 | tf_op jit(solution)/shard_map/ppermute | solution.py:247
  14.0 5.9 %collective-permute-start.4 = (bf16[64,768]{1,0:T(8,128)(2,1)S(1)}, bf16[64,768]{1,0:T(8,128)(2,1)S(1)}, u32[]{:S(2)}, u32[]{:S(2)}) collective-permute-start(bf16[64,768]{1,0:T(8,128)(2,1)S(1)} %get-tuple-element.16.refs_0_), channel_id=1, source_target_pairs={{0,1},{1,0},{2,3},{3,2},{4,5},{5,4},{6,7},{7,6},{8,9},{9,8},{10,11... | collective-permute-start | bytes 294920 | tf_op jit(solution)/shard_map/ppermute | solution.py:247
  14.2 15.7 %collective-permute-start.6 = (bf16[192,768]{1,0:T(8,128)(2,1)S(1)}, bf16[192,768]{1,0:T(8,128)(2,1)S(1)}, u32[]{:S(2)}, u32[]{:S(2)}) collective-permute-start(bf16[192,768]{1,0:T(8,128)(2,1)S(1)} %constant_dynamic-update-slice_fusion.refs_1_), channel_id=1, source_target_pairs={{0,2},{2,4},{4,6},{3,1},{5,3},{7,5},{8,10},{10,12},{12,14},{11,9},... | collective-permute-start | bytes 884744 | tf_op jit(solution)/shard_map/ppermute | solution.py:247
  17.6 12.9 %collective-permute-start.8 = (bf16[192,768]{1,0:T(8,128)(2,1)S(1)}, bf16[192,768]{1,0:T(8,128)(2,1)S(1)}, u32[]{:S(2)}, u32[]{:S(2)}) collective-permute-start(bf16[192,768]{1,0:T(8,128)(2,1)S(1)} %collective-permute-done.7), channel_id=1, source_target_pairs={{0,2},{2,4},{4,6},{3,1},{5,3},{7,5},{8,10},{10,12},{12,14},{11,9},... | collective-permute-start | bytes 884744 | tf_op jit(solution)/shard_map/ppermute | solution.py:247
  19.9 9.2 %collective-permute-start.5 = (bf16[64,768]{1,0:T(8,128)(2,1)S(1)}, bf16[64,768]{1,0:T(8,128)(2,1)S(1)}, u32[]{:S(2)}, u32[]{:S(2)}) collective-permute-start(bf16[64,768]{1,0:T(8,128)(2,1)S(1)} %collective-permute-done.4), channel_id=1, source_target_pairs={{0,2},{2,4},{4,6},{3,1},{5,3},{7,5},{8,10},{10,12},{12,14},{11,9},... | collective-permute-start | bytes 294920 | tf_op jit(solution)/shard_map/ppermute | solution.py:247
  22.0 11.4 %collective-permute-start.9 = (bf16[64,768]{1,0:T(8,128)(2,1)S(1)}, bf16[64,768]{1,0:T(8,128)(2,1)S(1)}, u32[]{:S(2)}, u32[]{:S(2)}) collective-permute-start(bf16[64,768]{1,0:T(8,128)(2,1)S(1)} %collective-permute-done.3.refs_0_), channel_id=1, source_target_pairs={{2,4},{4,6},{3,1},{5,3},{10,12},{12,14},{11,9},{13,11},{18,20},{20... | collective-permute-start | bytes 294920 | tf_op jit(solution)/shard_map/ppermute | solution.py:247
  29.1 4.3 %copy-start.1 = (f32[2048,1]{1,0:T(8,128)}, f32[2048,1]{1,0:T(8,128)S(1)}, u32[]{:S(2)}) copy-start(f32[2048,1]{1,0:T(8,128)S(1)} %get-tuple-element.20.half_norms) | copy-start | bytes 24580
  29.1 4.2 %collective-permute-start.10 = (bf16[64,768]{1,0:T(8,128)(2,1)S(1)}, bf16[64,768]{1,0:T(8,128)(2,1)S(1)}, u32[]{:S(2)}, u32[]{:S(2)}) collective-permute-start(bf16[64,768]{1,0:T(8,128)(2,1)S(1)} %collective-permute-done.5.refs_1_), channel_id=1, source_target_pairs={{2,4},{4,6},{3,1},{5,3},{10,12},{12,14},{11,9},{13,11},{18,20},{20... | collective-permute-start | bytes 294920 | tf_op jit(solution)/shard_map/ppermute | solution.py:247
  29.8 3.5 %collective-permute-start.11 = (bf16[192,768]{1,0:T(8,128)(2,1)S(1)}, bf16[192,768]{1,0:T(8,128)(2,1)S(1)}, u32[]{:S(2)}, u32[]{:S(2)}) collective-permute-start(bf16[192,768]{1,0:T(8,128)(2,1)S(1)} %collective-permute-done.6.refs_2_), channel_id=1, source_target_pairs={{2,4},{4,6},{3,1},{5,3},{10,12},{12,14},{11,9},{13,11},{18,20},{20... | collective-permute-start | bytes 884744 | tf_op jit(solution)/shard_map/ppermute | solution.py:247
  30.5 2.9 %collective-permute-start.12 = (bf16[192,768]{1,0:T(8,128)(2,1)S(1)}, bf16[192,768]{1,0:T(8,128)(2,1)S(1)}, u32[]{:S(2)}, u32[]{:S(2)}) collective-permute-start(bf16[192,768]{1,0:T(8,128)(2,1)S(1)} %collective-permute-done.8.refs_3_), channel_id=1, source_target_pairs={{2,4},{4,6},{3,1},{5,3},{10,12},{12,14},{11,9},{13,11},{18,20},{20... | collective-permute-start | bytes 884744 | tf_op jit(solution)/shard_map/ppermute | solution.py:247
  35.5 0.9 %copy-start.3 = (f32[256,896]{1,0:T(8,128)}, f32[256,896]{1,0:T(8,128)S(1)}, u32[]{:S(2)}) copy-start(f32[256,896]{1,0:T(8,128)S(1)} %get-tuple-element.25.keep) | copy-start | bytes 2752516
  36.5 34.7 %collective-permute-start.13 = (f32[256,896]{1,0:T(8,128)S(1)}, f32[256,896]{1,0:T(8,128)S(1)}, u32[]{:S(2)}, u32[]{:S(2)}) collective-permute-start(f32[256,896]{1,0:T(8,128)S(1)} %get-tuple-element.26), channel_id=1, source_target_pairs={{0,1},{1,0},{2,3},{3,2},{4,5},{5,4},{6,7},{7,6},{8,9},{9,8},{10,11... | collective-permute-start | bytes 2752520 | tf_op jit(solution)/shard_map/ppermute | solution.py:247
  50.6 1.4 %collective-permute-start.16 = (bf16[192,768]{1,0:T(8,128)(2,1)S(1)}, bf16[192,768]{1,0:T(8,128)(2,1)S(1)}, u32[]{:S(2)}, u32[]{:S(2)}) collective-permute-start(bf16[192,768]{1,0:T(8,128)(2,1)S(1)} %collective-permute-done.11.refs_2_), channel_id=1, source_target_pairs={{4,6},{3,1},{12,14},{11,9},{20,22},{19,17},{28,30},{27,25}} | collective-permute-start | bytes 884744 | tf_op jit(solution)/shard_map/ppermute | solution.py:247
  51.3 7.9 %collective-permute-start.17 = (bf16[192,768]{1,0:T(8,128)(2,1)S(1)}, bf16[192,768]{1,0:T(8,128)(2,1)S(1)}, u32[]{:S(2)}, u32[]{:S(2)}) collective-permute-start(bf16[192,768]{1,0:T(8,128)(2,1)S(1)} %collective-permute-done.12.refs_3_), channel_id=1, source_target_pairs={{4,6},{3,1},{12,14},{11,9},{20,22},{19,17},{28,30},{27,25}} | collective-permute-start | bytes 884744 | tf_op jit(solution)/shard_map/ppermute | solution.py:247
  52.0 19.1 %collective-permute-start.20 = (bf16[192,768]{1,0:T(8,128)(2,1)S(1)}, bf16[192,768]{1,0:T(8,128)(2,1)S(1)}, u32[]{:S(2)}, u32[]{:S(2)}) collective-permute-start(bf16[192,768]{1,0:T(8,128)(2,1)S(1)} %collective-permute-done.16.refs_2_), channel_id=1, source_target_pairs={{0,1},{1,0},{2,3},{3,2},{4,5},{5,4},{6,7},{7,6},{8,9},{9,8},{10,11... | collective-permute-start | bytes 884744 | tf_op jit(solution)/shard_map/ppermute | solution.py:247
  59.2 11.9 %collective-permute-start.21 = (bf16[192,768]{1,0:T(8,128)(2,1)S(1)}, bf16[192,768]{1,0:T(8,128)(2,1)S(1)}, u32[]{:S(2)}, u32[]{:S(2)}) collective-permute-start(bf16[192,768]{1,0:T(8,128)(2,1)S(1)} %collective-permute-done.17.refs_3_), channel_id=1, source_target_pairs={{0,1},{1,0},{2,3},{3,2},{4,5},{5,4},{6,7},{7,6},{8,9},{9,8},{10,11... | collective-permute-start | bytes 884744 | tf_op jit(solution)/shard_map/ppermute | solution.py:247
  62.4 1.4 %collective-permute-start.14 = (bf16[64,768]{1,0:T(8,128)(2,1)S(1)}, bf16[64,768]{1,0:T(8,128)(2,1)S(1)}, u32[]{:S(2)}, u32[]{:S(2)}) collective-permute-start(bf16[64,768]{1,0:T(8,128)(2,1)S(1)} %collective-permute-done.9.refs_0_), channel_id=1, source_target_pairs={{4,6},{3,1},{12,14},{11,9},{20,22},{19,17},{28,30},{27,25}} | collective-permute-start | bytes 294920 | tf_op jit(solution)/shard_map/ppermute | solution.py:247
  63.0 5.8 %collective-permute-start.15 = (bf16[64,768]{1,0:T(8,128)(2,1)S(1)}, bf16[64,768]{1,0:T(8,128)(2,1)S(1)}, u32[]{:S(2)}, u32[]{:S(2)}) collective-permute-start(bf16[64,768]{1,0:T(8,128)(2,1)S(1)} %collective-permute-done.10.refs_1_), channel_id=1, source_target_pairs={{4,6},{3,1},{12,14},{11,9},{20,22},{19,17},{28,30},{27,25}} | collective-permute-start | bytes 294920 | tf_op jit(solution)/shard_map/ppermute | solution.py:247
  63.7 6.5 %collective-permute-start.18 = (bf16[64,768]{1,0:T(8,128)(2,1)S(1)}, bf16[64,768]{1,0:T(8,128)(2,1)S(1)}, u32[]{:S(2)}, u32[]{:S(2)}) collective-permute-start(bf16[64,768]{1,0:T(8,128)(2,1)S(1)} %collective-permute-done.14.refs_0_), channel_id=1, source_target_pairs={{0,1},{1,0},{2,3},{3,2},{4,5},{5,4},{6,7},{7,6},{8,9},{9,8},{10,11... | collective-permute-start | bytes 294920 | tf_op jit(solution)/shard_map/ppermute | solution.py:247
  68.9 2.2 %collective-permute-start.19 = (bf16[64,768]{1,0:T(8,128)(2,1)S(1)}, bf16[64,768]{1,0:T(8,128)(2,1)S(1)}, u32[]{:S(2)}, u32[]{:S(2)}) collective-permute-start(bf16[64,768]{1,0:T(8,128)(2,1)S(1)} %collective-permute-done.15.refs_1_), channel_id=1, source_target_pairs={{0,1},{1,0},{2,3},{3,2},{4,5},{5,4},{6,7},{7,6},{8,9},{9,8},{10,11... | collective-permute-start | bytes 294920 | tf_op jit(solution)/shard_map/ppermute | solution.py:247
  71.1 1.2 %copy-start.2 = (f32[2048,1]{1,0:T(8,128)S(1)}, f32[2048,1]{1,0:T(8,128)}, u32[]{:S(2)}) copy-start(f32[2048,1]{1,0:T(8,128)} %copy-done.1) | copy-start | bytes 24580
  72.4 1.2 %copy-start.4 = (f32[256,896]{1,0:T(8,128)S(1)}, f32[256,896]{1,0:T(8,128)}, u32[]{:S(2)}) copy-start(f32[256,896]{1,0:T(8,128)} %copy-done.3) | copy-start | bytes 2752516

commit v2 on v0

--- a/solution.py
+++ b/solution.py
@@ -1,12 +1,20 @@
+import functools
+import math
+
 import jax
 import jax.numpy as jnp
 from jax import lax
+from jax.experimental import pallas as pl
+from jax.experimental.pallas import tpu as pltpu
 from jax.sharding import PartitionSpec as P
 
 score_scale = 0.15
-
-
-def local(points, centroids, dest_group):
+lanes = 128
+exponent_scale = score_scale * math.log2(math.e)
+vmem_limit = 20 * 1024 * 1024
+
+
+def general(points, centroids, dest_group):
     group_count = lax.axis_size("group")
     member_count = lax.axis_size("member")
     point_rows = points.shape[0]
@@ -63,7 +71,306 @@
     return refined
 
 
+def vmem():
+    return pl.BlockSpec(memory_space=pltpu.VMEM)
+
+
+def hbm():
+    return pl.BlockSpec(memory_space=pltpu.HBM)
+
+
+def unread():
+    return pl.BlockSpec(memory_space=pl.ANY)
+
+
+def like(x):
+    return jax.ShapeDtypeStruct(x.shape, x.dtype)
+
+
+def join_kernel(after_n, *refs):
+    gather_rows(refs[after_n:-1], refs[-1])
+
+
+def join(parts, *after):
+    rows = sum(part.shape[0] for part in parts)
+    return pl.pallas_call(
+        functools.partial(join_kernel, len(after)),
+        out_shape=jax.ShapeDtypeStruct((rows, parts[0].shape[1]), parts[0].dtype),
+        in_specs=[unread()] * len(after) + [vmem()] * len(parts),
+        out_specs=vmem(),
+        compiler_params=pltpu.CompilerParams(vmem_limit_bytes=vmem_limit),
+        cost_estimate=cost(),
+        name="join",
+    )(*after, *parts)
+
+
+def pack_kernel(dest_from, points, *refs):
+    packed, (dest, rows, dest_arrival, arrival) = refs[:-4], refs[-4:]
+    dest_copy = pltpu.make_async_copy(dest_from, dest, dest_arrival)
+    dest_copy.start()
+    copy = pltpu.make_async_copy(points, rows, arrival)
+    copy.start()
+    count = len(packed)
+    row_count = rows.shape[0]
+    capacity = row_count // count
+    dest_copy.wait()
+    apart = jnp.bitwise_xor(dest[...], lax.axis_index("group"))
+    named = lax.broadcasted_iota(jnp.int32, (8, row_count), 0) == apart
+    row_at = lax.broadcasted_iota(jnp.int32, (row_count, row_count), 0)
+    col_at = lax.broadcasted_iota(jnp.int32, (row_count, row_count), 1)
+    before = (row_at < col_at).astype(jnp.bfloat16)
+    named = named.astype(jnp.float32)
+    earlier = jnp.dot(named.astype(jnp.bfloat16), before, preferred_element_type=jnp.float32)
+    rank = jnp.sum(earlier * named, axis=0, keepdims=True)
+    slot = apart * capacity + rank.astype(jnp.int32)
+    placement = (row_at == slot).astype(jnp.bfloat16)
+    copy.wait()
+    for k in range(count):
+        part = placement[k * capacity : (k + 1) * capacity]
+        packed[k][...] = jnp.dot(part, rows[...], preferred_element_type=jnp.float32).astype(
+            jnp.bfloat16
+        )
+
+
+def pack(dest_row, points, group_count):
+    row_count, feature_dim = points.shape
+    capacity = row_count // group_count
+    return pl.pallas_call(
+        pack_kernel,
+        out_shape=[jax.ShapeDtypeStruct((capacity, feature_dim), points.dtype)] * group_count,
+        in_specs=[hbm(), hbm()],
+        out_specs=[vmem()] * group_count,
+        scratch_shapes=[
+            pltpu.VMEM((1, row_count), jnp.int32),
+            pltpu.VMEM((row_count, feature_dim), points.dtype),
+            pltpu.SemaphoreType.DMA,
+            pltpu.SemaphoreType.DMA,
+        ],
+        compiler_params=pltpu.CompilerParams(vmem_limit_bytes=vmem_limit),
+        cost_estimate=cost(),
+        name="pack",
+    )(dest_row, points)
+
+
+def scaled_scores(table, half_norms, rows):
+    dims = (((1,), (1,)), ((), ()))
+    product = lax.dot_general(table, rows, dims, preferred_element_type=jnp.float32)
+    return exponent_scale * (product - half_norms)
+
+
+def softmax_terms(table, half_norms, rows, scores, tile):
+    row_count = rows.shape[0]
+    top = jnp.full((1, row_count), -jnp.inf, jnp.float32)
+    total = jnp.zeros((1, row_count), jnp.float32)
+    for start in range(0, table.shape[0], tile):
+        at = slice(start, start + tile)
+        block = scaled_scores(table[at, :], half_norms[at, :], rows)
+        scores[at, :] = block
+        higher = jnp.maximum(top, jnp.max(block, axis=0, keepdims=True))
+        here = jnp.sum(jnp.exp2(block - higher), axis=0, keepdims=True)
+        total = total * jnp.exp2(top - higher) + here
+        top = higher
+    return top, 1.0 / total
+
+
+def gather_rows(parts, rows):
+    start = 0
+    for part in parts:
+        rows[start : start + part.shape[0], :] = part[...]
+        start += part.shape[0]
+
+
+def tile_sums(scores, top, inverse, rows):
+    weights = (jnp.exp2(scores - top) * inverse).astype(jnp.bfloat16)
+    sums = jnp.dot(weights, rows, preferred_element_type=jnp.float32)
+    count = jnp.sum(weights.astype(jnp.float32), axis=1, keepdims=True)
+    return sums, jnp.broadcast_to(count, (count.shape[0], lanes))
+
+
+def at_tile(index, tile):
+    return pl.ds(pl.multiple_of(index * tile, tile), tile)
+
+
+def chip_place():
+    member = lax.axis_index("member")
+    core = member % 2
+    return member // 2, core, member, member + 1 - 2 * core
+
+
+def two_tiles(table, half_norms, rows, scores, before, after, tile):
+    feature_dim = rows.shape[1]
+    _, _, mine, other = chip_place()
+    terms = softmax_terms(table, half_norms, rows, scores, tile)
+    for index, so_far, out in zip((mine, other), before, after):
+        sums, count = tile_sums(scores[at_tile(index, tile), :], *terms, rows)
+        if so_far is not None:
+            sums = sums + so_far[:, :feature_dim]
+            count = count + so_far[:, feature_dim:]
+        out[:, :feature_dim] = sums
+        out[:, feature_dim:] = count
+
+
+def own_kernel(tile, table, rows, keep, give, half_norms, scores):
+    for start in range(0, table.shape[0], tile):
+        block = table[start : start + tile, :].astype(jnp.float32)
+        half_norms[start : start + tile, :] = 0.5 * jnp.sum(block * block, axis=1, keepdims=True)
+    two_tiles(table, half_norms, rows[...], scores, (None, None), (keep, give), tile)
+
+
+def step_kernel(tile, step, depth, table, half_norms, keep_in, give_in, rows, keep, give, scores):
+    level, core, _, _ = chip_place()
+    here = ((core == 0) & (level >= step)) | ((core == 1) & (level < depth - step))
+
+    @pl.when(jnp.logical_not(here))
+    def _():
+        keep[...] = keep_in[...]
+        give[...] = give_in[...]
+
+    @pl.when(here)
+    def _():
+        two_tiles(table, half_norms, rows[...], scores, (keep_in, give_in), (keep, give), tile)
+
+
+def last_sums(tile, depth, table, half_norms, came, passed, rows, scores):
+    level, core, mine, _ = chip_place()
+    here = ((core == 0) & (level == depth - 1)) | ((core == 1) & (level == 0))
+
+    @pl.when(here)
+    def _():
+        rows[...] = came[...]
+
+    @pl.when(jnp.logical_not(here))
+    def _():
+        rows[...] = passed[...]
+
+    all_rows = rows[...]
+    terms = softmax_terms(table, half_norms, all_rows, scores, tile)
+    return tile_sums(scores[at_tile(mine, tile), :], *terms, all_rows)
+
+
+def end_chip(depth):
+    level = chip_place()[0]
+    return (level == 0) | (level == depth - 1)
+
+
+def end_kernel(tile, depth, table, half_norms, keep_in, came, passed, keep, rows, scores):
+    feature_dim = rows.shape[1]
+
+    @pl.when(jnp.logical_not(end_chip(depth)))
+    def _():
+        keep[...] = keep_in[...]
+
+    @pl.when(end_chip(depth))
+    def _():
+        sums, count = last_sums(tile, depth, table, half_norms, came, passed, rows, scores)
+        keep[:, :feature_dim] = keep_in[:, :feature_dim] + sums
+        keep[:, feature_dim:] = keep_in[:, feature_dim:] + count
+
+
+def refit_kernel(tile, depth, table, half_norms, keep, got, came, passed, refined, rows, scores):
+    feature_dim = rows.shape[1]
+    mine = chip_place()[2]
+    old = table[at_tile(mine, tile), :].astype(jnp.float32)
+
+    def refit(more, count):
+        sums = keep[:, :feature_dim] + got[:, :feature_dim] + more
+        count = keep[:, feature_dim:] + got[:, feature_dim:] + count
+        scale = 1.0 / (count[:, :1] + 1.0)
+        refined[...] = ((sums + old) * scale).astype(jnp.bfloat16)
+
+    @pl.when(jnp.logical_not(end_chip(depth)))
+    def _():
+        refit(0.0, 0.0)
+
+    @pl.when(end_chip(depth))
+    def _():
+        refit(*last_sums(tile, depth, table, half_norms, came, passed, rows, scores))
+
+
+def cost():
+    return pl.CostEstimate(flops=1 << 20, bytes_accessed=0, transcendentals=0)
+
+
+def handoff(points, centroids, dest_group):
+    group_count = lax.axis_size("group")
+    member_count = lax.axis_size("member")
+    depth = member_count // 2
+    row_count, feature_dim = points.shape
+    fine_count = centroids.shape[0]
+    tile = fine_count // member_count
+
+    def swap(x):
+        return lax.ppermute(x, "member", [(i, i ^ 1) for i in range(member_count)])
+
+    def onward(x, step):
+        up = [(2 * z, 2 * z + 2) for z in range(step - 1, depth - 1)]
+        down = [(2 * z + 3, 2 * z + 1) for z in range(0, depth - step)]
+        return lax.ppermute(x, "member", up + down)
+
+    sums_shape = jax.ShapeDtypeStruct((tile, feature_dim + lanes), jnp.float32)
+    norms_shape = jax.ShapeDtypeStruct((fine_count, 1), jnp.float32)
+
+    def kernel(body, out_shape, *operands, scratch_rows=0, aliases={}):
+        scratch = [pltpu.VMEM((fine_count, row_count), jnp.float32)]
+        if scratch_rows:
+            scratch = [pltpu.VMEM((scratch_rows, feature_dim), jnp.bfloat16)] + scratch
+        return pl.pallas_call(
+            body,
+            out_shape=out_shape,
+            in_specs=[vmem()] * len(operands),
+            out_specs=jax.tree.map(lambda _: vmem(), out_shape),
+            scratch_shapes=scratch,
+            input_output_aliases=aliases,
+            compiler_params=pltpu.CompilerParams(vmem_limit_bytes=vmem_limit),
+            cost_estimate=cost(),
+            name=body.func.__name__,
+        )(*operands)
+
+    packed = pack(dest_group.reshape(1, row_count), points, group_count)
+    fetched = [
+        lax.ppermute(packed[k], "group", [(i, i ^ k) for i in range(group_count)])
+        for k in reversed(range(1, group_count))
+    ]
+    own = join([packed[0]] + fetched)
+    first, second = onward(own, 1), onward(swap(own), 1)
+    keep, give, half_norms = kernel(
+        functools.partial(own_kernel, tile), [sums_shape, sums_shape, norms_shape], centroids, own
+    )
+    for step in range(1, depth - 1):
+        held = join([first], keep)
+        next_first = onward(held, step + 1)
+        body = functools.partial(step_kernel, tile, step, depth)
+        keep, give = kernel(
+            body, [sums_shape] * 2, centroids, half_norms, keep, give, held, aliases={2: 0, 3: 1}
+        )
+        held = join([second], keep)
+        next_second = onward(held, step + 1)
+        keep, give = kernel(
+            body, [sums_shape] * 2, centroids, half_norms, keep, give, held, aliases={2: 0, 3: 1}
+        )
+        first, second = next_first, next_second
+
+    got = swap(give)
+    held = join([first], keep)
+    keep = kernel(
+        functools.partial(end_kernel, tile, depth), sums_shape, centroids, half_norms, keep, held,
+        swap(held), scratch_rows=row_count, aliases={2: 0},
+    )
+    held = join([second], keep)
+    return kernel(
+        functools.partial(refit_kernel, tile, depth),
+        jax.ShapeDtypeStruct((tile, feature_dim), jnp.bfloat16),
+        centroids, half_norms, keep, got, held, swap(held), scratch_rows=row_count,
+    )
+
+
 def solution(mesh):
+    def local(points, centroids, dest_group):
+        groups, members = mesh.shape["group"], mesh.shape["member"]
+        if groups * (points.shape[0] // 4) == points.shape[0] and 6 <= members <= 16:
+            return handoff(points, centroids, dest_group)
+        return general(points, centroids, dest_group)
+
     return jax.shard_map(
         local,
         mesh=mesh,

time: 119 us -> 53.9 us (0.45)
  the two profiles are of different devices: /device:TPU:0 before, /device:TPU:25 now
where the time goes in v2:
time: 53.9 us; the launch traced here: 53.6 us
  starting transfers between devices  33.5 us (62%)
  waiting for transfers between devices  8.74 us (16%)
  Pallas kernels  7.54 us (14%)
  local copies, waits for them, and re-layouts  3.56 us (7%)
    ppermute x4, starting transfers between devices, swap(): return lax.ppermute(x, 'member', [(i, i ^ 1) for i in range(member_count)])  23.9 us
    ppermute x6, starting transfers between devices, onward(): return lax.ppermute(x, 'member', up + down)  6.89 us
    pallas_call x7, Pallas kernels, kernel(): pl.pallas_call(body, out_shape=out_shape, in_specs=[vmem()] * len(operand...  6.57 us
    ppermute x3, waiting for transfers between devices, handoff(): lax.ppermute(packed[k], 'group', [(i, i ^ k) for i in range(group_count)])  4.7 us
    unnamed x8, local copies, waits for them, and re-layouts  3.56 us
    ppermute x3, starting transfers between devices, handoff(): lax.ppermute(packed[k], 'group', [(i, i ^ k) for i in range(group_count)])  2.71 us
    ppermute x4, waiting for transfers between devices, swap(): return lax.ppermute(x, 'member', [(i, i ^ 1) for i in range(member_count)])  2.02 us
    ppermute x6, waiting for transfers between devices, onward(): return lax.ppermute(x, 'member', up + down)  2.02 us
  transfers between devices with their start and end apart: 13, of which 5 were waited for; matrix products, arithmetic and copies ran while one was open for 0% of the time, Pallas kernels for 8%

profile of v2, /device:TPU:25, one launch (start us, length us, event | category | flops | bytes accessed | tf_op | source)
XLA Modules:
  0.0 53.6 jit_solution(10354475941362638082)
XLA Ops:
  0.0 0.0 copy-start.2
  0.0 1.0 %copy-done.2 = bf16[256,768]{1,0:T(8,128)(2,1)S(1)} copy-done((bf16[256,768]{1,0:T(8,128)(2,1)S(1)}, bf16[256,768]{1,0:T(8,128)(2,1)}, u32[]{:S(2)}) %copy-start.2) | copy-done | bytes 393240
  1.0 0.0 copy-start.3
  1.0 0.7 %copy-done.3 = s32[256,1]{0,1:T(1,128)S(1)} copy-done((s32[256,1]{0,1:T(1,128)S(1)}, s32[256,1]{0,1:T(1,128)}, u32[]{:S(2)}) %copy-start.3) | copy-done | bytes 1048
  1.7 0.8 %pack.1 = (bf16[64,768]{1,0:T(8,128)(2,1)S(1)}, bf16[64,768]{1,0:T(8,128)(2,1)S(1)}, bf16[64,768]{1,0:T(8,128)(2,1)S(1)}, bf16[64,768]{1,0:T(8,128)(2,1)S(1)}) custom-call(s32[1,256]{1,0:T(1,128)S(1)} %bitcast.1, bf16[256,768]{1,0:T(8,128)(2,1)S(1)} %copy-done.2), custom_call_target="tpu_custom_call" | custom-call | flops 1048576 | tf_op jit(solution)/shard_map/pack/pallas_call | solution.py:138
  2.5 2.2 %collective-permute-start = (bf16[64,768]{1,0:T(8,128)(2,1)S(1)}, bf16[64,768]{1,0:T(8,128)(2,1)S(1)}, u32[]{:S(2)}, u32[]{:S(2)}) collective-permute-start(bf16[64,768]{1,0:T(8,128)(2,1)S(1)} %get-tuple-element.21), channel_id=1, source_target_pairs={{0,24},{8,16},{16,8},{24,0},{1,25},{9,17},{17,9},{25,1},{2,26},{10... | collective-permute-start | bytes 294920 | tf_op jit(solution)/shard_map/ppermute | solution.py:331
  4.7 0.2 collective-permute-start.1
  4.9 0.3 collective-permute-start.2
  5.2 1.7 %collective-permute-done.refs_1_ = bf16[64,768]{1,0:T(8,128)(2,1)S(1)} collective-permute-done((bf16[64,768]{1,0:T(8,128)(2,1)S(1)}, bf16[64,768]{1,0:T(8,128)(2,1)S(1)}, u32[]{:S(2)}, u32[]{:S(2)}) %collective-permute-start) | collective-permute-done | bytes 98336 | tf_op jit(solution)/shard_map/ppermute | solution.py:331
  6.9 3.0 %collective-permute-done.1.refs_2_ = bf16[64,768]{1,0:T(8,128)(2,1)S(1)} collective-permute-done((bf16[64,768]{1,0:T(8,128)(2,1)S(1)}, bf16[64,768]{1,0:T(8,128)(2,1)S(1)}, u32[]{:S(2)}, u32[]{:S(2)}) %collective-permute-start.1) | collective-permute-done | bytes 98336 | tf_op jit(solution)/shard_map/ppermute | solution.py:331
  9.9 0.0 collective-permute-done.2.refs_3_
  9.9 1.1 %collective-permute-start.4 = (bf16[256,768]{1,0:T(8,128)(2,1)S(1)}, bf16[256,768]{1,0:T(8,128)(2,1)S(1)}, u32[]{:S(2)}, u32[]{:S(2)}) collective-permute-start(bf16[256,768]{1,0:T(8,128)(2,1)S(1)} %join.7.rows), channel_id=1, source_target_pairs={{0,1},{1,0},{2,3},{3,2},{4,5},{5,4},{6,7},{7,6},{8,9},{9,8},{10,11... | collective-permute-start | bytes 1179656 | tf_op jit(solution)/shard_map/ppermute | solution.py:303
  11.0 2.1 %collective-permute-start.3 = (bf16[256,768]{1,0:T(8,128)(2,1)S(1)}, bf16[256,768]{1,0:T(8,128)(2,1)S(1)}, u32[]{:S(2)}, u32[]{:S(2)}) collective-permute-start(bf16[256,768]{1,0:T(8,128)(2,1)S(1)} %join.7.rows), channel_id=1, source_target_pairs={{0,2},{2,4},{4,6},{3,1},{5,3},{7,5},{8,10},{10,12},{12,14},{11,9},... | collective-permute-start | bytes 1179656 | tf_op jit(solution)/shard_map/ppermute | solution.py:308
  13.1 0.0 collective-permute-done.4
  13.1 2.1 %collective-permute-start.5 = (bf16[256,768]{1,0:T(8,128)(2,1)S(1)}, bf16[256,768]{1,0:T(8,128)(2,1)S(1)}, u32[]{:S(2)}, u32[]{:S(2)}) collective-permute-start(bf16[256,768]{1,0:T(8,128)(2,1)S(1)} %collective-permute-done.4), channel_id=1, source_target_pairs={{0,2},{2,4},{4,6},{3,1},{5,3},{7,5},{8,10},{10,12},{12,14},{11,9},... | collective-permute-start | bytes 1179656 | tf_op jit(solution)/shard_map/ppermute | solution.py:308
  15.2 0.0 copy-start
  15.2 1.9 %copy-done = bf16[2048,768]{1,0:T(8,128)(2,1)S(1)} copy-done((bf16[2048,768]{1,0:T(8,128)(2,1)S(1)}, bf16[2048,768]{1,0:T(8,128)(2,1)}, u32[]{:S(2)}) %copy-start) | copy-done | bytes 3145752
  17.1 0.0 copy-start.1
  17.1 1.9 %own_kernel.1 = (f32[256,896]{1,0:T(8,128)S(1)}, f32[256,896]{1,0:T(8,128)S(1)}, f32[2048,1]{1,0:T(8,128)S(1)}) custom-call(bf16[2048,768]{1,0:T(8,128)(2,1)S(1)} %copy-done, bf16[256,768]{1,0:T(8,128)(2,1)S(1)} %join.7.rows), custom_call_target="tpu_custom_call" | custom-call | flops 1048576 | tf_op jit(solution)/shard_map/own_kernel/pallas_call | solution.py:317
  19.0 0.0 collective-permute-done.3.refs_1_
  19.0 0.7 %collective-permute-start.6 = (bf16[256,768]{1,0:T(8,128)(2,1)S(1)}, bf16[256,768]{1,0:T(8,128)(2,1)S(1)}, u32[]{:S(2)}, u32[]{:S(2)}) collective-permute-start(bf16[256,768]{1,0:T(8,128)(2,1)S(1)} %join.8.rows), channel_id=1, source_target_pairs={{2,4},{4,6},{3,1},{5,3},{10,12},{12,14},{11,9},{13,11},{18,20},{20... | collective-permute-start | bytes 1179656 | tf_op jit(solution)/shard_map/ppermute | solution.py:308
  19.7 0.0 copy-done.1
  19.7 0.2 step_kernel.4
  20.0 2.0 %collective-permute-done.5.refs_1_ = bf16[256,768]{1,0:T(8,128)(2,1)S(1)} collective-permute-done((bf16[256,768]{1,0:T(8,128)(2,1)S(1)}, bf16[256,768]{1,0:T(8,128)(2,1)S(1)}, u32[]{:S(2)}, u32[]{:S(2)}) %collective-permute-start.5) | collective-permute-done | bytes 393248 | tf_op jit(solution)/shard_map/ppermute | solution.py:308
  22.0 0.7 %collective-permute-start.7 = (bf16[256,768]{1,0:T(8,128)(2,1)S(1)}, bf16[256,768]{1,0:T(8,128)(2,1)S(1)}, u32[]{:S(2)}, u32[]{:S(2)}) collective-permute-start(bf16[256,768]{1,0:T(8,128)(2,1)S(1)} %join.9.rows), channel_id=1, source_target_pairs={{2,4},{4,6},{3,1},{5,3},{10,12},{12,14},{11,9},{13,11},{18,20},{20... | collective-permute-start | bytes 1179656 | tf_op jit(solution)/shard_map/ppermute | solution.py:308
  22.7 0.2 step_kernel.5
  23.0 0.0 collective-permute-done.6.refs_1_
  23.0 0.7 %collective-permute-start.8 = (bf16[256,768]{1,0:T(8,128)(2,1)S(1)}, bf16[256,768]{1,0:T(8,128)(2,1)S(1)}, u32[]{:S(2)}, u32[]{:S(2)}) collective-permute-start(bf16[256,768]{1,0:T(8,128)(2,1)S(1)} %join.10.rows), channel_id=1, source_target_pairs={{4,6},{3,1},{12,14},{11,9},{20,22},{19,17},{28,30},{27,25}} | collective-permute-start | bytes 1179656 | tf_op jit(solution)/shard_map/ppermute | solution.py:308
  23.7 0.2 step_kernel.6
  24.0 0.0 collective-permute-done.7.refs_1_
  24.0 0.2 step_kernel.7
  24.3 12.0 %collective-permute-start.10 = (f32[256,896]{1,0:T(8,128)S(1)}, f32[256,896]{1,0:T(8,128)S(1)}, u32[]{:S(2)}, u32[]{:S(2)}) collective-permute-start(f32[256,896]{1,0:T(8,128)S(1)} %get-tuple-element.34), channel_id=1, source_target_pairs={{0,1},{1,0},{2,3},{3,2},{4,5},{5,4},{6,7},{7,6},{8,9},{9,8},{10,11... | collective-permute-start | bytes 2752520 | tf_op jit(solution)/shard_map/ppermute | solution.py:303
  36.3 0.0 collective-permute-done.8.refs_1_
  36.3 3.9 %collective-permute-start.9 = (bf16[256,768]{1,0:T(8,128)(2,1)S(1)}, bf16[256,768]{1,0:T(8,128)(2,1)S(1)}, u32[]{:S(2)}, u32[]{:S(2)}) collective-permute-start(bf16[256,768]{1,0:T(8,128)(2,1)S(1)} %join.12.came), channel_id=1, source_target_pairs={{0,1},{1,0},{2,3},{3,2},{4,5},{5,4},{6,7},{7,6},{8,9},{9,8},{10,11... | collective-permute-start | bytes 1179656 | tf_op jit(solution)/shard_map/ppermute | solution.py:303
  40.2 0.7 %collective-permute-start.11 = (bf16[256,768]{1,0:T(8,128)(2,1)S(1)}, bf16[256,768]{1,0:T(8,128)(2,1)S(1)}, u32[]{:S(2)}, u32[]{:S(2)}) collective-permute-start(bf16[256,768]{1,0:T(8,128)(2,1)S(1)} %join.11.rows), channel_id=1, source_target_pairs={{4,6},{3,1},{12,14},{11,9},{20,22},{19,17},{28,30},{27,25}} | collective-permute-start | bytes 1179656 | tf_op jit(solution)/shard_map/ppermute | solution.py:308
  40.9 0.7 %collective-permute-done.9.passed = bf16[256,768]{1,0:T(8,128)(2,1)S(1)} collective-permute-done((bf16[256,768]{1,0:T(8,128)(2,1)S(1)}, bf16[256,768]{1,0:T(8,128)(2,1)S(1)}, u32[]{:S(2)}, u32[]{:S(2)}) %collective-permute-start.9) | collective-permute-done | bytes 393248 | tf_op jit(solution)/shard_map/ppermute | solution.py:303
  41.5 1.4 %end_kernel.1.refs_0_.keep = f32[256,896]{1,0:T(8,128)S(1)} custom-call(bf16[2048,768]{1,0:T(8,128)(2,1)S(1)} %copy-done.1, f32[2048,1]{1,0:T(8,128)S(1)} %get-tuple-element.24.half_norms, f32[256,896]{1,0:T(8,128)S(1)} %get-tuple-element.33.refs_0_.keep_in, bf16[256,768]{1,0:T(8,128)(2,1)S(1)} %join.12.came, ...), custom_call_target="tpu_custom_call", output_to_operand_aliasing={{}: (2, {})} | custom-call | flops 1048576 | tf_op jit(solution)/shard_map/end_kernel/pallas_call | solution.py:317
  43.0 0.0 collective-permute-done.11.refs_1_
  43.0 6.9 %collective-permute-start.12 = (bf16[256,768]{1,0:T(8,128)(2,1)S(1)}, bf16[256,768]{1,0:T(8,128)(2,1)S(1)}, u32[]{:S(2)}, u32[]{:S(2)}) collective-permute-start(bf16[256,768]{1,0:T(8,128)(2,1)S(1)} %join.13.came), channel_id=1, source_target_pairs={{0,1},{1,0},{2,3},{3,2},{4,5},{5,4},{6,7},{7,6},{8,9},{9,8},{10,11... | collective-permute-start | bytes 1179656 | tf_op jit(solution)/shard_map/ppermute | solution.py:303
  50.0 1.3 %collective-permute-done.12.passed = bf16[256,768]{1,0:T(8,128)(2,1)S(1)} collective-permute-done((bf16[256,768]{1,0:T(8,128)(2,1)S(1)}, bf16[256,768]{1,0:T(8,128)(2,1)S(1)}, u32[]{:S(2)}, u32[]{:S(2)}) %collective-permute-start.12) | collective-permute-done | bytes 393248 | tf_op jit(solution)/shard_map/ppermute | solution.py:303
  51.3 0.0 collective-permute-done.10.got
  51.3 2.3 %refit_kernel.1 = bf16[256,768]{1,0:T(8,128)(2,1)} custom-call(bf16[2048,768]{1,0:T(8,128)(2,1)S(1)} %copy-done.1, f32[2048,1]{1,0:T(8,128)S(1)} %get-tuple-element.24.half_norms, f32[256,896]{1,0:T(8,128)S(1)} %end_kernel.1.refs_0_.keep, f32[256,896]{1,0:T(8,128)S(1)} %collective-permute-done.10.got, bf16[256,768]{1,0:T(8,128)(2,1)S(1)} %join.13.came, ...), custom_call_target="tpu_custom_call" | custom-call | flops 1048576 | tf_op jit(solution)/shard_map/refit_kernel/pallas_call | solution.py:317
  (7 shorter events, 0.2 us)
Async XLA Ops:
  0.0 1.0 %copy-start.2 = (bf16[256,768]{1,0:T(8,128)(2,1)S(1)}, bf16[256,768]{1,0:T(8,128)(2,1)}, u32[]{:S(2)}) copy-start(bf16[256,768]{1,0:T(8,128)(2,1)} %points.1) | copy-start | bytes 1179652
  1.0 0.7 %copy-start.3 = (s32[256,1]{0,1:T(1,128)S(1)}, s32[256,1]{0,1:T(1,128)}, u32[]{:S(2)}) copy-start(s32[256,1]{0,1:T(1,128)} %param.5) | copy-start | bytes 3076
  2.5 4.4 %collective-permute-start = (bf16[64,768]{1,0:T(8,128)(2,1)S(1)}, bf16[64,768]{1,0:T(8,128)(2,1)S(1)}, u32[]{:S(2)}, u32[]{:S(2)}) collective-permute-start(bf16[64,768]{1,0:T(8,128)(2,1)S(1)} %get-tuple-element.21), channel_id=1, source_target_pairs={{0,24},{8,16},{16,8},{24,0},{1,25},{9,17},{17,9},{25,1},{2,26},{10... | collective-permute-start | bytes 294920 | tf_op jit(solution)/shard_map/ppermute | solution.py:331
  4.7 5.2 %collective-permute-start.1 = (bf16[64,768]{1,0:T(8,128)(2,1)S(1)}, bf16[64,768]{1,0:T(8,128)(2,1)S(1)}, u32[]{:S(2)}, u32[]{:S(2)}) collective-permute-start(bf16[64,768]{1,0:T(8,128)(2,1)S(1)} %get-tuple-element.22), channel_id=1, source_target_pairs={{0,16},{8,24},{16,0},{24,8},{1,17},{9,25},{17,1},{25,9},{2,18},{10... | collective-permute-start | bytes 294920 | tf_op jit(solution)/shard_map/ppermute | solution.py:331
  4.9 5.0 %collective-permute-start.2 = (bf16[64,768]{1,0:T(8,128)(2,1)S(1)}, bf16[64,768]{1,0:T(8,128)(2,1)S(1)}, u32[]{:S(2)}, u32[]{:S(2)}) collective-permute-start(bf16[64,768]{1,0:T(8,128)(2,1)S(1)} %get-tuple-element.23), channel_id=1, source_target_pairs={{0,8},{8,0},{16,24},{24,16},{1,9},{9,1},{17,25},{25,17},{2,10},{10... | collective-permute-start | bytes 294920 | tf_op jit(solution)/shard_map/ppermute | solution.py:331
  9.9 3.2 %collective-permute-start.4 = (bf16[256,768]{1,0:T(8,128)(2,1)S(1)}, bf16[256,768]{1,0:T(8,128)(2,1)S(1)}, u32[]{:S(2)}, u32[]{:S(2)}) collective-permute-start(bf16[256,768]{1,0:T(8,128)(2,1)S(1)} %join.7.rows), channel_id=1, source_target_pairs={{0,1},{1,0},{2,3},{3,2},{4,5},{5,4},{6,7},{7,6},{8,9},{9,8},{10,11... | collective-permute-start | bytes 1179656 | tf_op jit(solution)/shard_map/ppermute | solution.py:303
  11.0 8.0 %collective-permute-start.3 = (bf16[256,768]{1,0:T(8,128)(2,1)S(1)}, bf16[256,768]{1,0:T(8,128)(2,1)S(1)}, u32[]{:S(2)}, u32[]{:S(2)}) collective-permute-start(bf16[256,768]{1,0:T(8,128)(2,1)S(1)} %join.7.rows), channel_id=1, source_target_pairs={{0,2},{2,4},{4,6},{3,1},{5,3},{7,5},{8,10},{10,12},{12,14},{11,9},... | collective-permute-start | bytes 1179656 | tf_op jit(solution)/shard_map/ppermute | solution.py:308
  13.1 8.9 %collective-permute-start.5 = (bf16[256,768]{1,0:T(8,128)(2,1)S(1)}, bf16[256,768]{1,0:T(8,128)(2,1)S(1)}, u32[]{:S(2)}, u32[]{:S(2)}) collective-permute-start(bf16[256,768]{1,0:T(8,128)(2,1)S(1)} %collective-permute-done.4), channel_id=1, source_target_pairs={{0,2},{2,4},{4,6},{3,1},{5,3},{7,5},{8,10},{10,12},{12,14},{11,9},... | collective-permute-start | bytes 1179656 | tf_op jit(solution)/shard_map/ppermute | solution.py:308
  15.2 1.9 %copy-start = (bf16[2048,768]{1,0:T(8,128)(2,1)S(1)}, bf16[2048,768]{1,0:T(8,128)(2,1)}, u32[]{:S(2)}) copy-start(bf16[2048,768]{1,0:T(8,128)(2,1)} %table.13) | copy-start | bytes 9437188
  17.1 2.6 %copy-start.1 = (bf16[2048,768]{1,0:T(8,128)(2,1)S(1)}, bf16[2048,768]{1,0:T(8,128)(2,1)}, u32[]{:S(2)}) copy-start(bf16[2048,768]{1,0:T(8,128)(2,1)} %table.13) | copy-start | bytes 9437188
  19.0 3.9 %collective-permute-start.6 = (bf16[256,768]{1,0:T(8,128)(2,1)S(1)}, bf16[256,768]{1,0:T(8,128)(2,1)S(1)}, u32[]{:S(2)}, u32[]{:S(2)}) collective-permute-start(bf16[256,768]{1,0:T(8,128)(2,1)S(1)} %join.8.rows), channel_id=1, source_target_pairs={{2,4},{4,6},{3,1},{5,3},{10,12},{12,14},{11,9},{13,11},{18,20},{20... | collective-permute-start | bytes 1179656 | tf_op jit(solution)/shard_map/ppermute | solution.py:308
  22.0 1.9 %collective-permute-start.7 = (bf16[256,768]{1,0:T(8,128)(2,1)S(1)}, bf16[256,768]{1,0:T(8,128)(2,1)S(1)}, u32[]{:S(2)}, u32[]{:S(2)}) collective-permute-start(bf16[256,768]{1,0:T(8,128)(2,1)S(1)} %join.9.rows), channel_id=1, source_target_pairs={{2,4},{4,6},{3,1},{5,3},{10,12},{12,14},{11,9},{13,11},{18,20},{20... | collective-permute-start | bytes 1179656 | tf_op jit(solution)/shard_map/ppermute | solution.py:308
  23.0 13.3 %collective-permute-start.8 = (bf16[256,768]{1,0:T(8,128)(2,1)S(1)}, bf16[256,768]{1,0:T(8,128)(2,1)S(1)}, u32[]{:S(2)}, u32[]{:S(2)}) collective-permute-start(bf16[256,768]{1,0:T(8,128)(2,1)S(1)} %join.10.rows), channel_id=1, source_target_pairs={{4,6},{3,1},{12,14},{11,9},{20,22},{19,17},{28,30},{27,25}} | collective-permute-start | bytes 1179656 | tf_op jit(solution)/shard_map/ppermute | solution.py:308
  24.3 27.0 %collective-permute-start.10 = (f32[256,896]{1,0:T(8,128)S(1)}, f32[256,896]{1,0:T(8,128)S(1)}, u32[]{:S(2)}, u32[]{:S(2)}) collective-permute-start(f32[256,896]{1,0:T(8,128)S(1)} %get-tuple-element.34), channel_id=1, source_target_pairs={{0,1},{1,0},{2,3},{3,2},{4,5},{5,4},{6,7},{7,6},{8,9},{9,8},{10,11... | collective-permute-start | bytes 2752520 | tf_op jit(solution)/shard_map/ppermute | solution.py:303
  36.3 5.2 %collective-permute-start.9 = (bf16[256,768]{1,0:T(8,128)(2,1)S(1)}, bf16[256,768]{1,0:T(8,128)(2,1)S(1)}, u32[]{:S(2)}, u32[]{:S(2)}) collective-permute-start(bf16[256,768]{1,0:T(8,128)(2,1)S(1)} %join.12.came), channel_id=1, source_target_pairs={{0,1},{1,0},{2,3},{3,2},{4,5},{5,4},{6,7},{7,6},{8,9},{9,8},{10,11... | collective-permute-start | bytes 1179656 | tf_op jit(solution)/shard_map/ppermute | solution.py:303
  40.2 2.8 %collective-permute-start.11 = (bf16[256,768]{1,0:T(8,128)(2,1)S(1)}, bf16[256,768]{1,0:T(8,128)(2,1)S(1)}, u32[]{:S(2)}, u32[]{:S(2)}) collective-permute-start(bf16[256,768]{1,0:T(8,128)(2,1)S(1)} %join.11.rows), channel_id=1, source_target_pairs={{4,6},{3,1},{12,14},{11,9},{20,22},{19,17},{28,30},{27,25}} | collective-permute-start | bytes 1179656 | tf_op jit(solution)/shard_map/ppermute | solution.py:308
  43.0 8.3 %collective-permute-start.12 = (bf16[256,768]{1,0:T(8,128)(2,1)S(1)}, bf16[256,768]{1,0:T(8,128)(2,1)S(1)}, u32[]{:S(2)}, u32[]{:S(2)}) collective-permute-start(bf16[256,768]{1,0:T(8,128)(2,1)S(1)} %join.13.came), channel_id=1, source_target_pairs={{0,1},{1,0},{2,3},{3,2},{4,5},{5,4},{6,7},{7,6},{8,9},{9,8},{10,11... | collective-permute-start | bytes 1179656 | tf_op jit(solution)/shard_map/ppermute | solution.py:303

commit v3 on v2

--- a/solution.py
+++ b/solution.py
@@ -102,6 +102,31 @@
         cost_estimate=cost(),
         name="join",
     )(*after, *parts)
+
+
+def pick_kernel(depth, own, came, after, out):
+    level, core, _, _ = chip_place()
+    forwards = ((core == 0) & (level == depth - 2)) | ((core == 1) & (level == 1))
+
+    @pl.when(forwards)
+    def _():
+        out[...] = came[...]
+
+    @pl.when(jnp.logical_not(forwards))
+    def _():
+        out[...] = own[...]
+
+
+def pick(depth, own, came, after):
+    return pl.pallas_call(
+        functools.partial(pick_kernel, depth),
+        out_shape=like(own),
+        in_specs=[vmem(), vmem(), unread()],
+        out_specs=vmem(),
+        compiler_params=pltpu.CompilerParams(vmem_limit_bytes=vmem_limit),
+        cost_estimate=cost(),
+        name="pick",
+    )(own, came, after)
 
 
 def pack_kernel(dest_from, points, *refs):
@@ -176,6 +201,8 @@
 def gather_rows(parts, rows):
     start = 0
     for part in parts:
+        if part is rows:
+            return
         rows[start : start + part.shape[0], :] = part[...]
         start += part.shape[0]
 
@@ -197,55 +224,43 @@
     return member // 2, core, member, member + 1 - 2 * core
 
 
-def two_tiles(table, half_norms, rows, scores, before, after, tile):
-    feature_dim = rows.shape[1]
-    _, _, mine, other = chip_place()
-    terms = softmax_terms(table, half_norms, rows, scores, tile)
-    for index, so_far, out in zip((mine, other), before, after):
-        sums, count = tile_sums(scores[at_tile(index, tile), :], *terms, rows)
-        if so_far is not None:
-            sums = sums + so_far[:, :feature_dim]
-            count = count + so_far[:, feature_dim:]
-        out[:, :feature_dim] = sums
-        out[:, feature_dim:] = count
-
-
-def own_kernel(tile, table, rows, keep, give, half_norms, scores):
+def add_rows(table, half_norms, parts, rows, scores, sums, tile):
+    feature_dim = table.shape[1]
+    gather_rows(parts, rows)
+    count = sum(part.shape[0] for part in parts)
+    all_rows = rows[:count, :]
+    scores = scores.at[:, :count]
+    terms = softmax_terms(table, half_norms, all_rows, scores, tile)
+    for index, out in sums:
+        more, count = tile_sums(scores[at_tile(index, tile), :], *terms, all_rows)
+        out[:, :feature_dim] += more
+        out[:, feature_dim:] += count
+
+
+def own_kernel(tile, table, own, keep, give, half_norms, rows, scores):
     for start in range(0, table.shape[0], tile):
         block = table[start : start + tile, :].astype(jnp.float32)
         half_norms[start : start + tile, :] = 0.5 * jnp.sum(block * block, axis=1, keepdims=True)
-    two_tiles(table, half_norms, rows[...], scores, (None, None), (keep, give), tile)
-
-
-def step_kernel(tile, step, depth, table, half_norms, keep_in, give_in, rows, keep, give, scores):
+    _, _, mine, other = chip_place()
+    keep[...] = jnp.zeros_like(keep)
+    give[...] = jnp.zeros_like(give)
+    add_rows(table, half_norms, [own], rows, scores, ((mine, keep), (other, give)), tile)
+
+
+def came_to(step, depth):
     level, core, _, _ = chip_place()
-    here = ((core == 0) & (level >= step)) | ((core == 1) & (level < depth - step))
-
-    @pl.when(jnp.logical_not(here))
-    def _():
-        keep[...] = keep_in[...]
-        give[...] = give_in[...]
-
-    @pl.when(here)
-    def _():
-        two_tiles(table, half_norms, rows[...], scores, (keep_in, give_in), (keep, give), tile)
-
-
-def last_sums(tile, depth, table, half_norms, came, passed, rows, scores):
-    level, core, mine, _ = chip_place()
-    here = ((core == 0) & (level == depth - 1)) | ((core == 1) & (level == 0))
-
-    @pl.when(here)
-    def _():
-        rows[...] = came[...]
-
-    @pl.when(jnp.logical_not(here))
-    def _():
-        rows[...] = passed[...]
-
-    all_rows = rows[...]
-    terms = softmax_terms(table, half_norms, all_rows, scores, tile)
-    return tile_sums(scores[at_tile(mine, tile), :], *terms, all_rows)
+    return ((core == 0) & (level >= step)) | ((core == 1) & (level < depth - step))
+
+
+def step_kernel(tile, depth, step, table, half_norms, keep_in, give_in, *refs):
+    parts, (keep, give, rows, scores) = refs[:-4], refs[-4:]
+    keep[...] = keep_in[...]
+    give[...] = give_in[...]
+
+    @pl.when(came_to(step, depth))
+    def _():
+        _, _, mine, other = chip_place()
+        add_rows(table, half_norms, parts, rows, scores, ((mine, keep), (other, give)), tile)
 
 
 def end_chip(depth):
@@ -253,42 +268,38 @@
     return (level == 0) | (level == depth - 1)
 
 
-def end_kernel(tile, depth, table, half_norms, keep_in, came, passed, keep, rows, scores):
-    feature_dim = rows.shape[1]
-
-    @pl.when(jnp.logical_not(end_chip(depth)))
-    def _():
-        keep[...] = keep_in[...]
+def add_last(tile, depth, table, half_norms, parts, keep, rows, scores):
+    half = len(parts) // 2
+    mine = chip_place()[2]
+
+    @pl.when(came_to(depth - 1, depth))
+    def _():
+        gather_rows(parts[:half], rows)
+
+    @pl.when(jnp.logical_not(came_to(depth - 1, depth)))
+    def _():
+        gather_rows(parts[half:], rows)
+
+    add_rows(table, half_norms, [rows], rows, scores, ((mine, keep),), tile)
+
+
+def refit_kernel(tile, depth, table, half_norms, keep, got, *refs):
+    parts, (refined, rows, scores, sums) = refs[:-4], refs[-4:]
+    feature_dim = table.shape[1]
+    mine = chip_place()[2]
+    sums[...] = keep[...] + got[...]
 
     @pl.when(end_chip(depth))
     def _():
-        sums, count = last_sums(tile, depth, table, half_norms, came, passed, rows, scores)
-        keep[:, :feature_dim] = keep_in[:, :feature_dim] + sums
-        keep[:, feature_dim:] = keep_in[:, feature_dim:] + count
-
-
-def refit_kernel(tile, depth, table, half_norms, keep, got, came, passed, refined, rows, scores):
-    feature_dim = rows.shape[1]
-    mine = chip_place()[2]
+        add_last(tile, depth, table, half_norms, parts, sums, rows, scores)
+
     old = table[at_tile(mine, tile), :].astype(jnp.float32)
-
-    def refit(more, count):
-        sums = keep[:, :feature_dim] + got[:, :feature_dim] + more
-        count = keep[:, feature_dim:] + got[:, feature_dim:] + count
-        scale = 1.0 / (count[:, :1] + 1.0)
-        refined[...] = ((sums + old) * scale).astype(jnp.bfloat16)
-
-    @pl.when(jnp.logical_not(end_chip(depth)))
-    def _():
-        refit(0.0, 0.0)
-
-    @pl.when(end_chip(depth))
-    def _():
-        refit(*last_sums(tile, depth, table, half_norms, came, passed, rows, scores))
-
-
-def cost():
-    return pl.CostEstimate(flops=1 << 20, bytes_accessed=0, transcendentals=0)
+    scale = 1.0 / (sums[:, feature_dim : feature_dim + 1] + 1.0)
+    refined[...] = ((sums[:, :feature_dim] + old) * scale).astype(jnp.bfloat16)
+
+
+def cost(flops=1 << 20):
+    return pl.CostEstimate(flops=flops, bytes_accessed=0, transcendentals=0)
 
 
 def handoff(points, centroids, dest_group):
@@ -302,18 +313,20 @@
     def swap(x):
         return lax.ppermute(x, "member", [(i, i ^ 1) for i in range(member_count)])
 
-    def onward(x, step):
-        up = [(2 * z, 2 * z + 2) for z in range(step - 1, depth - 1)]
-        down = [(2 * z + 3, 2 * z + 1) for z in range(0, depth - step)]
+    def along(x, moves):
+        up = [(2 * z, 2 * to) for z, to in moves]
+        down = [(2 * (depth - 1 - z) + 1, 2 * (depth - 1 - to) + 1) for z, to in moves]
         return lax.ppermute(x, "member", up + down)
+
+    last = depth - 1
+    apart = [(0, last - 1), (last - 1, last)]
+    over = [(1, last)]
+    beside = [(z, z + 1) for z in range(last)]
 
     sums_shape = jax.ShapeDtypeStruct((tile, feature_dim + lanes), jnp.float32)
     norms_shape = jax.ShapeDtypeStruct((fine_count, 1), jnp.float32)
 
-    def kernel(body, out_shape, *operands, scratch_rows=0, aliases={}):
-        scratch = [pltpu.VMEM((fine_count, row_count), jnp.float32)]
-        if scratch_rows:
-            scratch = [pltpu.VMEM((scratch_rows, feature_dim), jnp.bfloat16)] + scratch
+    def kernel(body, out_shape, *operands, scratch=(), aliases={}, flops=1 << 20):
         return pl.pallas_call(
             body,
             out_shape=out_shape,
@@ -322,52 +335,74 @@
             scratch_shapes=scratch,
             input_output_aliases=aliases,
             compiler_params=pltpu.CompilerParams(vmem_limit_bytes=vmem_limit),
-            cost_estimate=cost(),
+            cost_estimate=cost(flops),
             name=body.func.__name__,
         )(*operands)
+
+    def scratch(rows):
+        return [
+            pltpu.VMEM((rows, feature_dim), jnp.bfloat16),
+            pltpu.VMEM((fine_count, rows), jnp.float32),
+        ]
 
     packed = pack(dest_group.reshape(1, row_count), points, group_count)
     fetched = [
         lax.ppermute(packed[k], "group", [(i, i ^ k) for i in range(group_count)])
         for k in reversed(range(1, group_count))
     ]
-    own = join([packed[0]] + fetched)
-    first, second = onward(own, 1), onward(swap(own), 1)
+    first = join([packed[0]] + fetched)
+    over_first = along(first, over)
+    apart_first = along(first, apart)
+    second = swap(first)
+    apart_second = along(second, apart)
+    two_sums = [sums_shape, sums_shape]
     keep, give, half_norms = kernel(
-        functools.partial(own_kernel, tile), [sums_shape, sums_shape, norms_shape], centroids, own
-    )
-    for step in range(1, depth - 1):
-        held = join([first], keep)
-        next_first = onward(held, step + 1)
-        body = functools.partial(step_kernel, tile, step, depth)
-        keep, give = kernel(
-            body, [sums_shape] * 2, centroids, half_norms, keep, give, held, aliases={2: 0, 3: 1}
+        functools.partial(own_kernel, tile),
+        [*two_sums, norms_shape],
+        centroids,
+        first,
+        scratch=scratch(row_count),
+    )
+
+    def add(step, keep, give, *parts):
+        return kernel(
+            functools.partial(step_kernel, tile, depth, step),
+            two_sums,
+            centroids,
+            half_norms,
+            keep,
+            give,
+            *parts,
+            scratch=scratch(len(parts) * row_count),
+            aliases={2: 0, 3: 1},
+            flops=1 << 28,
         )
-        held = join([second], keep)
-        next_second = onward(held, step + 1)
-        keep, give = kernel(
-            body, [sums_shape] * 2, centroids, half_norms, keep, give, held, aliases={2: 0, 3: 1}
-        )
-        first, second = next_first, next_second
-
-    got = swap(give)
-    held = join([first], keep)
-    keep = kernel(
-        functools.partial(end_kernel, tile, depth), sums_shape, centroids, half_norms, keep, held,
-        swap(held), scratch_rows=row_count, aliases={2: 0},
-    )
-    held = join([second], keep)
+
+    beside_first = along(pick(depth, first, apart_first, keep), beside)
+    beside_second = along(pick(depth, second, apart_second, keep), beside)
+    over_second = along(second, over)
+    keep, give = add(last - 1, keep, give, apart_first, apart_second)
+    keep, give = add(last, keep, give, over_first)
+    keep, give = add(1, keep, give, beside_first, beside_second)
+    got = jnp.concatenate([swap(give[: tile // 2]), swap(give[tile // 2 :])], axis=0)
+    held = join([over_second], keep)
     return kernel(
         functools.partial(refit_kernel, tile, depth),
         jax.ShapeDtypeStruct((tile, feature_dim), jnp.bfloat16),
-        centroids, half_norms, keep, got, held, swap(held), scratch_rows=row_count,
+        centroids,
+        half_norms,
+        keep,
+        got,
+        held,
+        swap(held),
+        scratch=scratch(row_count) + [pltpu.VMEM(sums_shape.shape, jnp.float32)],
     )
 
 
 def solution(mesh):
     def local(points, centroids, dest_group):
         groups, members = mesh.shape["group"], mesh.shape["member"]
-        if groups * (points.shape[0] // 4) == points.shape[0] and 6 <= members <= 16:
+        if groups * (points.shape[0] // 4) == points.shape[0] and members // 2 == 4:
             return handoff(points, centroids, dest_group)
         return general(points, centroids, dest_group)
 

time: 53.9 us -> 47.9 us (0.89)
  the two profiles are of different devices: /device:TPU:25 before, /device:TPU:0 now
where the time goes in v3:
time: 47.9 us; the launch traced here: 47.6 us
  starting transfers between devices  26.6 us (56%)
  waiting for transfers between devices  11.2 us (23%)
  Pallas kernels  5.89 us (12%)
  local copies, waits for them, and re-layouts  3.62 us (8%)
    ppermute x6, starting transfers between devices, along(): return lax.ppermute(x, 'member', up + down)  14.5 us
    ppermute x4, starting transfers between devices, swap(): return lax.ppermute(x, 'member', [(i, i ^ 1) for i in range(member_count)])  7.51 us
    ppermute x6, waiting for transfers between devices, along(): return lax.ppermute(x, 'member', up + down)  5.37 us
    pallas_call x5, Pallas kernels, kernel(): pl.pallas_call(body, out_shape=out_shape, in_specs=[vmem()] * len(operand...  4.95 us
    ppermute x3, starting transfers between devices, handoff(): lax.ppermute(packed[k], 'group', [(i, i ^ k) for i in range(group_count)])  4.6 us
    ppermute x3, waiting for transfers between devices, handoff(): lax.ppermute(packed[k], 'group', [(i, i ^ k) for i in range(group_count)])  4.59 us
    unnamed x8, local copies, waits for them, and re-layouts  3.56 us
    ppermute x4, waiting for transfers between devices, swap(): return lax.ppermute(x, 'member', [(i, i ^ 1) for i in range(member_count)])  1.29 us
  transfers between devices with their start and end apart: 13, of which 6 were waited for; matrix products, arithmetic and copies ran while one was open for 0% of the time, Pallas kernels for 6%

profile of v3, /device:TPU:0, one launch (start us, length us, event | category | flops | bytes accessed | tf_op | source)
XLA Modules:
  0.0 47.6 jit_solution(1096257314654075873)
XLA Ops:
  0.0 0.0 copy-start.2
  0.0 1.0 %copy-done.2 = bf16[256,768]{1,0:T(8,128)(2,1)S(1)} copy-done((bf16[256,768]{1,0:T(8,128)(2,1)S(1)}, bf16[256,768]{1,0:T(8,128)(2,1)}, u32[]{:S(2)}) %copy-start.2) | copy-done | bytes 393240
  1.0 0.0 copy-start.3
  1.0 0.7 %copy-done.3 = s32[256,1]{0,1:T(1,128)S(1)} copy-done((s32[256,1]{0,1:T(1,128)S(1)}, s32[256,1]{0,1:T(1,128)}, u32[]{:S(2)}) %copy-start.3) | copy-done | bytes 1048
  1.7 0.8 %pack.1 = (bf16[64,768]{1,0:T(8,128)(2,1)S(1)}, bf16[64,768]{1,0:T(8,128)(2,1)S(1)}, bf16[64,768]{1,0:T(8,128)(2,1)S(1)}, bf16[64,768]{1,0:T(8,128)(2,1)S(1)}) custom-call(s32[1,256]{1,0:T(1,128)S(1)} %bitcast.1, bf16[256,768]{1,0:T(8,128)(2,1)S(1)} %copy-done.2), custom_call_target="tpu_custom_call" | custom-call | flops 1048576 | tf_op jit(solution)/shard_map/pack/pallas_call | solution.py:163
  2.5 4.0 %collective-permute-start = (bf16[64,768]{1,0:T(8,128)(2,1)S(1)}, bf16[64,768]{1,0:T(8,128)(2,1)S(1)}, u32[]{:S(2)}, u32[]{:S(2)}) collective-permute-start(bf16[64,768]{1,0:T(8,128)(2,1)S(1)} %get-tuple-element.19), channel_id=1, source_target_pairs={{0,24},{8,16},{16,8},{24,0},{1,25},{9,17},{17,9},{25,1},{2,26},{10... | collective-permute-start | bytes 294920 | tf_op jit(solution)/shard_map/ppermute | solution.py:350
  6.4 0.5 %collective-permute-start.1 = (bf16[64,768]{1,0:T(8,128)(2,1)S(1)}, bf16[64,768]{1,0:T(8,128)(2,1)S(1)}, u32[]{:S(2)}, u32[]{:S(2)}) collective-permute-start(bf16[64,768]{1,0:T(8,128)(2,1)S(1)} %get-tuple-element.20), channel_id=1, source_target_pairs={{0,16},{8,24},{16,0},{24,8},{1,17},{9,25},{17,1},{25,9},{2,18},{10... | collective-permute-start | bytes 294920 | tf_op jit(solution)/shard_map/ppermute | solution.py:350
  6.9 0.1 collective-permute-start.2
  7.1 2.5 %collective-permute-done.refs_1_ = bf16[64,768]{1,0:T(8,128)(2,1)S(1)} collective-permute-done((bf16[64,768]{1,0:T(8,128)(2,1)S(1)}, bf16[64,768]{1,0:T(8,128)(2,1)S(1)}, u32[]{:S(2)}, u32[]{:S(2)}) %collective-permute-start) | collective-permute-done | bytes 98336 | tf_op jit(solution)/shard_map/ppermute | solution.py:350
  9.6 1.7 %collective-permute-done.1.refs_2_ = bf16[64,768]{1,0:T(8,128)(2,1)S(1)} collective-permute-done((bf16[64,768]{1,0:T(8,128)(2,1)S(1)}, bf16[64,768]{1,0:T(8,128)(2,1)S(1)}, u32[]{:S(2)}, u32[]{:S(2)}) %collective-permute-start.1) | collective-permute-done | bytes 98336 | tf_op jit(solution)/shard_map/ppermute | solution.py:350
  11.3 0.3 collective-permute-done.2.refs_3_
  11.7 0.1 collective-permute-start.4
  11.8 4.5 %collective-permute-start.3 = (bf16[256,768]{1,0:T(8,128)(2,1)S(1)}, bf16[256,768]{1,0:T(8,128)(2,1)S(1)}, u32[]{:S(2)}, u32[]{:S(2)}) collective-permute-start(bf16[256,768]{1,0:T(8,128)(2,1)S(1)} %join.2.own), channel_id=1, source_target_pairs={{0,4},{4,6},{7,3},{3,1},{8,12},{12,14},{15,11},{11,9},{16,20},{20,... | collective-permute-start | bytes 1179656 | tf_op jit(solution)/shard_map/ppermute | solution.py:319
  16.3 0.0 collective-permute-done.4.own
  16.3 3.5 %collective-permute-start.5 = (bf16[256,768]{1,0:T(8,128)(2,1)S(1)}, bf16[256,768]{1,0:T(8,128)(2,1)S(1)}, u32[]{:S(2)}, u32[]{:S(2)}) collective-permute-start(bf16[256,768]{1,0:T(8,128)(2,1)S(1)} %collective-permute-done.4.own), channel_id=1, source_target_pairs={{0,4},{4,6},{7,3},{3,1},{8,12},{12,14},{15,11},{11,9},{16,20},{20,... | collective-permute-start | bytes 1179656 | tf_op jit(solution)/shard_map/ppermute | solution.py:319
  19.8 0.7 %collective-permute-start.6 = (bf16[256,768]{1,0:T(8,128)(2,1)S(1)}, bf16[256,768]{1,0:T(8,128)(2,1)S(1)}, u32[]{:S(2)}, u32[]{:S(2)}) collective-permute-start(bf16[256,768]{1,0:T(8,128)(2,1)S(1)} %join.2.own), channel_id=1, source_target_pairs={{2,6},{5,1},{10,14},{13,9},{18,22},{21,17},{26,30},{29,25}} | collective-permute-start | bytes 1179656 | tf_op jit(solution)/shard_map/ppermute | solution.py:319
  20.5 0.0 copy-start
  20.5 1.9 %copy-done = bf16[2048,768]{1,0:T(8,128)(2,1)S(1)} copy-done((bf16[2048,768]{1,0:T(8,128)(2,1)S(1)}, bf16[2048,768]{1,0:T(8,128)(2,1)}, u32[]{:S(2)}) %copy-start) | copy-done | bytes 3145752
  22.4 0.0 copy-start.1
  22.4 1.9 %own_kernel.1 = (f32[256,896]{1,0:T(8,128)S(1)}, f32[256,896]{1,0:T(8,128)S(1)}, f32[2048,1]{1,0:T(8,128)S(1)}) custom-call(bf16[2048,768]{1,0:T(8,128)(2,1)S(1)} %copy-done, bf16[256,768]{1,0:T(8,128)(2,1)S(1)} %join.2.own), custom_call_target="tpu_custom_call" | custom-call | flops 1048576 | tf_op jit(solution)/shard_map/own_kernel/pallas_call | solution.py:330
  24.3 0.0 collective-permute-done.3.refs_0_.came
  24.3 2.3 %collective-permute-start.7 = (bf16[256,768]{1,0:T(8,128)(2,1)S(1)}, bf16[256,768]{1,0:T(8,128)(2,1)S(1)}, u32[]{:S(2)}, u32[]{:S(2)}) collective-permute-start(bf16[256,768]{1,0:T(8,128)(2,1)S(1)} %pick.2), channel_id=1, source_target_pairs={{0,2},{2,4},{4,6},{7,5},{5,3},{3,1},{8,10},{10,12},{12,14},{15,13}... | collective-permute-start | bytes 1179656 | tf_op jit(solution)/shard_map/ppermute | solution.py:319
  26.7 0.0 collective-permute-done.5.refs_1_.came
  26.7 2.8 %collective-permute-start.8 = (bf16[256,768]{1,0:T(8,128)(2,1)S(1)}, bf16[256,768]{1,0:T(8,128)(2,1)S(1)}, u32[]{:S(2)}, u32[]{:S(2)}) collective-permute-start(bf16[256,768]{1,0:T(8,128)(2,1)S(1)} %pick.3), channel_id=1, source_target_pairs={{0,2},{2,4},{4,6},{7,5},{5,3},{3,1},{8,10},{10,12},{12,14},{15,13}... | collective-permute-start | bytes 1179656 | tf_op jit(solution)/shard_map/ppermute | solution.py:319
  29.5 0.7 %collective-permute-start.11 = (bf16[256,768]{1,0:T(8,128)(2,1)S(1)}, bf16[256,768]{1,0:T(8,128)(2,1)S(1)}, u32[]{:S(2)}, u32[]{:S(2)}) collective-permute-start(bf16[256,768]{1,0:T(8,128)(2,1)S(1)} %collective-permute-done.4.own), channel_id=1, source_target_pairs={{2,6},{5,1},{10,14},{13,9},{18,22},{21,17},{26,30},{29,25}} | collective-permute-start | bytes 1179656 | tf_op jit(solution)/shard_map/ppermute | solution.py:319
  30.2 0.0 copy-done.1
  30.3 0.2 step_kernel.3
  30.5 0.0 collective-permute-done.6.refs_0_
  30.5 0.2 step_kernel.4
  30.8 1.1 %collective-permute-done.7.refs_0_ = bf16[256,768]{1,0:T(8,128)(2,1)S(1)} collective-permute-done((bf16[256,768]{1,0:T(8,128)(2,1)S(1)}, bf16[256,768]{1,0:T(8,128)(2,1)S(1)}, u32[]{:S(2)}, u32[]{:S(2)}) %collective-permute-start.7) | collective-permute-done | bytes 393248 | tf_op jit(solution)/shard_map/ppermute | solution.py:319
  31.9 4.2 %collective-permute-done.8.refs_1_ = bf16[256,768]{1,0:T(8,128)(2,1)S(1)} collective-permute-done((bf16[256,768]{1,0:T(8,128)(2,1)S(1)}, bf16[256,768]{1,0:T(8,128)(2,1)S(1)}, u32[]{:S(2)}, u32[]{:S(2)}) %collective-permute-start.8) | collective-permute-done | bytes 393248 | tf_op jit(solution)/shard_map/ppermute | solution.py:319
  36.1 0.2 step_kernel.5
  36.4 0.1 fusion
  36.4 5.0 %collective-permute-start.9 = (f32[128,896]{1,0:T(8,128)S(1)}, f32[128,896]{1,0:T(8,128)S(1)}, u32[]{:S(2)}, u32[]{:S(2)}) collective-permute-start(f32[128,896]{1,0:T(8,128)S(1)} %get-tuple-element.31), channel_id=1, source_target_pairs={{0,1},{1,0},{2,3},{3,2},{4,5},{5,4},{6,7},{7,6},{8,9},{9,8},{10,11... | collective-permute-start | bytes 1376264 | tf_op jit(solution)/shard_map/ppermute | solution.py:314
  41.4 0.1 collective-permute-start.10
  41.5 0.0 collective-permute-done.11.refs_1_
  41.5 2.4 %collective-permute-start.12 = (bf16[256,768]{1,0:T(8,128)(2,1)S(1)}, bf16[256,768]{1,0:T(8,128)(2,1)S(1)}, u32[]{:S(2)}, u32[]{:S(2)}) collective-permute-start(bf16[256,768]{1,0:T(8,128)(2,1)S(1)} %join.3.refs_0_), channel_id=1, source_target_pairs={{0,1},{1,0},{2,3},{3,2},{4,5},{5,4},{6,7},{7,6},{8,9},{9,8},{10,11... | collective-permute-start | bytes 1179656 | tf_op jit(solution)/shard_map/ppermute | solution.py:314
  43.9 0.0 collective-permute-done.9
  43.9 0.0 collective-permute-done.10
  43.9 0.1 pad_maximum_fusion.got
  44.0 1.3 %collective-permute-done.12.refs_1_ = bf16[256,768]{1,0:T(8,128)(2,1)S(1)} collective-permute-done((bf16[256,768]{1,0:T(8,128)(2,1)S(1)}, bf16[256,768]{1,0:T(8,128)(2,1)S(1)}, u32[]{:S(2)}, u32[]{:S(2)}) %collective-permute-start.12) | collective-permute-done | bytes 393248 | tf_op jit(solution)/shard_map/ppermute | solution.py:314
  45.2 2.4 %refit_kernel.1 = bf16[256,768]{1,0:T(8,128)(2,1)} custom-call(bf16[2048,768]{1,0:T(8,128)(2,1)S(1)} %copy-done.1, f32[2048,1]{1,0:T(8,128)S(1)} %get-tuple-element.22.half_norms, f32[256,896]{1,0:T(8,128)S(1)} %get-tuple-element.29.refs_0_.keep, f32[256,896]{1,0:T(8,128)S(1)} %pad_maximum_fusion.got, bf16[256,768]{1,0:T(8,128)(2,1)S(1)} %join.3.refs_0_, ...), custom_call_target="tpu_custom_call" | custom-call | flops 1048576 | tf_op jit(solution)/shard_map/refit_kernel/pallas_call | solution.py:330
  (4 shorter events, 0.1 us)
Async XLA Ops:
  0.0 1.0 %copy-start.2 = (bf16[256,768]{1,0:T(8,128)(2,1)S(1)}, bf16[256,768]{1,0:T(8,128)(2,1)}, u32[]{:S(2)}) copy-start(bf16[256,768]{1,0:T(8,128)(2,1)} %points.1) | copy-start | bytes 1179652
  1.0 0.7 %copy-start.3 = (s32[256,1]{0,1:T(1,128)S(1)}, s32[256,1]{0,1:T(1,128)}, u32[]{:S(2)}) copy-start(s32[256,1]{0,1:T(1,128)} %param.5) | copy-start | bytes 3076
  2.5 7.1 %collective-permute-start = (bf16[64,768]{1,0:T(8,128)(2,1)S(1)}, bf16[64,768]{1,0:T(8,128)(2,1)S(1)}, u32[]{:S(2)}, u32[]{:S(2)}) collective-permute-start(bf16[64,768]{1,0:T(8,128)(2,1)S(1)} %get-tuple-element.19), channel_id=1, source_target_pairs={{0,24},{8,16},{16,8},{24,0},{1,25},{9,17},{17,9},{25,1},{2,26},{10... | collective-permute-start | bytes 294920 | tf_op jit(solution)/shard_map/ppermute | solution.py:350
  6.4 4.9 %collective-permute-start.1 = (bf16[64,768]{1,0:T(8,128)(2,1)S(1)}, bf16[64,768]{1,0:T(8,128)(2,1)S(1)}, u32[]{:S(2)}, u32[]{:S(2)}) collective-permute-start(bf16[64,768]{1,0:T(8,128)(2,1)S(1)} %get-tuple-element.20), channel_id=1, source_target_pairs={{0,16},{8,24},{16,0},{24,8},{1,17},{9,25},{17,1},{25,9},{2,18},{10... | collective-permute-start | bytes 294920 | tf_op jit(solution)/shard_map/ppermute | solution.py:350
  6.9 4.7 %collective-permute-start.2 = (bf16[64,768]{1,0:T(8,128)(2,1)S(1)}, bf16[64,768]{1,0:T(8,128)(2,1)S(1)}, u32[]{:S(2)}, u32[]{:S(2)}) collective-permute-start(bf16[64,768]{1,0:T(8,128)(2,1)S(1)} %get-tuple-element.21), channel_id=1, source_target_pairs={{0,8},{8,0},{16,24},{24,16},{1,9},{9,1},{17,25},{25,17},{2,10},{10... | collective-permute-start | bytes 294920 | tf_op jit(solution)/shard_map/ppermute | solution.py:350
  11.7 4.6 %collective-permute-start.4 = (bf16[256,768]{1,0:T(8,128)(2,1)S(1)}, bf16[256,768]{1,0:T(8,128)(2,1)S(1)}, u32[]{:S(2)}, u32[]{:S(2)}) collective-permute-start(bf16[256,768]{1,0:T(8,128)(2,1)S(1)} %join.2.own), channel_id=1, source_target_pairs={{0,1},{1,0},{2,3},{3,2},{4,5},{5,4},{6,7},{7,6},{8,9},{9,8},{10,11... | collective-permute-start | bytes 1179656 | tf_op jit(solution)/shard_map/ppermute | solution.py:314
  11.8 12.5 %collective-permute-start.3 = (bf16[256,768]{1,0:T(8,128)(2,1)S(1)}, bf16[256,768]{1,0:T(8,128)(2,1)S(1)}, u32[]{:S(2)}, u32[]{:S(2)}) collective-permute-start(bf16[256,768]{1,0:T(8,128)(2,1)S(1)} %join.2.own), channel_id=1, source_target_pairs={{0,4},{4,6},{7,3},{3,1},{8,12},{12,14},{15,11},{11,9},{16,20},{20,... | collective-permute-start | bytes 1179656 | tf_op jit(solution)/shard_map/ppermute | solution.py:319
  16.3 10.3 %collective-permute-start.5 = (bf16[256,768]{1,0:T(8,128)(2,1)S(1)}, bf16[256,768]{1,0:T(8,128)(2,1)S(1)}, u32[]{:S(2)}, u32[]{:S(2)}) collective-permute-start(bf16[256,768]{1,0:T(8,128)(2,1)S(1)} %collective-permute-done.4.own), channel_id=1, source_target_pairs={{0,4},{4,6},{7,3},{3,1},{8,12},{12,14},{15,11},{11,9},{16,20},{20,... | collective-permute-start | bytes 1179656 | tf_op jit(solution)/shard_map/ppermute | solution.py:319
  19.8 10.7 %collective-permute-start.6 = (bf16[256,768]{1,0:T(8,128)(2,1)S(1)}, bf16[256,768]{1,0:T(8,128)(2,1)S(1)}, u32[]{:S(2)}, u32[]{:S(2)}) collective-permute-start(bf16[256,768]{1,0:T(8,128)(2,1)S(1)} %join.2.own), channel_id=1, source_target_pairs={{2,6},{5,1},{10,14},{13,9},{18,22},{21,17},{26,30},{29,25}} | collective-permute-start | bytes 1179656 | tf_op jit(solution)/shard_map/ppermute | solution.py:319
  20.5 1.9 %copy-start = (bf16[2048,768]{1,0:T(8,128)(2,1)S(1)}, bf16[2048,768]{1,0:T(8,128)(2,1)}, u32[]{:S(2)}) copy-start(bf16[2048,768]{1,0:T(8,128)(2,1)} %table.9) | copy-start | bytes 9437188
  22.4 7.9 %copy-start.1 = (bf16[2048,768]{1,0:T(8,128)(2,1)S(1)}, bf16[2048,768]{1,0:T(8,128)(2,1)}, u32[]{:S(2)}) copy-start(bf16[2048,768]{1,0:T(8,128)(2,1)} %table.9) | copy-start | bytes 9437188
  24.3 7.6 %collective-permute-start.7 = (bf16[256,768]{1,0:T(8,128)(2,1)S(1)}, bf16[256,768]{1,0:T(8,128)(2,1)S(1)}, u32[]{:S(2)}, u32[]{:S(2)}) collective-permute-start(bf16[256,768]{1,0:T(8,128)(2,1)S(1)} %pick.2), channel_id=1, source_target_pairs={{0,2},{2,4},{4,6},{7,5},{5,3},{3,1},{8,10},{10,12},{12,14},{15,13}... | collective-permute-start | bytes 1179656 | tf_op jit(solution)/shard_map/ppermute | solution.py:319
  26.7 9.4 %collective-permute-start.8 = (bf16[256,768]{1,0:T(8,128)(2,1)S(1)}, bf16[256,768]{1,0:T(8,128)(2,1)S(1)}, u32[]{:S(2)}, u32[]{:S(2)}) collective-permute-start(bf16[256,768]{1,0:T(8,128)(2,1)S(1)} %pick.3), channel_id=1, source_target_pairs={{0,2},{2,4},{4,6},{7,5},{5,3},{3,1},{8,10},{10,12},{12,14},{15,13}... | collective-permute-start | bytes 1179656 | tf_op jit(solution)/shard_map/ppermute | solution.py:319
  29.5 11.9 %collective-permute-start.11 = (bf16[256,768]{1,0:T(8,128)(2,1)S(1)}, bf16[256,768]{1,0:T(8,128)(2,1)S(1)}, u32[]{:S(2)}, u32[]{:S(2)}) collective-permute-start(bf16[256,768]{1,0:T(8,128)(2,1)S(1)} %collective-permute-done.4.own), channel_id=1, source_target_pairs={{2,6},{5,1},{10,14},{13,9},{18,22},{21,17},{26,30},{29,25}} | collective-permute-start | bytes 1179656 | tf_op jit(solution)/shard_map/ppermute | solution.py:319
  36.4 7.5 %collective-permute-start.9 = (f32[128,896]{1,0:T(8,128)S(1)}, f32[128,896]{1,0:T(8,128)S(1)}, u32[]{:S(2)}, u32[]{:S(2)}) collective-permute-start(f32[128,896]{1,0:T(8,128)S(1)} %get-tuple-element.31), channel_id=1, source_target_pairs={{0,1},{1,0},{2,3},{3,2},{4,5},{5,4},{6,7},{7,6},{8,9},{9,8},{10,11... | collective-permute-start | bytes 1376264 | tf_op jit(solution)/shard_map/ppermute | solution.py:314
  41.4 2.5 %collective-permute-start.10 = (f32[128,896]{1,0:T(8,128)S(1)}, f32[128,896]{1,0:T(8,128)S(1)}, u32[]{:S(2)}, u32[]{:S(2)}) collective-permute-start(f32[128,896]{1,0:T(8,128)S(1)} %get-tuple-element.32), channel_id=1, source_target_pairs={{0,1},{1,0},{2,3},{3,2},{4,5},{5,4},{6,7},{7,6},{8,9},{9,8},{10,11... | collective-permute-start | bytes 1376264 | tf_op jit(solution)/shard_map/ppermute | solution.py:314
  41.5 3.7 %collective-permute-start.12 = (bf16[256,768]{1,0:T(8,128)(2,1)S(1)}, bf16[256,768]{1,0:T(8,128)(2,1)S(1)}, u32[]{:S(2)}, u32[]{:S(2)}) collective-permute-start(bf16[256,768]{1,0:T(8,128)(2,1)S(1)} %join.3.refs_0_), channel_id=1, source_target_pairs={{0,1},{1,0},{2,3},{3,2},{4,5},{5,4},{6,7},{7,6},{8,9},{9,8},{10,11... | collective-permute-start | bytes 1179656 | tf_op jit(solution)/shard_map/ppermute | solution.py:314

commit v4 on v3

--- a/solution.py
+++ b/solution.py
@@ -11,6 +11,10 @@
 score_scale = 0.15
 lanes = 128
 exponent_scale = score_scale * math.log2(math.e)
+own_flops = 1 << 31
+beside_flops = 1 << 28
+over_flops = 1 << 32
+last_flops = 1 << 26
 vmem_limit = 20 * 1024 * 1024
 
 
@@ -91,7 +95,7 @@
     gather_rows(refs[after_n:-1], refs[-1])
 
 
-def join(parts, *after):
+def join(parts, *after, flops=1 << 20):
     rows = sum(part.shape[0] for part in parts)
     return pl.pallas_call(
         functools.partial(join_kernel, len(after)),
@@ -99,7 +103,7 @@
         in_specs=[unread()] * len(after) + [vmem()] * len(parts),
         out_specs=vmem(),
         compiler_params=pltpu.CompilerParams(vmem_limit_bytes=vmem_limit),
-        cost_estimate=cost(),
+        cost_estimate=cost(flops),
         name="join",
     )(*after, *parts)
 
@@ -174,7 +178,10 @@
         compiler_params=pltpu.CompilerParams(vmem_limit_bytes=vmem_limit),
         cost_estimate=cost(),
         name="pack",
-    )(dest_row, points)
+    )(
+        pltpu.with_memory_space_constraint(dest_row, pltpu.HBM),
+        pltpu.with_memory_space_constraint(points, pltpu.HBM),
+    )
 
 
 def scaled_scores(table, half_norms, rows):
@@ -237,19 +244,56 @@
         out[:, feature_dim:] += count
 
 
-def own_kernel(tile, table, own, keep, give, half_norms, rows, scores):
-    for start in range(0, table.shape[0], tile):
-        block = table[start : start + tile, :].astype(jnp.float32)
-        half_norms[start : start + tile, :] = 0.5 * jnp.sum(block * block, axis=1, keepdims=True)
-    _, _, mine, other = chip_place()
-    keep[...] = jnp.zeros_like(keep)
-    give[...] = jnp.zeros_like(give)
-    add_rows(table, half_norms, [own], rows, scores, ((mine, keep), (other, give)), tile)
-
-
 def came_to(step, depth):
     level, core, _, _ = chip_place()
     return ((core == 0) & (level >= step)) | ((core == 1) & (level < depth - step))
+
+
+def first_kernel(tile, depth, table_from, near, far, apart, over, *refs):
+    table, keep, give, half_norms, arrivals, rows, scores = refs
+    copies = []
+    for index in range(arrivals.shape[0]):
+        at = pl.ds(index * tile, tile)
+        copies.append(pltpu.make_async_copy(table_from.at[at], table.at[at], arrivals.at[index]))
+    for copy in copies:
+        copy.start()
+    keep[...] = jnp.zeros_like(keep)
+    give[...] = jnp.zeros_like(give)
+    for index, copy in enumerate(copies):
+        copy.wait()
+        at = slice(index * tile, (index + 1) * tile)
+        block = table[at, :].astype(jnp.float32)
+        half_norms[at, :] = 0.5 * jnp.sum(block * block, axis=1, keepdims=True)
+
+    @pl.when(came_to(depth - 1, depth))
+    def _():
+        _, _, mine, other = chip_place()
+        parts = (near, far, apart, over)
+        add_rows(table, half_norms, parts, rows, scores, ((mine, keep), (other, give)), tile)
+
+
+def own_kernel(tile, depth, table, half_norms, keep_in, give_in, near, far, apart_near, *refs):
+    came, (keep, give, rows, scores) = refs[:-4], refs[-4:]
+    keep[...] = keep_in[...]
+    give[...] = give_in[...]
+    _, _, mine, other = chip_place()
+
+    def add(*parts):
+        add_rows(table, half_norms, parts, rows, scores, ((mine, keep), (other, give)), tile)
+
+    end, here = came_to(depth - 1, depth), came_to(depth - 2, depth)
+
+    @pl.when(end)
+    def _():
+        add(*came)
+
+    @pl.when(here & jnp.logical_not(end))
+    def _():
+        add(near, far, apart_near, *came)
+
+    @pl.when(jnp.logical_not(here))
+    def _():
+        add(near, far)
 
 
 def step_kernel(tile, depth, step, table, half_norms, keep_in, give_in, *refs):
@@ -268,31 +312,29 @@
     return (level == 0) | (level == depth - 1)
 
 
-def add_last(tile, depth, table, half_norms, parts, keep, rows, scores):
-    half = len(parts) // 2
-    mine = chip_place()[2]
-
-    @pl.when(came_to(depth - 1, depth))
-    def _():
-        gather_rows(parts[:half], rows)
-
-    @pl.when(jnp.logical_not(came_to(depth - 1, depth)))
-    def _():
-        gather_rows(parts[half:], rows)
-
-    add_rows(table, half_norms, [rows], rows, scores, ((mine, keep),), tile)
-
-
-def refit_kernel(tile, depth, table, half_norms, keep, got, *refs):
-    parts, (refined, rows, scores, sums) = refs[:-4], refs[-4:]
+def refit_kernel(tile, depth, table, half_norms, keep, got, came, passed, *refs):
+    over_came, over_passed, refined, rows, scores, sums = refs
     feature_dim = table.shape[1]
     mine = chip_place()[2]
+    end, here = end_chip(depth), came_to(1, depth)
     sums[...] = keep[...] + got[...]
 
-    @pl.when(end_chip(depth))
-    def _():
-        add_last(tile, depth, table, half_norms, parts, sums, rows, scores)
-
+    def add(*parts):
+        add_rows(table, half_norms, parts, rows, scores, ((mine, sums),), tile)
+
+    @pl.when(end & here)
+    def _():
+        gather_rows((came, over_came), rows)
+
+    @pl.when(end & jnp.logical_not(here))
+    def _():
+        gather_rows((passed, over_passed), rows)
+
+    @pl.when(jnp.logical_not(end))
+    def _():
+        gather_rows((came, passed), rows)
+
+    add(rows)
     old = table[at_tile(mine, tile), :].astype(jnp.float32)
     scale = 1.0 / (sums[:, feature_dim : feature_dim + 1] + 1.0)
     refined[...] = ((sums[:, :feature_dim] + old) * scale).astype(jnp.bfloat16)
@@ -326,11 +368,11 @@
     sums_shape = jax.ShapeDtypeStruct((tile, feature_dim + lanes), jnp.float32)
     norms_shape = jax.ShapeDtypeStruct((fine_count, 1), jnp.float32)
 
-    def kernel(body, out_shape, *operands, scratch=(), aliases={}, flops=1 << 20):
+    def kernel(body, out_shape, *operands, scratch=(), aliases={}, flops=1 << 28, specs=()):
         return pl.pallas_call(
             body,
             out_shape=out_shape,
-            in_specs=[vmem()] * len(operands),
+            in_specs=list(specs) + [vmem()] * (len(operands) - len(specs)),
             out_specs=jax.tree.map(lambda _: vmem(), out_shape),
             scratch_shapes=scratch,
             input_output_aliases=aliases,
@@ -350,52 +392,68 @@
         lax.ppermute(packed[k], "group", [(i, i ^ k) for i in range(group_count)])
         for k in reversed(range(1, group_count))
     ]
-    first = join([packed[0]] + fetched)
-    over_first = along(first, over)
+    near = join([packed[0], swap(packed[0])])
+    apart_near, over_near = along(near, apart), along(near, over)
+    first = join(fetched)
     apart_first = along(first, apart)
-    second = swap(first)
+    swapped = [swap(rows) for rows in fetched]
+    second = join(swapped)
     apart_second = along(second, apart)
+    over_first = along(join(fetched + swapped[:1]), over)
     two_sums = [sums_shape, sums_shape]
-    keep, give, half_norms = kernel(
-        functools.partial(own_kernel, tile),
-        [*two_sums, norms_shape],
-        centroids,
+    table, keep, give, half_norms = kernel(
+        functools.partial(first_kernel, tile, depth),
+        [like(centroids), *two_sums, norms_shape],
+        pltpu.with_memory_space_constraint(centroids, pltpu.HBM),
+        packed[0],
         first,
-        scratch=scratch(row_count),
-    )
-
-    def add(step, keep, give, *parts):
+        apart_near,
+        over_near,
+        scratch=[pltpu.SemaphoreType.DMA((member_count,)), *scratch(row_count + 2 * near.shape[0])],
+        flops=own_flops,
+        specs=[hbm()],
+    )
+
+    def add(body, keep, give, *parts, flops=1 << 28):
         return kernel(
-            functools.partial(step_kernel, tile, depth, step),
+            body,
             two_sums,
-            centroids,
+            table,
             half_norms,
             keep,
             give,
             *parts,
-            scratch=scratch(len(parts) * row_count),
+            scratch=scratch(sum(part.shape[0] for part in parts)),
             aliases={2: 0, 3: 1},
-            flops=1 << 28,
+            flops=flops,
         )
 
     beside_first = along(pick(depth, first, apart_first, keep), beside)
     beside_second = along(pick(depth, second, apart_second, keep), beside)
-    over_second = along(second, over)
-    keep, give = add(last - 1, keep, give, apart_first, apart_second)
-    keep, give = add(last, keep, give, over_first)
-    keep, give = add(1, keep, give, beside_first, beside_second)
+    beside_near = along(pick(depth, near, apart_near, keep), beside)
+    over_second = along(join(swapped[1:]), over)
+    own_body = functools.partial(own_kernel, tile, depth)
+    keep, give = add(own_body, keep, give, packed[0], first, apart_near, apart_first, apart_second)
+    over_body = functools.partial(step_kernel, tile, depth, last)
+    keep, give = add(over_body, keep, give, over_first)
+    beside_body = functools.partial(step_kernel, tile, depth, 1)
+    keep, give = add(beside_body, keep, give, beside_first, flops=beside_flops)
+    keep, give = add(beside_body, keep, give, beside_second)
     got = jnp.concatenate([swap(give[: tile // 2]), swap(give[tile // 2 :])], axis=0)
-    held = join([over_second], keep)
+    over_last = join([over_second], keep, flops=over_flops)
+    beside_last = join([beside_near], keep, flops=last_flops)
     return kernel(
         functools.partial(refit_kernel, tile, depth),
         jax.ShapeDtypeStruct((tile, feature_dim), jnp.bfloat16),
-        centroids,
+        table,
         half_norms,
         keep,
         got,
-        held,
-        swap(held),
-        scratch=scratch(row_count) + [pltpu.VMEM(sums_shape.shape, jnp.float32)],
+        beside_last,
+        swap(beside_last),
+        over_last,
+        swap(over_last),
+        scratch=scratch(2 * near.shape[0]) + [pltpu.VMEM(sums_shape.shape, jnp.float32)],
     )
 
 

time: 47.9 us -> 44.3 us (0.925)
  waiting for transfers between devices: 11.2 us -> 1.71 us
  starting transfers between devices: 26.6 us -> 33 us
  local copies, waits for them, and re-layouts: 3.62 us -> 0.06 us
  Pallas kernels: 5.89 us -> 8.89 us
    ppermute x6 -> x9, starting transfers between devices: 14.5 us -> 23.1 us  [along(): return lax.ppermute(x, 'member', up + down)]
    ppermute x6 -> x9, waiting for transfers between devices: 5.37 us -> 0.02 us  [along(): return lax.ppermute(x, 'member', up + down)]
    ppermute x3, waiting for transfers between devices: 4.59 us -> 0.01 us  [handoff(): lax.ppermute(packed[k], 'group', [(i, i ^ k) for i in range(group_count)])]
    unnamed x8 -> x0, local copies, waits for them, and re-layouts: 3.56 us -> none
    pallas_call x5 -> x6, Pallas kernels: 4.95 us -> 7.22 us  [kernel(): pl.pallas_call(body, out_shape=out_shape, in_specs=list(specs) + [vmem()]...]
    ppermute x4 -> x8, starting transfers between devices: 7.51 us -> 5.72 us  [swap(): return lax.ppermute(x, 'member', [(i, i ^ 1) for i in range(member_count)])]
    pallas_call x1, Pallas kernels: 0.79 us -> 1.43 us  [pack(): pl.pallas_call(pack_kernel, out_shape=[jax.ShapeDtypeStruct((capacity, fe...]
    ppermute x4 -> x8, waiting for transfers between devices: 1.29 us -> 1.68 us  [swap(): return lax.ppermute(x, 'member', [(i, i ^ 1) for i in range(member_count)])]
  transfers between devices with their start and end apart: 13 -> 20, of which waited for: 6 -> 3; matrix products, arithmetic and copies ran while one was open for 0% -> 0% of each run, Pallas kernels for 6% -> 12%
where the time goes in v4:
time: 44.3 us; the launch traced here: 44 us
  starting transfers between devices  33 us (74%)
  Pallas kernels  8.89 us (20%)
  waiting for transfers between devices  1.71 us (4%)
    ppermute x9, starting transfers between devices, along(): return lax.ppermute(x, 'member', up + down)  23.1 us
    pallas_call x6, Pallas kernels, kernel(): pl.pallas_call(body, out_shape=out_shape, in_specs=list(specs) + [vmem()]...  7.22 us
    ppermute x8, starting transfers between devices, swap(): return lax.ppermute(x, 'member', [(i, i ^ 1) for i in range(member_count)])  5.72 us
    ppermute x3, starting transfers between devices, handoff(): lax.ppermute(packed[k], 'group', [(i, i ^ k) for i in range(group_count)])  4.16 us
    ppermute x8, waiting for transfers between devices, swap(): return lax.ppermute(x, 'member', [(i, i ^ 1) for i in range(member_count)])  1.68 us
    pallas_call x1, Pallas kernels, pack(): pl.pallas_call(pack_kernel, out_shape=[jax.ShapeDtypeStruct((capacity, fe...  1.43 us
  transfers between devices with their start and end apart: 20, of which 3 were waited for; matrix products, arithmetic and copies ran while one was open for 0% of the time, Pallas kernels for 12%

profile of v4, /device:TPU:0, one launch (start us, length us, event | category | flops | bytes accessed | tf_op | source)
XLA Modules:
  0.0 44.0 jit_solution(4658516709239008489)
XLA Ops:
  0.0 1.4 %pack.1 = (bf16[64,768]{1,0:T(8,128)(2,1)S(1)}, bf16[64,768]{1,0:T(8,128)(2,1)S(1)}, bf16[64,768]{1,0:T(8,128)(2,1)S(1)}, bf16[64,768]{1,0:T(8,128)(2,1)S(1)}) custom-call(s32[1,256]{1,0:T(1,128)} %bitcast.1, bf16[256,768]{1,0:T(8,128)(2,1)} %points.1), custom_call_target="tpu_custom_call" | custom-call | flops 1048576 | tf_op jit(solution)/shard_map/pack/pallas_call | solution.py:167
  1.4 0.5 %collective-permute-start.3 = (bf16[64,768]{1,0:T(8,128)(2,1)S(1)}, bf16[64,768]{1,0:T(8,128)(2,1)S(1)}, u32[]{:S(2)}, u32[]{:S(2)}) collective-permute-start(bf16[64,768]{1,0:T(8,128)(2,1)S(1)} %get-tuple-element.21.refs_0_.near), channel_id=1, source_target_pairs={{0,1},{1,0},{2,3},{3,2},{4,5},{5,4},{6,7},{7,6},{8,9},{9,8},{10,11... | collective-permute-start | bytes 294920 | tf_op jit(solution)/shard_map/ppermute | solution.py:356
  2.0 3.5 %collective-permute-start = (bf16[64,768]{1,0:T(8,128)(2,1)S(1)}, bf16[64,768]{1,0:T(8,128)(2,1)S(1)}, u32[]{:S(2)}, u32[]{:S(2)}) collective-permute-start(bf16[64,768]{1,0:T(8,128)(2,1)S(1)} %get-tuple-element.22), channel_id=1, source_target_pairs={{0,24},{8,16},{16,8},{24,0},{1,25},{9,17},{17,9},{25,1},{2,26},{10... | collective-permute-start | bytes 294920 | tf_op jit(solution)/shard_map/ppermute | solution.py:392
  5.5 0.5 %collective-permute-start.1 = (bf16[64,768]{1,0:T(8,128)(2,1)S(1)}, bf16[64,768]{1,0:T(8,128)(2,1)S(1)}, u32[]{:S(2)}, u32[]{:S(2)}) collective-permute-start(bf16[64,768]{1,0:T(8,128)(2,1)S(1)} %get-tuple-element.23), channel_id=1, source_target_pairs={{0,16},{8,24},{16,0},{24,8},{1,17},{9,25},{17,1},{25,9},{2,18},{10... | collective-permute-start | bytes 294920 | tf_op jit(solution)/shard_map/ppermute | solution.py:392
  6.0 0.1 collective-permute-start.2
  6.1 0.0 collective-permute-done.3.refs_1_
  6.1 0.7 %collective-permute-start.5 = (bf16[128,768]{1,0:T(8,128)(2,1)S(1)}, bf16[128,768]{1,0:T(8,128)(2,1)S(1)}, u32[]{:S(2)}, u32[]{:S(2)}) collective-permute-start(bf16[128,768]{1,0:T(8,128)(2,1)S(1)} %join.8.own), channel_id=1, source_target_pairs={{2,6},{5,1},{10,14},{13,9},{18,22},{21,17},{26,30},{29,25}} | collective-permute-start | bytes 589832 | tf_op jit(solution)/shard_map/ppermute | solution.py:361
  6.8 4.9 %collective-permute-start.4 = (bf16[128,768]{1,0:T(8,128)(2,1)S(1)}, bf16[128,768]{1,0:T(8,128)(2,1)S(1)}, u32[]{:S(2)}, u32[]{:S(2)}) collective-permute-start(bf16[128,768]{1,0:T(8,128)(2,1)S(1)} %join.8.own), channel_id=1, source_target_pairs={{0,4},{4,6},{7,3},{3,1},{8,12},{12,14},{15,11},{11,9},{16,20},{20,... | collective-permute-start | bytes 589832 | tf_op jit(solution)/shard_map/ppermute | solution.py:361
  11.7 0.0 collective-permute-done.refs_0_
  11.7 0.1 collective-permute-start.7
  11.8 0.0 collective-permute-done.1.refs_1_
  11.8 0.5 %collective-permute-start.8 = (bf16[64,768]{1,0:T(8,128)(2,1)S(1)}, bf16[64,768]{1,0:T(8,128)(2,1)S(1)}, u32[]{:S(2)}, u32[]{:S(2)}) collective-permute-start(bf16[64,768]{1,0:T(8,128)(2,1)S(1)} %collective-permute-done.1.refs_1_), channel_id=1, source_target_pairs={{0,1},{1,0},{2,3},{3,2},{4,5},{5,4},{6,7},{7,6},{8,9},{9,8},{10,11... | collective-permute-start | bytes 294920 | tf_op jit(solution)/shard_map/ppermute | solution.py:356
  12.3 0.0 collective-permute-done.2.refs_2_
  12.3 0.1 collective-permute-start.9
  12.4 0.7 %collective-permute-done.7.refs_0_.refs_3_ = bf16[64,768]{1,0:T(8,128)(2,1)S(1)} collective-permute-done((bf16[64,768]{1,0:T(8,128)(2,1)S(1)}, bf16[64,768]{1,0:T(8,128)(2,1)S(1)}, u32[]{:S(2)}, u32[]{:S(2)}) %collective-permute-start.7) | collective-permute-done | bytes 98336 | tf_op jit(solution)/shard_map/ppermute | solution.py:356
  13.1 4.1 %collective-permute-start.6 = (bf16[192,768]{1,0:T(8,128)(2,1)S(1)}, bf16[192,768]{1,0:T(8,128)(2,1)S(1)}, u32[]{:S(2)}, u32[]{:S(2)}) collective-permute-start(bf16[192,768]{1,0:T(8,128)(2,1)S(1)} %join.7.far.own), channel_id=1, source_target_pairs={{0,4},{4,6},{7,3},{3,1},{8,12},{12,14},{15,11},{11,9},{16,20},{20,... | collective-permute-start | bytes 884744 | tf_op jit(solution)/shard_map/ppermute | solution.py:361
  17.2 0.0 collective-permute-done.8.refs_1_.refs_0_
  17.2 0.0 collective-permute-done.9.refs_2_.refs_1_
  17.3 2.5 %collective-permute-start.10 = (bf16[192,768]{1,0:T(8,128)(2,1)S(1)}, bf16[192,768]{1,0:T(8,128)(2,1)S(1)}, u32[]{:S(2)}, u32[]{:S(2)}) collective-permute-start(bf16[192,768]{1,0:T(8,128)(2,1)S(1)} %join.9.own), channel_id=1, source_target_pairs={{0,4},{4,6},{7,3},{3,1},{8,12},{12,14},{15,11},{11,9},{16,20},{20,... | collective-permute-start | bytes 884744 | tf_op jit(solution)/shard_map/ppermute | solution.py:361
  19.8 0.7 %collective-permute-start.11 = (bf16[256,768]{1,0:T(8,128)(2,1)S(1)}, bf16[256,768]{1,0:T(8,128)(2,1)S(1)}, u32[]{:S(2)}, u32[]{:S(2)}) collective-permute-start(bf16[256,768]{1,0:T(8,128)(2,1)S(1)} %join.10), channel_id=1, source_target_pairs={{2,6},{5,1},{10,14},{13,9},{18,22},{21,17},{26,30},{29,25}} | collective-permute-start | bytes 1179656 | tf_op jit(solution)/shard_map/ppermute | solution.py:361
  20.5 0.0 collective-permute-done.5.over
  20.5 0.0 collective-permute-done.4.apart.apart_near.came
  20.5 2.3 %first_kernel.1 = (bf16[2048,768]{1,0:T(8,128)(2,1)S(1)}, f32[256,896]{1,0:T(8,128)S(1)}, f32[256,896]{1,0:T(8,128)S(1)}, f32[2048,1]{1,0:T(8,128)S(1)}) custom-call(bf16[2048,768]{1,0:T(8,128)(2,1)} %table_from.1, bf16[64,768]{1,0:T(8,128)(2,1)S(1)} %get-tuple-element.21.refs_0_.near, bf16[192,768]{1,0:T(8,128)(2,1)S(1)} %join.7.far.own, ...), custom_call_target="tpu_custom_call" | custom-call | flops 2147483648 | tf_op jit(solution)/shard_map/first_kernel/pallas_call | solution.py:372
  22.8 0.0 collective-permute-done.6.refs_0_.came
  22.9 1.9 %collective-permute-start.12 = (bf16[192,768]{1,0:T(8,128)(2,1)S(1)}, bf16[192,768]{1,0:T(8,128)(2,1)S(1)}, u32[]{:S(2)}, u32[]{:S(2)}) collective-permute-start(bf16[192,768]{1,0:T(8,128)(2,1)S(1)} %pick.3), channel_id=1, source_target_pairs={{0,2},{2,4},{4,6},{7,5},{5,3},{3,1},{8,10},{10,12},{12,14},{15,13}... | collective-permute-start | bytes 884744 | tf_op jit(solution)/shard_map/ppermute | solution.py:361
  24.8 0.0 collective-permute-done.10.refs_1_.came
  24.9 4.5 %collective-permute-start.13 = (bf16[192,768]{1,0:T(8,128)(2,1)S(1)}, bf16[192,768]{1,0:T(8,128)(2,1)S(1)}, u32[]{:S(2)}, u32[]{:S(2)}) collective-permute-start(bf16[192,768]{1,0:T(8,128)(2,1)S(1)} %pick.4), channel_id=1, source_target_pairs={{0,2},{2,4},{4,6},{7,5},{5,3},{3,1},{8,10},{10,12},{12,14},{15,13}... | collective-permute-start | bytes 884744 | tf_op jit(solution)/shard_map/ppermute | solution.py:361
  29.4 3.1 %collective-permute-start.16 = (bf16[128,768]{1,0:T(8,128)(2,1)S(1)}, bf16[128,768]{1,0:T(8,128)(2,1)S(1)}, u32[]{:S(2)}, u32[]{:S(2)}) collective-permute-start(bf16[128,768]{1,0:T(8,128)(2,1)S(1)} %pick.5), channel_id=1, source_target_pairs={{0,2},{2,4},{4,6},{7,5},{5,3},{3,1},{8,10},{10,12},{12,14},{15,13}... | collective-permute-start | bytes 589832 | tf_op jit(solution)/shard_map/ppermute | solution.py:361
  32.6 0.7 %collective-permute-start.18 = (bf16[128,768]{1,0:T(8,128)(2,1)S(1)}, bf16[128,768]{1,0:T(8,128)(2,1)S(1)}, u32[]{:S(2)}, u32[]{:S(2)}) collective-permute-start(bf16[128,768]{1,0:T(8,128)(2,1)S(1)} %join.12), channel_id=1, source_target_pairs={{2,6},{5,1},{10,14},{13,9},{18,22},{21,17},{26,30},{29,25}} | collective-permute-start | bytes 589832 | tf_op jit(solution)/shard_map/ppermute | solution.py:361
  33.3 1.9 %own_kernel.1 = (f32[256,896]{1,0:T(8,128)S(1)}, f32[256,896]{1,0:T(8,128)S(1)}) custom-call(bf16[2048,768]{1,0:T(8,128)(2,1)S(1)} %get-tuple-element.25.table, f32[2048,1]{1,0:T(8,128)S(1)} %get-tuple-element.26.half_norms, f32[256,896]{1,0:T(8,128)S(1)} %get-tuple-element.27.keep_in.after, ...), custom_call_target="tpu_custom_call", output_to_operand_aliasing={{0}: (2, {}), {1}: (3, {})} | custom-call | flops 268435456 | tf_op jit(solution)/shard_map/own_kernel/pallas_call | solution.py:372
  35.2 0.0 collective-permute-done.11.refs_0_
  35.2 0.2 step_kernel.3
  35.5 0.0 collective-permute-done.12.refs_0_
  35.5 0.2 step_kernel.4
  35.7 0.0 collective-permute-done.13.refs_0_
  35.7 0.2 step_kernel.5
  36.0 0.0 collective-permute-done.16.refs_1_
  36.0 2.5 %collective-permute-start.17 = (bf16[128,768]{1,0:T(8,128)(2,1)S(1)}, bf16[128,768]{1,0:T(8,128)(2,1)S(1)}, u32[]{:S(2)}, u32[]{:S(2)}) collective-permute-start(bf16[128,768]{1,0:T(8,128)(2,1)S(1)} %join.11.came), channel_id=1, source_target_pairs={{0,1},{1,0},{2,3},{3,2},{4,5},{5,4},{6,7},{7,6},{8,9},{9,8},{10,11... | collective-permute-start | bytes 589832 | tf_op jit(solution)/shard_map/ppermute | solution.py:356
  38.5 0.1 fusion
  38.6 0.1 collective-permute-start.14
  38.7 0.5 %collective-permute-start.15 = (f32[128,896]{1,0:T(8,128)S(1)}, f32[128,896]{1,0:T(8,128)S(1)}, u32[]{:S(2)}, u32[]{:S(2)}) collective-permute-start(f32[128,896]{1,0:T(8,128)S(1)} %get-tuple-element.38), channel_id=1, source_target_pairs={{0,1},{1,0},{2,3},{3,2},{4,5},{5,4},{6,7},{7,6},{8,9},{9,8},{10,11... | collective-permute-start | bytes 1376264 | tf_op jit(solution)/shard_map/ppermute | solution.py:356
  39.2 0.0 collective-permute-done.18.refs_1_
  39.2 1.5 %collective-permute-start.19 = (bf16[128,768]{1,0:T(8,128)(2,1)S(1)}, bf16[128,768]{1,0:T(8,128)(2,1)S(1)}, u32[]{:S(2)}, u32[]{:S(2)}) collective-permute-start(bf16[128,768]{1,0:T(8,128)(2,1)S(1)} %join.13.refs_0_), channel_id=1, source_target_pairs={{0,1},{1,0},{2,3},{3,2},{4,5},{5,4},{6,7},{7,6},{8,9},{9,8},{10,11... | collective-permute-start | bytes 589832 | tf_op jit(solution)/shard_map/ppermute | solution.py:356
  40.7 0.0 collective-permute-done.14
  40.7 0.4 %collective-permute-done.15 = f32[128,896]{1,0:T(8,128)S(1)} collective-permute-done((f32[128,896]{1,0:T(8,128)S(1)}, f32[128,896]{1,0:T(8,128)S(1)}, u32[]{:S(2)}, u32[]{:S(2)}) %collective-permute-start.15) | collective-permute-done | bytes 458784 | tf_op jit(solution)/shard_map/ppermute | solution.py:356
  41.1 0.1 pad_maximum_fusion.got
  41.2 0.0 collective-permute-done.17.passed
  41.2 0.5 %collective-permute-done.19.refs_1_ = bf16[128,768]{1,0:T(8,128)(2,1)S(1)} collective-permute-done((bf16[128,768]{1,0:T(8,128)(2,1)S(1)}, bf16[128,768]{1,0:T(8,128)(2,1)S(1)}, u32[]{:S(2)}, u32[]{:S(2)}) %collective-permute-start.19) | collective-permute-done | bytes 196640 | tf_op jit(solution)/shard_map/ppermute | solution.py:356
  41.7 2.3 %refit_kernel.1 = bf16[256,768]{1,0:T(8,128)(2,1)} custom-call(bf16[2048,768]{1,0:T(8,128)(2,1)S(1)} %get-tuple-element.25.table, f32[2048,1]{1,0:T(8,128)S(1)} %get-tuple-element.26.half_norms, f32[256,896]{1,0:T(8,128)S(1)} %get-tuple-element.35.refs_0_.keep, f32[256,896]{1,0:T(8,128)S(1)} %pad_maximum_fusion.got, bf16[128,768]{1,0:T(8,128)(2,1)S(1)} %join.11.came, ...), custom_call_target="tpu_custom_call" | custom-call | flops 268435456 | tf_op jit(solution)/shard_map/refit_kernel/pallas_call | solution.py:372
  (10 shorter events, 0.2 us)
Async XLA Ops:
  1.4 4.7 %collective-permute-start.3 = (bf16[64,768]{1,0:T(8,128)(2,1)S(1)}, bf16[64,768]{1,0:T(8,128)(2,1)S(1)}, u32[]{:S(2)}, u32[]{:S(2)}) collective-permute-start(bf16[64,768]{1,0:T(8,128)(2,1)S(1)} %get-tuple-element.21.refs_0_.near), channel_id=1, source_target_pairs={{0,1},{1,0},{2,3},{3,2},{4,5},{5,4},{6,7},{7,6},{8,9},{9,8},{10,11... | collective-permute-start | bytes 294920 | tf_op jit(solution)/shard_map/ppermute | solution.py:356
  2.0 9.8 %collective-permute-start = (bf16[64,768]{1,0:T(8,128)(2,1)S(1)}, bf16[64,768]{1,0:T(8,128)(2,1)S(1)}, u32[]{:S(2)}, u32[]{:S(2)}) collective-permute-start(bf16[64,768]{1,0:T(8,128)(2,1)S(1)} %get-tuple-element.22), channel_id=1, source_target_pairs={{0,24},{8,16},{16,8},{24,0},{1,25},{9,17},{17,9},{25,1},{2,26},{10... | collective-permute-start | bytes 294920 | tf_op jit(solution)/shard_map/ppermute | solution.py:392
  5.5 6.3 %collective-permute-start.1 = (bf16[64,768]{1,0:T(8,128)(2,1)S(1)}, bf16[64,768]{1,0:T(8,128)(2,1)S(1)}, u32[]{:S(2)}, u32[]{:S(2)}) collective-permute-start(bf16[64,768]{1,0:T(8,128)(2,1)S(1)} %get-tuple-element.23), channel_id=1, source_target_pairs={{0,16},{8,24},{16,0},{24,8},{1,17},{9,25},{17,1},{25,9},{2,18},{10... | collective-permute-start | bytes 294920 | tf_op jit(solution)/shard_map/ppermute | solution.py:392
  6.0 6.3 %collective-permute-start.2 = (bf16[64,768]{1,0:T(8,128)(2,1)S(1)}, bf16[64,768]{1,0:T(8,128)(2,1)S(1)}, u32[]{:S(2)}, u32[]{:S(2)}) collective-permute-start(bf16[64,768]{1,0:T(8,128)(2,1)S(1)} %get-tuple-element.24), channel_id=1, source_target_pairs={{0,8},{8,0},{16,24},{24,16},{1,9},{9,1},{17,25},{25,17},{2,10},{10... | collective-permute-start | bytes 294920 | tf_op jit(solution)/shard_map/ppermute | solution.py:392
  6.1 14.4 %collective-permute-start.5 = (bf16[128,768]{1,0:T(8,128)(2,1)S(1)}, bf16[128,768]{1,0:T(8,128)(2,1)S(1)}, u32[]{:S(2)}, u32[]{:S(2)}) collective-permute-start(bf16[128,768]{1,0:T(8,128)(2,1)S(1)} %join.8.own), channel_id=1, source_target_pairs={{2,6},{5,1},{10,14},{13,9},{18,22},{21,17},{26,30},{29,25}} | collective-permute-start | bytes 589832 | tf_op jit(solution)/shard_map/ppermute | solution.py:361
  6.8 13.7 %collective-permute-start.4 = (bf16[128,768]{1,0:T(8,128)(2,1)S(1)}, bf16[128,768]{1,0:T(8,128)(2,1)S(1)}, u32[]{:S(2)}, u32[]{:S(2)}) collective-permute-start(bf16[128,768]{1,0:T(8,128)(2,1)S(1)} %join.8.own), channel_id=1, source_target_pairs={{0,4},{4,6},{7,3},{3,1},{8,12},{12,14},{15,11},{11,9},{16,20},{20,... | collective-permute-start | bytes 589832 | tf_op jit(solution)/shard_map/ppermute | solution.py:361
  11.7 1.4 %collective-permute-start.7 = (bf16[64,768]{1,0:T(8,128)(2,1)S(1)}, bf16[64,768]{1,0:T(8,128)(2,1)S(1)}, u32[]{:S(2)}, u32[]{:S(2)}) collective-permute-start(bf16[64,768]{1,0:T(8,128)(2,1)S(1)} %collective-permute-done.refs_0_), channel_id=1, source_target_pairs={{0,1},{1,0},{2,3},{3,2},{4,5},{5,4},{6,7},{7,6},{8,9},{9,8},{10,11... | collective-permute-start | bytes 294920 | tf_op jit(solution)/shard_map/ppermute | solution.py:356
  11.8 5.4 %collective-permute-start.8 = (bf16[64,768]{1,0:T(8,128)(2,1)S(1)}, bf16[64,768]{1,0:T(8,128)(2,1)S(1)}, u32[]{:S(2)}, u32[]{:S(2)}) collective-permute-start(bf16[64,768]{1,0:T(8,128)(2,1)S(1)} %collective-permute-done.1.refs_1_), channel_id=1, source_target_pairs={{0,1},{1,0},{2,3},{3,2},{4,5},{5,4},{6,7},{7,6},{8,9},{9,8},{10,11... | collective-permute-start | bytes 294920 | tf_op jit(solution)/shard_map/ppermute | solution.py:356
  12.3 4.9 %collective-permute-start.9 = (bf16[64,768]{1,0:T(8,128)(2,1)S(1)}, bf16[64,768]{1,0:T(8,128)(2,1)S(1)}, u32[]{:S(2)}, u32[]{:S(2)}) collective-permute-start(bf16[64,768]{1,0:T(8,128)(2,1)S(1)} %collective-permute-done.2.refs_2_), channel_id=1, source_target_pairs={{0,1},{1,0},{2,3},{3,2},{4,5},{5,4},{6,7},{7,6},{8,9},{9,8},{10,11... | collective-permute-start | bytes 294920 | tf_op jit(solution)/shard_map/ppermute | solution.py:356
  13.1 9.7 %collective-permute-start.6 = (bf16[192,768]{1,0:T(8,128)(2,1)S(1)}, bf16[192,768]{1,0:T(8,128)(2,1)S(1)}, u32[]{:S(2)}, u32[]{:S(2)}) collective-permute-start(bf16[192,768]{1,0:T(8,128)(2,1)S(1)} %join.7.far.own), channel_id=1, source_target_pairs={{0,4},{4,6},{7,3},{3,1},{8,12},{12,14},{15,11},{11,9},{16,20},{20,... | collective-permute-start | bytes 884744 | tf_op jit(solution)/shard_map/ppermute | solution.py:361
  17.3 7.6 %collective-permute-start.10 = (bf16[192,768]{1,0:T(8,128)(2,1)S(1)}, bf16[192,768]{1,0:T(8,128)(2,1)S(1)}, u32[]{:S(2)}, u32[]{:S(2)}) collective-permute-start(bf16[192,768]{1,0:T(8,128)(2,1)S(1)} %join.9.own), channel_id=1, source_target_pairs={{0,4},{4,6},{7,3},{3,1},{8,12},{12,14},{15,11},{11,9},{16,20},{20,... | collective-permute-start | bytes 884744 | tf_op jit(solution)/shard_map/ppermute | solution.py:361
  19.8 15.4 %collective-permute-start.11 = (bf16[256,768]{1,0:T(8,128)(2,1)S(1)}, bf16[256,768]{1,0:T(8,128)(2,1)S(1)}, u32[]{:S(2)}, u32[]{:S(2)}) collective-permute-start(bf16[256,768]{1,0:T(8,128)(2,1)S(1)} %join.10), channel_id=1, source_target_pairs={{2,6},{5,1},{10,14},{13,9},{18,22},{21,17},{26,30},{29,25}} | collective-permute-start | bytes 1179656 | tf_op jit(solution)/shard_map/ppermute | solution.py:361
  22.9 12.6 %collective-permute-start.12 = (bf16[192,768]{1,0:T(8,128)(2,1)S(1)}, bf16[192,768]{1,0:T(8,128)(2,1)S(1)}, u32[]{:S(2)}, u32[]{:S(2)}) collective-permute-start(bf16[192,768]{1,0:T(8,128)(2,1)S(1)} %pick.3), channel_id=1, source_target_pairs={{0,2},{2,4},{4,6},{7,5},{5,3},{3,1},{8,10},{10,12},{12,14},{15,13}... | collective-permute-start | bytes 884744 | tf_op jit(solution)/shard_map/ppermute | solution.py:361
  24.9 10.8 %collective-permute-start.13 = (bf16[192,768]{1,0:T(8,128)(2,1)S(1)}, bf16[192,768]{1,0:T(8,128)(2,1)S(1)}, u32[]{:S(2)}, u32[]{:S(2)}) collective-permute-start(bf16[192,768]{1,0:T(8,128)(2,1)S(1)} %pick.4), channel_id=1, source_target_pairs={{0,2},{2,4},{4,6},{7,5},{5,3},{3,1},{8,10},{10,12},{12,14},{15,13}... | collective-permute-start | bytes 884744 | tf_op jit(solution)/shard_map/ppermute | solution.py:361
  29.4 6.5 %collective-permute-start.16 = (bf16[128,768]{1,0:T(8,128)(2,1)S(1)}, bf16[128,768]{1,0:T(8,128)(2,1)S(1)}, u32[]{:S(2)}, u32[]{:S(2)}) collective-permute-start(bf16[128,768]{1,0:T(8,128)(2,1)S(1)} %pick.5), channel_id=1, source_target_pairs={{0,2},{2,4},{4,6},{7,5},{5,3},{3,1},{8,10},{10,12},{12,14},{15,13}... | collective-permute-start | bytes 589832 | tf_op jit(solution)/shard_map/ppermute | solution.py:361
  32.6 6.5 %collective-permute-start.18 = (bf16[128,768]{1,0:T(8,128)(2,1)S(1)}, bf16[128,768]{1,0:T(8,128)(2,1)S(1)}, u32[]{:S(2)}, u32[]{:S(2)}) collective-permute-start(bf16[128,768]{1,0:T(8,128)(2,1)S(1)} %join.12), channel_id=1, source_target_pairs={{2,6},{5,1},{10,14},{13,9},{18,22},{21,17},{26,30},{29,25}} | collective-permute-start | bytes 589832 | tf_op jit(solution)/shard_map/ppermute | solution.py:361
  36.0 5.2 %collective-permute-start.17 = (bf16[128,768]{1,0:T(8,128)(2,1)S(1)}, bf16[128,768]{1,0:T(8,128)(2,1)S(1)}, u32[]{:S(2)}, u32[]{:S(2)}) collective-permute-start(bf16[128,768]{1,0:T(8,128)(2,1)S(1)} %join.11.came), channel_id=1, source_target_pairs={{0,1},{1,0},{2,3},{3,2},{4,5},{5,4},{6,7},{7,6},{8,9},{9,8},{10,11... | collective-permute-start | bytes 589832 | tf_op jit(solution)/shard_map/ppermute | solution.py:356
  38.6 2.1 %collective-permute-start.14 = (f32[128,896]{1,0:T(8,128)S(1)}, f32[128,896]{1,0:T(8,128)S(1)}, u32[]{:S(2)}, u32[]{:S(2)}) collective-permute-start(f32[128,896]{1,0:T(8,128)S(1)} %get-tuple-element.37), channel_id=1, source_target_pairs={{0,1},{1,0},{2,3},{3,2},{4,5},{5,4},{6,7},{7,6},{8,9},{9,8},{10,11... | collective-permute-start | bytes 1376264 | tf_op jit(solution)/shard_map/ppermute | solution.py:356
  38.7 2.5 %collective-permute-start.15 = (f32[128,896]{1,0:T(8,128)S(1)}, f32[128,896]{1,0:T(8,128)S(1)}, u32[]{:S(2)}, u32[]{:S(2)}) collective-permute-start(f32[128,896]{1,0:T(8,128)S(1)} %get-tuple-element.38), channel_id=1, source_target_pairs={{0,1},{1,0},{2,3},{3,2},{4,5},{5,4},{6,7},{7,6},{8,9},{9,8},{10,11... | collective-permute-start | bytes 1376264 | tf_op jit(solution)/shard_map/ppermute | solution.py:356
  39.2 2.6 %collective-permute-start.19 = (bf16[128,768]{1,0:T(8,128)(2,1)S(1)}, bf16[128,768]{1,0:T(8,128)(2,1)S(1)}, u32[]{:S(2)}, u32[]{:S(2)}) collective-permute-start(bf16[128,768]{1,0:T(8,128)(2,1)S(1)} %join.13.refs_0_), channel_id=1, source_target_pairs={{0,1},{1,0},{2,3},{3,2},{4,5},{5,4},{6,7},{7,6},{8,9},{9,8},{10,11... | collective-permute-start | bytes 589832 | tf_op jit(solution)/shard_map/ppermute | solution.py:356

commit v5 on v4

--- a/solution.py
+++ b/solution.py
@@ -312,15 +312,25 @@
     return (level == 0) | (level == depth - 1)
 
 
-def refit_kernel(tile, depth, table, half_norms, keep, got, came, passed, *refs):
-    over_came, over_passed, refined, rows, scores, sums = refs
+def base_kernel(tile, table, keep, *refs):
+    parts, base = refs[:-1], refs[-1]
+    feature_dim = table.shape[1]
+    mine = chip_place()[2]
+    start = 0
+    for got in parts:
+        rows = got.shape[0]
+        span = slice(start, start + rows)
+        old = table[pl.ds(pl.multiple_of(mine * tile + start, rows), rows), :].astype(jnp.float32)
+        base[span, :feature_dim] = keep[span, :feature_dim] + got[:, :feature_dim] + old
+        base[span, feature_dim:] = keep[span, feature_dim:] + got[:, feature_dim:] + 1.0
+        start += rows
+
+
+def refit_kernel(tile, depth, table, half_norms, base, came, passed, *refs):
+    over_came, over_passed, refined, rows, scores, out, sent = refs
     feature_dim = table.shape[1]
     mine = chip_place()[2]
     end, here = end_chip(depth), came_to(1, depth)
-    sums[...] = keep[...] + got[...]
-
-    def add(*parts):
-        add_rows(table, half_norms, parts, rows, scores, ((mine, sums),), tile)
 
     @pl.when(end & here)
     def _():
@@ -334,10 +344,20 @@
     def _():
         gather_rows((came, passed), rows)
 
-    add(rows)
-    old = table[at_tile(mine, tile), :].astype(jnp.float32)
-    scale = 1.0 / (sums[:, feature_dim : feature_dim + 1] + 1.0)
-    refined[...] = ((sums[:, :feature_dim] + old) * scale).astype(jnp.bfloat16)
+    all_rows = rows[...]
+    terms = softmax_terms(table, half_norms, all_rows, scores, tile)
+    half = tile // sent.shape[0]
+    copies = []
+    for index in range(sent.shape[0]):
+        span = slice(index * half, (index + 1) * half)
+        at = pl.ds(pl.multiple_of(mine * tile + index * half, half), half)
+        sums, count = tile_sums(scores[at, :], *terms, all_rows)
+        scale = 1.0 / (base[span, feature_dim : feature_dim + 1] + count[:, :1])
+        out[span, :] = ((base[span, :feature_dim] + sums) * scale).astype(jnp.bfloat16)
+        copies.append(pltpu.make_async_copy(out.at[span], refined.at[span], sent.at[index]))
+        copies[-1].start()
+    for copy in copies:
+        copy.wait()
 
 
 def cost(flops=1 << 20):
@@ -368,12 +388,12 @@
     sums_shape = jax.ShapeDtypeStruct((tile, feature_dim + lanes), jnp.float32)
     norms_shape = jax.ShapeDtypeStruct((fine_count, 1), jnp.float32)
 
-    def kernel(body, out_shape, *operands, scratch=(), aliases={}, flops=1 << 28, specs=()):
+    def kernel(body, out_shape, *operands, scratch=(), aliases={}, flops=1 << 28, specs=(), out_specs=None):
         return pl.pallas_call(
             body,
             out_shape=out_shape,
             in_specs=list(specs) + [vmem()] * (len(operands) - len(specs)),
-            out_specs=jax.tree.map(lambda _: vmem(), out_shape),
+            out_specs=out_specs or jax.tree.map(lambda _: vmem(), out_shape),
             scratch_shapes=scratch,
             input_output_aliases=aliases,
             compiler_params=pltpu.CompilerParams(vmem_limit_bytes=vmem_limit),
@@ -439,7 +459,15 @@
     beside_body = functools.partial(step_kernel, tile, depth, 1)
     keep, give = add(beside_body, keep, give, beside_first, flops=beside_flops)
     keep, give = add(beside_body, keep, give, beside_second)
-    got = jnp.concatenate([swap(give[: tile // 2]), swap(give[tile // 2 :])], axis=0)
+    base = kernel(
+        functools.partial(base_kernel, tile),
+        sums_shape,
+        table,
+        keep,
+        swap(give[: tile // 2]),
+        swap(give[tile // 2 :]),
+        flops=1 << 20,
+    )
     over_last = join([over_second], keep, flops=over_flops)
     beside_last = join([beside_near], keep, flops=last_flops)
     return kernel(
@@ -447,13 +475,14 @@
         jax.ShapeDtypeStruct((tile, feature_dim), jnp.bfloat16),
         table,
         half_norms,
-        keep,
-        got,
+        base,
         beside_last,
         swap(beside_last),
         over_last,
         swap(over_last),
-        scratch=scratch(2 * near.shape[0]) + [pltpu.VMEM(sums_shape.shape, jnp.float32)],
+        scratch=scratch(2 * near.shape[0])
+        + [pltpu.VMEM((tile, feature_dim), jnp.bfloat16), pltpu.SemaphoreType.DMA((2,))],
+        out_specs=hbm(),
     )
 
 

time: 44.3 us -> 44.3 us (level)
    pallas_call x6 -> x7, Pallas kernels: 7.22 us -> 7.17 us  [kernel(): pl.pallas_call(body, out_shape=out_shape, in_specs=list(specs) + [vmem()]...]
where the time goes in v5:
time: 44.3 us; the launch traced here: 44 us
  starting transfers between devices  33 us (74%)
  Pallas kernels  8.85 us (20%)
  waiting for transfers between devices  1.66 us (4%)
  between operations  0.47 us (1%)
    ppermute x9, starting transfers between devices, along(): return lax.ppermute(x, 'member', up + down)  23.1 us
    pallas_call x7, Pallas kernels, kernel(): pl.pallas_call(body, out_shape=out_shape, in_specs=list(specs) + [vmem()]...  7.17 us
    ppermute x8, starting transfers between devices, swap(): return lax.ppermute(x, 'member', [(i, i ^ 1) for i in range(member_count)])  5.72 us
    ppermute x3, starting transfers between devices, handoff(): lax.ppermute(packed[k], 'group', [(i, i ^ k) for i in range(group_count)])  4.16 us
    ppermute x8, waiting for transfers between devices, swap(): return lax.ppermute(x, 'member', [(i, i ^ 1) for i in range(member_count)])  1.63 us
    pallas_call x1, Pallas kernels, pack(): pl.pallas_call(pack_kernel, out_shape=[jax.ShapeDtypeStruct((capacity, fe...  1.43 us
  transfers between devices with their start and end apart: 20, of which 3 were waited for; matrix products, arithmetic and copies ran while one was open for 0% of the time, Pallas kernels for 12%

profile of v5, /device:TPU:0, one launch (start us, length us, event | category | flops | bytes accessed | tf_op | source)
XLA Modules:
  0.0 44.0 jit_solution(11809644772689058390)
XLA Ops:
  0.0 1.4 %pack.1 = (bf16[64,768]{1,0:T(8,128)(2,1)S(1)}, bf16[64,768]{1,0:T(8,128)(2,1)S(1)}, bf16[64,768]{1,0:T(8,128)(2,1)S(1)}, bf16[64,768]{1,0:T(8,128)(2,1)S(1)}) custom-call(s32[1,256]{1,0:T(1,128)} %bitcast.1, bf16[256,768]{1,0:T(8,128)(2,1)} %points.1), custom_call_target="tpu_custom_call" | custom-call | flops 1048576 | tf_op jit(solution)/shard_map/pack/pallas_call | solution.py:167
  1.4 0.5 %collective-permute-start.3 = (bf16[64,768]{1,0:T(8,128)(2,1)S(1)}, bf16[64,768]{1,0:T(8,128)(2,1)S(1)}, u32[]{:S(2)}, u32[]{:S(2)}) collective-permute-start(bf16[64,768]{1,0:T(8,128)(2,1)S(1)} %get-tuple-element.21.refs_0_.near), channel_id=1, source_target_pairs={{0,1},{1,0},{2,3},{3,2},{4,5},{5,4},{6,7},{7,6},{8,9},{9,8},{10,11... | collective-permute-start | bytes 294920 | tf_op jit(solution)/shard_map/ppermute | solution.py:376
  2.0 3.5 %collective-permute-start = (bf16[64,768]{1,0:T(8,128)(2,1)S(1)}, bf16[64,768]{1,0:T(8,128)(2,1)S(1)}, u32[]{:S(2)}, u32[]{:S(2)}) collective-permute-start(bf16[64,768]{1,0:T(8,128)(2,1)S(1)} %get-tuple-element.22), channel_id=1, source_target_pairs={{0,24},{8,16},{16,8},{24,0},{1,25},{9,17},{17,9},{25,1},{2,26},{10... | collective-permute-start | bytes 294920 | tf_op jit(solution)/shard_map/ppermute | solution.py:412
  5.5 0.5 %collective-permute-start.1 = (bf16[64,768]{1,0:T(8,128)(2,1)S(1)}, bf16[64,768]{1,0:T(8,128)(2,1)S(1)}, u32[]{:S(2)}, u32[]{:S(2)}) collective-permute-start(bf16[64,768]{1,0:T(8,128)(2,1)S(1)} %get-tuple-element.23), channel_id=1, source_target_pairs={{0,16},{8,24},{16,0},{24,8},{1,17},{9,25},{17,1},{25,9},{2,18},{10... | collective-permute-start | bytes 294920 | tf_op jit(solution)/shard_map/ppermute | solution.py:412
  6.0 0.1 collective-permute-start.2
  6.1 0.0 collective-permute-done.3.refs_1_
  6.1 0.7 %collective-permute-start.5 = (bf16[128,768]{1,0:T(8,128)(2,1)S(1)}, bf16[128,768]{1,0:T(8,128)(2,1)S(1)}, u32[]{:S(2)}, u32[]{:S(2)}) collective-permute-start(bf16[128,768]{1,0:T(8,128)(2,1)S(1)} %join.8.own), channel_id=1, source_target_pairs={{2,6},{5,1},{10,14},{13,9},{18,22},{21,17},{26,30},{29,25}} | collective-permute-start | bytes 589832 | tf_op jit(solution)/shard_map/ppermute | solution.py:381
  6.8 4.9 %collective-permute-start.4 = (bf16[128,768]{1,0:T(8,128)(2,1)S(1)}, bf16[128,768]{1,0:T(8,128)(2,1)S(1)}, u32[]{:S(2)}, u32[]{:S(2)}) collective-permute-start(bf16[128,768]{1,0:T(8,128)(2,1)S(1)} %join.8.own), channel_id=1, source_target_pairs={{0,4},{4,6},{7,3},{3,1},{8,12},{12,14},{15,11},{11,9},{16,20},{20,... | collective-permute-start | bytes 589832 | tf_op jit(solution)/shard_map/ppermute | solution.py:381
  11.7 0.0 collective-permute-done.refs_0_
  11.7 0.1 collective-permute-start.7
  11.8 0.0 collective-permute-done.1.refs_1_
  11.8 0.5 %collective-permute-start.8 = (bf16[64,768]{1,0:T(8,128)(2,1)S(1)}, bf16[64,768]{1,0:T(8,128)(2,1)S(1)}, u32[]{:S(2)}, u32[]{:S(2)}) collective-permute-start(bf16[64,768]{1,0:T(8,128)(2,1)S(1)} %collective-permute-done.1.refs_1_), channel_id=1, source_target_pairs={{0,1},{1,0},{2,3},{3,2},{4,5},{5,4},{6,7},{7,6},{8,9},{9,8},{10,11... | collective-permute-start | bytes 294920 | tf_op jit(solution)/shard_map/ppermute | solution.py:376
  12.3 0.0 collective-permute-done.2.refs_2_
  12.3 0.1 collective-permute-start.9
  12.4 0.7 %collective-permute-done.7.refs_0_.refs_3_ = bf16[64,768]{1,0:T(8,128)(2,1)S(1)} collective-permute-done((bf16[64,768]{1,0:T(8,128)(2,1)S(1)}, bf16[64,768]{1,0:T(8,128)(2,1)S(1)}, u32[]{:S(2)}, u32[]{:S(2)}) %collective-permute-start.7) | collective-permute-done | bytes 98336 | tf_op jit(solution)/shard_map/ppermute | solution.py:376
  13.1 4.1 %collective-permute-start.6 = (bf16[192,768]{1,0:T(8,128)(2,1)S(1)}, bf16[192,768]{1,0:T(8,128)(2,1)S(1)}, u32[]{:S(2)}, u32[]{:S(2)}) collective-permute-start(bf16[192,768]{1,0:T(8,128)(2,1)S(1)} %join.7.far.own), channel_id=1, source_target_pairs={{0,4},{4,6},{7,3},{3,1},{8,12},{12,14},{15,11},{11,9},{16,20},{20,... | collective-permute-start | bytes 884744 | tf_op jit(solution)/shard_map/ppermute | solution.py:381
  17.2 0.0 collective-permute-done.8.refs_1_.refs_0_
  17.2 0.0 collective-permute-done.9.refs_2_.refs_1_
  17.3 2.5 %collective-permute-start.10 = (bf16[192,768]{1,0:T(8,128)(2,1)S(1)}, bf16[192,768]{1,0:T(8,128)(2,1)S(1)}, u32[]{:S(2)}, u32[]{:S(2)}) collective-permute-start(bf16[192,768]{1,0:T(8,128)(2,1)S(1)} %join.9.own), channel_id=1, source_target_pairs={{0,4},{4,6},{7,3},{3,1},{8,12},{12,14},{15,11},{11,9},{16,20},{20,... | collective-permute-start | bytes 884744 | tf_op jit(solution)/shard_map/ppermute | solution.py:381
  19.8 0.7 %collective-permute-start.11 = (bf16[256,768]{1,0:T(8,128)(2,1)S(1)}, bf16[256,768]{1,0:T(8,128)(2,1)S(1)}, u32[]{:S(2)}, u32[]{:S(2)}) collective-permute-start(bf16[256,768]{1,0:T(8,128)(2,1)S(1)} %join.10), channel_id=1, source_target_pairs={{2,6},{5,1},{10,14},{13,9},{18,22},{21,17},{26,30},{29,25}} | collective-permute-start | bytes 1179656 | tf_op jit(solution)/shard_map/ppermute | solution.py:381
  20.5 0.0 collective-permute-done.5.over
  20.5 0.0 collective-permute-done.4.apart.apart_near.came
  20.5 2.3 %first_kernel.1 = (bf16[2048,768]{1,0:T(8,128)(2,1)S(1)}, f32[256,896]{1,0:T(8,128)S(1)}, f32[256,896]{1,0:T(8,128)S(1)}, f32[2048,1]{1,0:T(8,128)S(1)}) custom-call(bf16[2048,768]{1,0:T(8,128)(2,1)} %table_from.1, bf16[64,768]{1,0:T(8,128)(2,1)S(1)} %get-tuple-element.21.refs_0_.near, bf16[192,768]{1,0:T(8,128)(2,1)S(1)} %join.7.far.own, ...), custom_call_target="tpu_custom_call" | custom-call | flops 2147483648 | tf_op jit(solution)/shard_map/first_kernel/pallas_call | solution.py:392
  22.8 0.0 collective-permute-done.6.refs_0_.came
  22.9 1.9 %collective-permute-start.12 = (bf16[192,768]{1,0:T(8,128)(2,1)S(1)}, bf16[192,768]{1,0:T(8,128)(2,1)S(1)}, u32[]{:S(2)}, u32[]{:S(2)}) collective-permute-start(bf16[192,768]{1,0:T(8,128)(2,1)S(1)} %pick.3), channel_id=1, source_target_pairs={{0,2},{2,4},{4,6},{7,5},{5,3},{3,1},{8,10},{10,12},{12,14},{15,13}... | collective-permute-start | bytes 884744 | tf_op jit(solution)/shard_map/ppermute | solution.py:381
  24.8 0.0 collective-permute-done.10.refs_1_.came
  24.9 4.5 %collective-permute-start.13 = (bf16[192,768]{1,0:T(8,128)(2,1)S(1)}, bf16[192,768]{1,0:T(8,128)(2,1)S(1)}, u32[]{:S(2)}, u32[]{:S(2)}) collective-permute-start(bf16[192,768]{1,0:T(8,128)(2,1)S(1)} %pick.4), channel_id=1, source_target_pairs={{0,2},{2,4},{4,6},{7,5},{5,3},{3,1},{8,10},{10,12},{12,14},{15,13}... | collective-permute-start | bytes 884744 | tf_op jit(solution)/shard_map/ppermute | solution.py:381
  29.4 3.1 %collective-permute-start.16 = (bf16[128,768]{1,0:T(8,128)(2,1)S(1)}, bf16[128,768]{1,0:T(8,128)(2,1)S(1)}, u32[]{:S(2)}, u32[]{:S(2)}) collective-permute-start(bf16[128,768]{1,0:T(8,128)(2,1)S(1)} %pick.5), channel_id=1, source_target_pairs={{0,2},{2,4},{4,6},{7,5},{5,3},{3,1},{8,10},{10,12},{12,14},{15,13}... | collective-permute-start | bytes 589832 | tf_op jit(solution)/shard_map/ppermute | solution.py:381
  32.6 0.7 %collective-permute-start.18 = (bf16[128,768]{1,0:T(8,128)(2,1)S(1)}, bf16[128,768]{1,0:T(8,128)(2,1)S(1)}, u32[]{:S(2)}, u32[]{:S(2)}) collective-permute-start(bf16[128,768]{1,0:T(8,128)(2,1)S(1)} %join.12), channel_id=1, source_target_pairs={{2,6},{5,1},{10,14},{13,9},{18,22},{21,17},{26,30},{29,25}} | collective-permute-start | bytes 589832 | tf_op jit(solution)/shard_map/ppermute | solution.py:381
  33.3 1.9 %own_kernel.1 = (f32[256,896]{1,0:T(8,128)S(1)}, f32[256,896]{1,0:T(8,128)S(1)}) custom-call(bf16[2048,768]{1,0:T(8,128)(2,1)S(1)} %get-tuple-element.25.table, f32[2048,1]{1,0:T(8,128)S(1)} %get-tuple-element.26.half_norms, f32[256,896]{1,0:T(8,128)S(1)} %get-tuple-element.27.keep_in.after, ...), custom_call_target="tpu_custom_call", output_to_operand_aliasing={{0}: (2, {}), {1}: (3, {})} | custom-call | flops 268435456 | tf_op jit(solution)/shard_map/own_kernel/pallas_call | solution.py:392
  35.2 0.0 collective-permute-done.11.refs_0_
  35.2 0.2 step_kernel.3
  35.5 0.0 collective-permute-done.12.refs_0_
  35.5 0.2 step_kernel.4
  35.7 0.0 collective-permute-done.13.refs_0_
  35.7 0.2 step_kernel.5
  36.0 0.0 collective-permute-done.16.refs_1_
  36.0 2.5 %collective-permute-start.17 = (bf16[128,768]{1,0:T(8,128)(2,1)S(1)}, bf16[128,768]{1,0:T(8,128)(2,1)S(1)}, u32[]{:S(2)}, u32[]{:S(2)}) collective-permute-start(bf16[128,768]{1,0:T(8,128)(2,1)S(1)} %join.11.came), channel_id=1, source_target_pairs={{0,1},{1,0},{2,3},{3,2},{4,5},{5,4},{6,7},{7,6},{8,9},{9,8},{10,11... | collective-permute-start | bytes 589832 | tf_op jit(solution)/shard_map/ppermute | solution.py:376
  38.5 0.1 fusion
  38.6 0.1 collective-permute-start.15
  38.7 0.5 %collective-permute-start.14 = (f32[128,896]{1,0:T(8,128)S(1)}, f32[128,896]{1,0:T(8,128)S(1)}, u32[]{:S(2)}, u32[]{:S(2)}) collective-permute-start(f32[128,896]{1,0:T(8,128)S(1)} %get-tuple-element.38), channel_id=1, source_target_pairs={{0,1},{1,0},{2,3},{3,2},{4,5},{5,4},{6,7},{7,6},{8,9},{9,8},{10,11... | collective-permute-start | bytes 1376264 | tf_op jit(solution)/shard_map/ppermute | solution.py:376
  39.2 0.0 collective-permute-done.18.refs_1_
  39.2 1.5 %collective-permute-start.19 = (bf16[128,768]{1,0:T(8,128)(2,1)S(1)}, bf16[128,768]{1,0:T(8,128)(2,1)S(1)}, u32[]{:S(2)}, u32[]{:S(2)}) collective-permute-start(bf16[128,768]{1,0:T(8,128)(2,1)S(1)} %join.13.refs_0_), channel_id=1, source_target_pairs={{0,1},{1,0},{2,3},{3,2},{4,5},{5,4},{6,7},{7,6},{8,9},{9,8},{10,11... | collective-permute-start | bytes 589832 | tf_op jit(solution)/shard_map/ppermute | solution.py:376
  40.7 0.0 collective-permute-done.15.refs_1_
  40.7 0.4 %collective-permute-done.14.refs_0_ = f32[128,896]{1,0:T(8,128)S(1)} collective-permute-done((f32[128,896]{1,0:T(8,128)S(1)}, f32[128,896]{1,0:T(8,128)S(1)}, u32[]{:S(2)}, u32[]{:S(2)}) %collective-permute-start.14) | collective-permute-done | bytes 458784 | tf_op jit(solution)/shard_map/ppermute | solution.py:376
  41.1 0.1 base_kernel.1.base
  41.2 0.0 collective-permute-done.17.passed
  41.2 0.5 %collective-permute-done.19.refs_1_ = bf16[128,768]{1,0:T(8,128)(2,1)S(1)} collective-permute-done((bf16[128,768]{1,0:T(8,128)(2,1)S(1)}, bf16[128,768]{1,0:T(8,128)(2,1)S(1)}, u32[]{:S(2)}, u32[]{:S(2)}) %collective-permute-start.19) | collective-permute-done | bytes 196640 | tf_op jit(solution)/shard_map/ppermute | solution.py:376
  41.7 2.1 %refit_kernel.1 = bf16[256,768]{1,0:T(8,128)(2,1)} custom-call(bf16[2048,768]{1,0:T(8,128)(2,1)S(1)} %get-tuple-element.25.table, f32[2048,1]{1,0:T(8,128)S(1)} %get-tuple-element.26.half_norms, f32[256,896]{1,0:T(8,128)S(1)} %base_kernel.1.base, bf16[128,768]{1,0:T(8,128)(2,1)S(1)} %join.11.came, bf16[128,768]{1,0:T(8,128)(2,1)S(1)} %collective-permute-done.17.passed, ...), custom_call_target="tpu_custom_call" | custom-call | flops 268435456 | tf_op jit(solution)/shard_map/refit_kernel/pallas_call | solution.py:392
  (10 shorter events, 0.2 us)
Async XLA Ops:
  1.4 4.7 %collective-permute-start.3 = (bf16[64,768]{1,0:T(8,128)(2,1)S(1)}, bf16[64,768]{1,0:T(8,128)(2,1)S(1)}, u32[]{:S(2)}, u32[]{:S(2)}) collective-permute-start(bf16[64,768]{1,0:T(8,128)(2,1)S(1)} %get-tuple-element.21.refs_0_.near), channel_id=1, source_target_pairs={{0,1},{1,0},{2,3},{3,2},{4,5},{5,4},{6,7},{7,6},{8,9},{9,8},{10,11... | collective-permute-start | bytes 294920 | tf_op jit(solution)/shard_map/ppermute | solution.py:376
  2.0 9.8 %collective-permute-start = (bf16[64,768]{1,0:T(8,128)(2,1)S(1)}, bf16[64,768]{1,0:T(8,128)(2,1)S(1)}, u32[]{:S(2)}, u32[]{:S(2)}) collective-permute-start(bf16[64,768]{1,0:T(8,128)(2,1)S(1)} %get-tuple-element.22), channel_id=1, source_target_pairs={{0,24},{8,16},{16,8},{24,0},{1,25},{9,17},{17,9},{25,1},{2,26},{10... | collective-permute-start | bytes 294920 | tf_op jit(solution)/shard_map/ppermute | solution.py:412
  5.5 6.3 %collective-permute-start.1 = (bf16[64,768]{1,0:T(8,128)(2,1)S(1)}, bf16[64,768]{1,0:T(8,128)(2,1)S(1)}, u32[]{:S(2)}, u32[]{:S(2)}) collective-permute-start(bf16[64,768]{1,0:T(8,128)(2,1)S(1)} %get-tuple-element.23), channel_id=1, source_target_pairs={{0,16},{8,24},{16,0},{24,8},{1,17},{9,25},{17,1},{25,9},{2,18},{10... | collective-permute-start | bytes 294920 | tf_op jit(solution)/shard_map/ppermute | solution.py:412
  6.0 6.3 %collective-permute-start.2 = (bf16[64,768]{1,0:T(8,128)(2,1)S(1)}, bf16[64,768]{1,0:T(8,128)(2,1)S(1)}, u32[]{:S(2)}, u32[]{:S(2)}) collective-permute-start(bf16[64,768]{1,0:T(8,128)(2,1)S(1)} %get-tuple-element.24), channel_id=1, source_target_pairs={{0,8},{8,0},{16,24},{24,16},{1,9},{9,1},{17,25},{25,17},{2,10},{10... | collective-permute-start | bytes 294920 | tf_op jit(solution)/shard_map/ppermute | solution.py:412
  6.1 14.4 %collective-permute-start.5 = (bf16[128,768]{1,0:T(8,128)(2,1)S(1)}, bf16[128,768]{1,0:T(8,128)(2,1)S(1)}, u32[]{:S(2)}, u32[]{:S(2)}) collective-permute-start(bf16[128,768]{1,0:T(8,128)(2,1)S(1)} %join.8.own), channel_id=1, source_target_pairs={{2,6},{5,1},{10,14},{13,9},{18,22},{21,17},{26,30},{29,25}} | collective-permute-start | bytes 589832 | tf_op jit(solution)/shard_map/ppermute | solution.py:381
  6.8 13.7 %collective-permute-start.4 = (bf16[128,768]{1,0:T(8,128)(2,1)S(1)}, bf16[128,768]{1,0:T(8,128)(2,1)S(1)}, u32[]{:S(2)}, u32[]{:S(2)}) collective-permute-start(bf16[128,768]{1,0:T(8,128)(2,1)S(1)} %join.8.own), channel_id=1, source_target_pairs={{0,4},{4,6},{7,3},{3,1},{8,12},{12,14},{15,11},{11,9},{16,20},{20,... | collective-permute-start | bytes 589832 | tf_op jit(solution)/shard_map/ppermute | solution.py:381
  11.7 1.4 %collective-permute-start.7 = (bf16[64,768]{1,0:T(8,128)(2,1)S(1)}, bf16[64,768]{1,0:T(8,128)(2,1)S(1)}, u32[]{:S(2)}, u32[]{:S(2)}) collective-permute-start(bf16[64,768]{1,0:T(8,128)(2,1)S(1)} %collective-permute-done.refs_0_), channel_id=1, source_target_pairs={{0,1},{1,0},{2,3},{3,2},{4,5},{5,4},{6,7},{7,6},{8,9},{9,8},{10,11... | collective-permute-start | bytes 294920 | tf_op jit(solution)/shard_map/ppermute | solution.py:376
  11.8 5.4 %collective-permute-start.8 = (bf16[64,768]{1,0:T(8,128)(2,1)S(1)}, bf16[64,768]{1,0:T(8,128)(2,1)S(1)}, u32[]{:S(2)}, u32[]{:S(2)}) collective-permute-start(bf16[64,768]{1,0:T(8,128)(2,1)S(1)} %collective-permute-done.1.refs_1_), channel_id=1, source_target_pairs={{0,1},{1,0},{2,3},{3,2},{4,5},{5,4},{6,7},{7,6},{8,9},{9,8},{10,11... | collective-permute-start | bytes 294920 | tf_op jit(solution)/shard_map/ppermute | solution.py:376
  12.3 4.9 %collective-permute-start.9 = (bf16[64,768]{1,0:T(8,128)(2,1)S(1)}, bf16[64,768]{1,0:T(8,128)(2,1)S(1)}, u32[]{:S(2)}, u32[]{:S(2)}) collective-permute-start(bf16[64,768]{1,0:T(8,128)(2,1)S(1)} %collective-permute-done.2.refs_2_), channel_id=1, source_target_pairs={{0,1},{1,0},{2,3},{3,2},{4,5},{5,4},{6,7},{7,6},{8,9},{9,8},{10,11... | collective-permute-start | bytes 294920 | tf_op jit(solution)/shard_map/ppermute | solution.py:376
  13.1 9.7 %collective-permute-start.6 = (bf16[192,768]{1,0:T(8,128)(2,1)S(1)}, bf16[192,768]{1,0:T(8,128)(2,1)S(1)}, u32[]{:S(2)}, u32[]{:S(2)}) collective-permute-start(bf16[192,768]{1,0:T(8,128)(2,1)S(1)} %join.7.far.own), channel_id=1, source_target_pairs={{0,4},{4,6},{7,3},{3,1},{8,12},{12,14},{15,11},{11,9},{16,20},{20,... | collective-permute-start | bytes 884744 | tf_op jit(solution)/shard_map/ppermute | solution.py:381
  17.3 7.6 %collective-permute-start.10 = (bf16[192,768]{1,0:T(8,128)(2,1)S(1)}, bf16[192,768]{1,0:T(8,128)(2,1)S(1)}, u32[]{:S(2)}, u32[]{:S(2)}) collective-permute-start(bf16[192,768]{1,0:T(8,128)(2,1)S(1)} %join.9.own), channel_id=1, source_target_pairs={{0,4},{4,6},{7,3},{3,1},{8,12},{12,14},{15,11},{11,9},{16,20},{20,... | collective-permute-start | bytes 884744 | tf_op jit(solution)/shard_map/ppermute | solution.py:381
  19.8 15.4 %collective-permute-start.11 = (bf16[256,768]{1,0:T(8,128)(2,1)S(1)}, bf16[256,768]{1,0:T(8,128)(2,1)S(1)}, u32[]{:S(2)}, u32[]{:S(2)}) collective-permute-start(bf16[256,768]{1,0:T(8,128)(2,1)S(1)} %join.10), channel_id=1, source_target_pairs={{2,6},{5,1},{10,14},{13,9},{18,22},{21,17},{26,30},{29,25}} | collective-permute-start | bytes 1179656 | tf_op jit(solution)/shard_map/ppermute | solution.py:381
  22.9 12.6 %collective-permute-start.12 = (bf16[192,768]{1,0:T(8,128)(2,1)S(1)}, bf16[192,768]{1,0:T(8,128)(2,1)S(1)}, u32[]{:S(2)}, u32[]{:S(2)}) collective-permute-start(bf16[192,768]{1,0:T(8,128)(2,1)S(1)} %pick.3), channel_id=1, source_target_pairs={{0,2},{2,4},{4,6},{7,5},{5,3},{3,1},{8,10},{10,12},{12,14},{15,13}... | collective-permute-start | bytes 884744 | tf_op jit(solution)/shard_map/ppermute | solution.py:381
  24.9 10.8 %collective-permute-start.13 = (bf16[192,768]{1,0:T(8,128)(2,1)S(1)}, bf16[192,768]{1,0:T(8,128)(2,1)S(1)}, u32[]{:S(2)}, u32[]{:S(2)}) collective-permute-start(bf16[192,768]{1,0:T(8,128)(2,1)S(1)} %pick.4), channel_id=1, source_target_pairs={{0,2},{2,4},{4,6},{7,5},{5,3},{3,1},{8,10},{10,12},{12,14},{15,13}... | collective-permute-start | bytes 884744 | tf_op jit(solution)/shard_map/ppermute | solution.py:381
  29.4 6.5 %collective-permute-start.16 = (bf16[128,768]{1,0:T(8,128)(2,1)S(1)}, bf16[128,768]{1,0:T(8,128)(2,1)S(1)}, u32[]{:S(2)}, u32[]{:S(2)}) collective-permute-start(bf16[128,768]{1,0:T(8,128)(2,1)S(1)} %pick.5), channel_id=1, source_target_pairs={{0,2},{2,4},{4,6},{7,5},{5,3},{3,1},{8,10},{10,12},{12,14},{15,13}... | collective-permute-start | bytes 589832 | tf_op jit(solution)/shard_map/ppermute | solution.py:381
  32.6 6.5 %collective-permute-start.18 = (bf16[128,768]{1,0:T(8,128)(2,1)S(1)}, bf16[128,768]{1,0:T(8,128)(2,1)S(1)}, u32[]{:S(2)}, u32[]{:S(2)}) collective-permute-start(bf16[128,768]{1,0:T(8,128)(2,1)S(1)} %join.12), channel_id=1, source_target_pairs={{2,6},{5,1},{10,14},{13,9},{18,22},{21,17},{26,30},{29,25}} | collective-permute-start | bytes 589832 | tf_op jit(solution)/shard_map/ppermute | solution.py:381
  36.0 5.2 %collective-permute-start.17 = (bf16[128,768]{1,0:T(8,128)(2,1)S(1)}, bf16[128,768]{1,0:T(8,128)(2,1)S(1)}, u32[]{:S(2)}, u32[]{:S(2)}) collective-permute-start(bf16[128,768]{1,0:T(8,128)(2,1)S(1)} %join.11.came), channel_id=1, source_target_pairs={{0,1},{1,0},{2,3},{3,2},{4,5},{5,4},{6,7},{7,6},{8,9},{9,8},{10,11... | collective-permute-start | bytes 589832 | tf_op jit(solution)/shard_map/ppermute | solution.py:376
  38.6 2.1 %collective-permute-start.15 = (f32[128,896]{1,0:T(8,128)S(1)}, f32[128,896]{1,0:T(8,128)S(1)}, u32[]{:S(2)}, u32[]{:S(2)}) collective-permute-start(f32[128,896]{1,0:T(8,128)S(1)} %get-tuple-element.37), channel_id=1, source_target_pairs={{0,1},{1,0},{2,3},{3,2},{4,5},{5,4},{6,7},{7,6},{8,9},{9,8},{10,11... | collective-permute-start | bytes 1376264 | tf_op jit(solution)/shard_map/ppermute | solution.py:376
  38.7 2.5 %collective-permute-start.14 = (f32[128,896]{1,0:T(8,128)S(1)}, f32[128,896]{1,0:T(8,128)S(1)}, u32[]{:S(2)}, u32[]{:S(2)}) collective-permute-start(f32[128,896]{1,0:T(8,128)S(1)} %get-tuple-element.38), channel_id=1, source_target_pairs={{0,1},{1,0},{2,3},{3,2},{4,5},{5,4},{6,7},{7,6},{8,9},{9,8},{10,11... | collective-permute-start | bytes 1376264 | tf_op jit(solution)/shard_map/ppermute | solution.py:376
  39.2 2.6 %collective-permute-start.19 = (bf16[128,768]{1,0:T(8,128)(2,1)S(1)}, bf16[128,768]{1,0:T(8,128)(2,1)S(1)}, u32[]{:S(2)}, u32[]{:S(2)}) collective-permute-start(bf16[128,768]{1,0:T(8,128)(2,1)S(1)} %join.13.refs_0_), channel_id=1, source_target_pairs={{0,1},{1,0},{2,3},{3,2},{4,5},{5,4},{6,7},{7,6},{8,9},{9,8},{10,11... | collective-permute-start | bytes 589832 | tf_op jit(solution)/shard_map/ppermute | solution.py:376

commit v6 on v5

--- a/solution.py
+++ b/solution.py
@@ -11,6 +11,7 @@
 score_scale = 0.15
 lanes = 128
 exponent_scale = score_scale * math.log2(math.e)
+pick_flops = 1 << 30
 own_flops = 1 << 31
 beside_flops = 1 << 28
 over_flops = 1 << 32
@@ -91,14 +92,18 @@
     return jax.ShapeDtypeStruct(x.shape, x.dtype)
 
 
-def join_kernel(after_n, *refs):
-    gather_rows(refs[after_n:-1], refs[-1])
-
-
-def join(parts, *after, flops=1 << 20):
-    rows = sum(part.shape[0] for part in parts)
+def join_kernel(after_n, spans, *refs):
+    out, start = refs[-1], 0
+    for (low, high), part in zip(spans, refs[after_n:-1]):
+        out[start : start + high - low, :] = part[low:high, :]
+        start += high - low
+
+
+def join(parts, *after, flops=1 << 20, spans=None):
+    spans = spans or [(0, part.shape[0]) for part in parts]
+    rows = sum(high - low for low, high in spans)
     return pl.pallas_call(
-        functools.partial(join_kernel, len(after)),
+        functools.partial(join_kernel, len(after), spans),
         out_shape=jax.ShapeDtypeStruct((rows, parts[0].shape[1]), parts[0].dtype),
         in_specs=[unread()] * len(after) + [vmem()] * len(parts),
         out_specs=vmem(),
@@ -108,6 +113,24 @@
     )(*after, *parts)
 
 
+def halve_kernel(whole, upper, lower):
+    upper[...] = whole[: upper.shape[0], :]
+    lower[...] = whole[upper.shape[0] :, :]
+
+
+def halve(whole):
+    half = jax.ShapeDtypeStruct((whole.shape[0] // 2, whole.shape[1]), whole.dtype)
+    return pl.pallas_call(
+        halve_kernel,
+        out_shape=[half, half],
+        in_specs=[vmem()],
+        out_specs=[vmem(), vmem()],
+        compiler_params=pltpu.CompilerParams(vmem_limit_bytes=vmem_limit),
+        cost_estimate=cost(),
+        name="halve",
+    )(whole)
+
+
 def pick_kernel(depth, own, came, after, out):
     level, core, _, _ = chip_place()
     forwards = ((core == 0) & (level == depth - 2)) | ((core == 1) & (level == 1))
@@ -121,14 +144,14 @@
         out[...] = own[...]
 
 
-def pick(depth, own, came, after):
+def pick(depth, own, came, after, flops=1 << 20):
     return pl.pallas_call(
         functools.partial(pick_kernel, depth),
         out_shape=like(own),
         in_specs=[vmem(), vmem(), unread()],
         out_specs=vmem(),
         compiler_params=pltpu.CompilerParams(vmem_limit_bytes=vmem_limit),
-        cost_estimate=cost(),
+        cost_estimate=cost(flops),
         name="pick",
     )(own, came, after)
 
@@ -249,7 +272,7 @@
     return ((core == 0) & (level >= step)) | ((core == 1) & (level < depth - step))
 
 
-def first_kernel(tile, depth, table_from, near, far, apart, over, *refs):
+def first_kernel(tile, depth, table_from, near, far, over, apart, *refs):
     table, keep, give, half_norms, arrivals, rows, scores = refs
     copies = []
     for index in range(arrivals.shape[0]):
@@ -415,11 +438,13 @@
     near = join([packed[0], swap(packed[0])])
     apart_near, over_near = along(near, apart), along(near, over)
     first = join(fetched)
+    slot_rows, far_rows = packed[0].shape[0], first.shape[0]
     apart_first = along(first, apart)
-    swapped = [swap(rows) for rows in fetched]
+    halves = halve(first)
+    swapped = [swap(half) for half in halves]
     second = join(swapped)
     apart_second = along(second, apart)
-    over_first = along(join(fetched + swapped[:1]), over)
+    over_first = along(join([first, second], spans=[(0, far_rows), (0, slot_rows)]), over)
     two_sums = [sums_shape, sums_shape]
     table, keep, give, half_norms = kernel(
         functools.partial(first_kernel, tile, depth),
@@ -427,8 +452,8 @@
         pltpu.with_memory_space_constraint(centroids, pltpu.HBM),
         packed[0],
         first,
+        over_near,
         apart_near,
-        over_near,
         scratch=[pltpu.SemaphoreType.DMA((member_count,)), *scratch(row_count + 2 * near.shape[0])],
         flops=own_flops,
         specs=[hbm()],
@@ -448,10 +473,10 @@
             flops=flops,
         )
 
-    beside_first = along(pick(depth, first, apart_first, keep), beside)
+    beside_first = along(pick(depth, first, apart_first, keep, pick_flops), beside)
     beside_second = along(pick(depth, second, apart_second, keep), beside)
     beside_near = along(pick(depth, near, apart_near, keep), beside)
-    over_second = along(join(swapped[1:]), over)
+    over_second = along(join([second], spans=[(slot_rows, far_rows)]), over)
     own_body = functools.partial(own_kernel, tile, depth)
     keep, give = add(own_body, keep, give, packed[0], first, apart_near, apart_first, apart_second)
     over_body = functools.partial(step_kernel, tile, depth, last)

time: 44.3 us -> 44.1 us (level)
  waiting for transfers between devices: 1.66 us -> 0.99 us
    ppermute x9, starting transfers between devices: 23.1 us -> 24.3 us  [along(): return lax.ppermute(x, 'member', up + down)]
    ppermute x8 -> x7, starting transfers between devices: 5.72 us -> 4.92 us  [swap(): return lax.ppermute(x, 'member', [(i, i ^ 1) for i in range(member_count)])]
    ppermute x8 -> x7, waiting for transfers between devices: 1.63 us -> 0.96 us  [swap(): return lax.ppermute(x, 'member', [(i, i ^ 1) for i in range(member_count)])]
  transfers between devices with their start and end apart: 20 -> 19, of which waited for: 3 -> 1; matrix products, arithmetic and copies ran while one was open for 0% -> 0% of each run, Pallas kernels for 12% -> 12%
where the time goes in v6:
time: 44.1 us; the launch traced here: 43.8 us
  starting transfers between devices  33.4 us (76%)
  Pallas kernels  8.88 us (20%)
  waiting for transfers between devices  0.99 us (2%)
  between operations  0.49 us (1%)
    ppermute x9, starting transfers between devices, along(): return lax.ppermute(x, 'member', up + down)  24.3 us
    pallas_call x7, Pallas kernels, kernel(): pl.pallas_call(body, out_shape=out_shape, in_specs=list(specs) + [vmem()]...  7.19 us
    ppermute x7, starting transfers between devices, swap(): return lax.ppermute(x, 'member', [(i, i ^ 1) for i in range(member_count)])  4.92 us
    ppermute x3, starting transfers between devices, handoff(): lax.ppermute(packed[k], 'group', [(i, i ^ k) for i in range(group_count)])  4.16 us
    pallas_call x1, Pallas kernels, pack(): pl.pallas_call(pack_kernel, out_shape=[jax.ShapeDtypeStruct((capacity, fe...  1.43 us
    ppermute x7, waiting for transfers between devices, swap(): return lax.ppermute(x, 'member', [(i, i ^ 1) for i in range(member_count)])  0.96 us
  transfers between devices with their start and end apart: 19, of which 1 were waited for; matrix products, arithmetic and copies ran while one was open for 0% of the time, Pallas kernels for 12%

profile of v6, /device:TPU:0, one launch (start us, length us, event | category | flops | bytes accessed | tf_op | source)
XLA Modules:
  0.0 43.8 jit_solution(1295331960742386573)
XLA Ops:
  0.0 1.4 %pack.1 = (bf16[64,768]{1,0:T(8,128)(2,1)S(1)}, bf16[64,768]{1,0:T(8,128)(2,1)S(1)}, bf16[64,768]{1,0:T(8,128)(2,1)S(1)}, bf16[64,768]{1,0:T(8,128)(2,1)S(1)}) custom-call(s32[1,256]{1,0:T(1,128)} %bitcast.1, bf16[256,768]{1,0:T(8,128)(2,1)} %points.1), custom_call_target="tpu_custom_call" | custom-call | flops 1048576 | tf_op jit(solution)/shard_map/pack/pallas_call | solution.py:190
  1.4 0.5 %collective-permute-start.3 = (bf16[64,768]{1,0:T(8,128)(2,1)S(1)}, bf16[64,768]{1,0:T(8,128)(2,1)S(1)}, u32[]{:S(2)}, u32[]{:S(2)}) collective-permute-start(bf16[64,768]{1,0:T(8,128)(2,1)S(1)} %get-tuple-element.23.refs_0_.near), channel_id=1, source_target_pairs={{0,1},{1,0},{2,3},{3,2},{4,5},{5,4},{6,7},{7,6},{8,9},{9,8},{10,11... | collective-permute-start | bytes 294920 | tf_op jit(solution)/shard_map/ppermute | solution.py:399
  2.0 3.5 %collective-permute-start = (bf16[64,768]{1,0:T(8,128)(2,1)S(1)}, bf16[64,768]{1,0:T(8,128)(2,1)S(1)}, u32[]{:S(2)}, u32[]{:S(2)}) collective-permute-start(bf16[64,768]{1,0:T(8,128)(2,1)S(1)} %get-tuple-element.24), channel_id=1, source_target_pairs={{0,24},{8,16},{16,8},{24,0},{1,25},{9,17},{17,9},{25,1},{2,26},{10... | collective-permute-start | bytes 294920 | tf_op jit(solution)/shard_map/ppermute | solution.py:435
  5.5 0.5 %collective-permute-start.1 = (bf16[64,768]{1,0:T(8,128)(2,1)S(1)}, bf16[64,768]{1,0:T(8,128)(2,1)S(1)}, u32[]{:S(2)}, u32[]{:S(2)}) collective-permute-start(bf16[64,768]{1,0:T(8,128)(2,1)S(1)} %get-tuple-element.25), channel_id=1, source_target_pairs={{0,16},{8,24},{16,0},{24,8},{1,17},{9,25},{17,1},{25,9},{2,18},{10... | collective-permute-start | bytes 294920 | tf_op jit(solution)/shard_map/ppermute | solution.py:435
  6.0 0.1 collective-permute-start.2
  6.1 0.0 collective-permute-done.3.refs_1_
  6.1 4.9 %collective-permute-start.5 = (bf16[128,768]{1,0:T(8,128)(2,1)S(1)}, bf16[128,768]{1,0:T(8,128)(2,1)S(1)}, u32[]{:S(2)}, u32[]{:S(2)}) collective-permute-start(bf16[128,768]{1,0:T(8,128)(2,1)S(1)} %join.8.own), channel_id=1, source_target_pairs={{0,4},{4,6},{7,3},{3,1},{8,12},{12,14},{15,11},{11,9},{16,20},{20,... | collective-permute-start | bytes 589832 | tf_op jit(solution)/shard_map/ppermute | solution.py:404
  11.1 0.7 %collective-permute-start.4 = (bf16[128,768]{1,0:T(8,128)(2,1)S(1)}, bf16[128,768]{1,0:T(8,128)(2,1)S(1)}, u32[]{:S(2)}, u32[]{:S(2)}) collective-permute-start(bf16[128,768]{1,0:T(8,128)(2,1)S(1)} %join.8.own), channel_id=1, source_target_pairs={{2,6},{5,1},{10,14},{13,9},{18,22},{21,17},{26,30},{29,25}} | collective-permute-start | bytes 589832 | tf_op jit(solution)/shard_map/ppermute | solution.py:404
  11.7 0.0 collective-permute-done.refs_0_
  11.7 0.0 collective-permute-done.1.refs_1_
  11.8 0.0 collective-permute-done.2.refs_2_
  11.8 0.1 collective-permute-start.7
  11.9 0.5 %collective-permute-start.8 = (bf16[96,768]{1,0:T(8,128)(2,1)S(1)}, bf16[96,768]{1,0:T(8,128)(2,1)S(1)}, u32[]{:S(2)}, u32[]{:S(2)}) collective-permute-start(bf16[96,768]{1,0:T(8,128)(2,1)S(1)} %get-tuple-element.32), channel_id=1, source_target_pairs={{0,1},{1,0},{2,3},{3,2},{4,5},{5,4},{6,7},{7,6},{8,9},{9,8},{10,11... | collective-permute-start | bytes 442376 | tf_op jit(solution)/shard_map/ppermute | solution.py:399
  12.4 4.0 %collective-permute-start.6 = (bf16[192,768]{1,0:T(8,128)(2,1)S(1)}, bf16[192,768]{1,0:T(8,128)(2,1)S(1)}, u32[]{:S(2)}, u32[]{:S(2)}) collective-permute-start(bf16[192,768]{1,0:T(8,128)(2,1)S(1)} %join.7.far.whole.refs_0_.own), channel_id=1, source_target_pairs={{0,4},{4,6},{7,3},{3,1},{8,12},{12,14},{15,11},{11,9},{16,20},{20,... | collective-permute-start | bytes 884744 | tf_op jit(solution)/shard_map/ppermute | solution.py:404
  16.4 0.0 collective-permute-done.7.refs_0_
  16.4 0.0 collective-permute-done.8.refs_1_
  16.4 3.5 %collective-permute-start.9 = (bf16[192,768]{1,0:T(8,128)(2,1)S(1)}, bf16[192,768]{1,0:T(8,128)(2,1)S(1)}, u32[]{:S(2)}, u32[]{:S(2)}) collective-permute-start(bf16[192,768]{1,0:T(8,128)(2,1)S(1)} %join.9.refs_1_.own.refs_0_), channel_id=1, source_target_pairs={{0,4},{4,6},{7,3},{3,1},{8,12},{12,14},{15,11},{11,9},{16,20},{20,... | collective-permute-start | bytes 884744 | tf_op jit(solution)/shard_map/ppermute | solution.py:404
  20.0 0.7 %collective-permute-start.10 = (bf16[256,768]{1,0:T(8,128)(2,1)S(1)}, bf16[256,768]{1,0:T(8,128)(2,1)S(1)}, u32[]{:S(2)}, u32[]{:S(2)}) collective-permute-start(bf16[256,768]{1,0:T(8,128)(2,1)S(1)} %join.10), channel_id=1, source_target_pairs={{2,6},{5,1},{10,14},{13,9},{18,22},{21,17},{26,30},{29,25}} | collective-permute-start | bytes 1179656 | tf_op jit(solution)/shard_map/ppermute | solution.py:404
  20.6 0.0 collective-permute-done.5.apart.apart_near.came
  20.7 0.0 collective-permute-done.4.over
  20.7 2.3 %first_kernel.1 = (bf16[2048,768]{1,0:T(8,128)(2,1)S(1)}, f32[256,896]{1,0:T(8,128)S(1)}, f32[256,896]{1,0:T(8,128)S(1)}, f32[2048,1]{1,0:T(8,128)S(1)}) custom-call(bf16[2048,768]{1,0:T(8,128)(2,1)} %table_from.1, bf16[64,768]{1,0:T(8,128)(2,1)S(1)} %get-tuple-element.23.refs_0_.near, bf16[192,768]{1,0:T(8,128)(2,1)S(1)} %join.7.far.whole.refs_0_.own, ...), custom_call_target="tpu_custom_call" | custom-call | flops 2147483648 | tf_op jit(solution)/shard_map/first_kernel/pallas_call | solution.py:415
  23.0 0.0 collective-permute-done.6.refs_0_.came
  23.0 1.9 %collective-permute-start.11 = (bf16[192,768]{1,0:T(8,128)(2,1)S(1)}, bf16[192,768]{1,0:T(8,128)(2,1)S(1)}, u32[]{:S(2)}, u32[]{:S(2)}) collective-permute-start(bf16[192,768]{1,0:T(8,128)(2,1)S(1)} %pick.3), channel_id=1, source_target_pairs={{0,2},{2,4},{4,6},{7,5},{5,3},{3,1},{8,10},{10,12},{12,14},{15,13}... | collective-permute-start | bytes 884744 | tf_op jit(solution)/shard_map/ppermute | solution.py:404
  25.0 0.0 collective-permute-done.9.refs_1_.came
  25.0 3.5 %collective-permute-start.12 = (bf16[192,768]{1,0:T(8,128)(2,1)S(1)}, bf16[192,768]{1,0:T(8,128)(2,1)S(1)}, u32[]{:S(2)}, u32[]{:S(2)}) collective-permute-start(bf16[192,768]{1,0:T(8,128)(2,1)S(1)} %pick.4), channel_id=1, source_target_pairs={{0,2},{2,4},{4,6},{7,5},{5,3},{3,1},{8,10},{10,12},{12,14},{15,13}... | collective-permute-start | bytes 884744 | tf_op jit(solution)/shard_map/ppermute | solution.py:404
  28.5 0.7 %collective-permute-start.17 = (bf16[128,768]{1,0:T(8,128)(2,1)S(1)}, bf16[128,768]{1,0:T(8,128)(2,1)S(1)}, u32[]{:S(2)}, u32[]{:S(2)}) collective-permute-start(bf16[128,768]{1,0:T(8,128)(2,1)S(1)} %join.12), channel_id=1, source_target_pairs={{2,6},{5,1},{10,14},{13,9},{18,22},{21,17},{26,30},{29,25}} | collective-permute-start | bytes 589832 | tf_op jit(solution)/shard_map/ppermute | solution.py:404
  29.2 4.6 %collective-permute-start.15 = (bf16[128,768]{1,0:T(8,128)(2,1)S(1)}, bf16[128,768]{1,0:T(8,128)(2,1)S(1)}, u32[]{:S(2)}, u32[]{:S(2)}) collective-permute-start(bf16[128,768]{1,0:T(8,128)(2,1)S(1)} %pick.5), channel_id=1, source_target_pairs={{0,2},{2,4},{4,6},{7,5},{5,3},{3,1},{8,10},{10,12},{12,14},{15,13}... | collective-permute-start | bytes 589832 | tf_op jit(solution)/shard_map/ppermute | solution.py:404
  33.8 1.9 %own_kernel.1 = (f32[256,896]{1,0:T(8,128)S(1)}, f32[256,896]{1,0:T(8,128)S(1)}) custom-call(bf16[2048,768]{1,0:T(8,128)(2,1)S(1)} %get-tuple-element.27.table, f32[2048,1]{1,0:T(8,128)S(1)} %get-tuple-element.28.half_norms, f32[256,896]{1,0:T(8,128)S(1)} %get-tuple-element.29.keep_in.after, ...), custom_call_target="tpu_custom_call", output_to_operand_aliasing={{0}: (2, {}), {1}: (3, {})} | custom-call | flops 268435456 | tf_op jit(solution)/shard_map/own_kernel/pallas_call | solution.py:415
  35.7 0.0 collective-permute-done.10.refs_0_
  35.7 0.2 step_kernel.3
  36.0 0.0 collective-permute-done.11.refs_0_
  36.0 0.2 step_kernel.4
  36.3 0.0 collective-permute-done.12.refs_0_
  36.3 0.2 step_kernel.5
  36.5 0.1 fusion
  36.6 1.4 %collective-permute-start.13 = (f32[128,896]{1,0:T(8,128)S(1)}, f32[128,896]{1,0:T(8,128)S(1)}, u32[]{:S(2)}, u32[]{:S(2)}) collective-permute-start(f32[128,896]{1,0:T(8,128)S(1)} %get-tuple-element.42), channel_id=1, source_target_pairs={{0,1},{1,0},{2,3},{3,2},{4,5},{5,4},{6,7},{7,6},{8,9},{9,8},{10,11... | collective-permute-start | bytes 1376264 | tf_op jit(solution)/shard_map/ppermute | solution.py:399
  38.0 0.1 collective-permute-start.14
  38.1 0.0 collective-permute-done.17.refs_1_
  38.1 0.5 %collective-permute-start.18 = (bf16[128,768]{1,0:T(8,128)(2,1)S(1)}, bf16[128,768]{1,0:T(8,128)(2,1)S(1)}, u32[]{:S(2)}, u32[]{:S(2)}) collective-permute-start(bf16[128,768]{1,0:T(8,128)(2,1)S(1)} %join.13.refs_0_), channel_id=1, source_target_pairs={{0,1},{1,0},{2,3},{3,2},{4,5},{5,4},{6,7},{7,6},{8,9},{9,8},{10,11... | collective-permute-start | bytes 589832 | tf_op jit(solution)/shard_map/ppermute | solution.py:399
  38.6 0.0 collective-permute-done.15.refs_1_
  38.6 1.8 %collective-permute-start.16 = (bf16[128,768]{1,0:T(8,128)(2,1)S(1)}, bf16[128,768]{1,0:T(8,128)(2,1)S(1)}, u32[]{:S(2)}, u32[]{:S(2)}) collective-permute-start(bf16[128,768]{1,0:T(8,128)(2,1)S(1)} %join.11.came), channel_id=1, source_target_pairs={{0,1},{1,0},{2,3},{3,2},{4,5},{5,4},{6,7},{7,6},{8,9},{9,8},{10,11... | collective-permute-start | bytes 589832 | tf_op jit(solution)/shard_map/ppermute | solution.py:399
  40.5 0.0 collective-permute-done.13.refs_0_
  40.5 0.0 collective-permute-done.14.refs_1_
  40.5 0.1 base_kernel.1.base
  40.6 0.0 collective-permute-done.18.refs_1_
  40.6 0.9 %collective-permute-done.16.passed = bf16[128,768]{1,0:T(8,128)(2,1)S(1)} collective-permute-done((bf16[128,768]{1,0:T(8,128)(2,1)S(1)}, bf16[128,768]{1,0:T(8,128)(2,1)S(1)}, u32[]{:S(2)}, u32[]{:S(2)}) %collective-permute-start.16) | collective-permute-done | bytes 196640 | tf_op jit(solution)/shard_map/ppermute | solution.py:399
  41.5 2.1 %refit_kernel.1 = bf16[256,768]{1,0:T(8,128)(2,1)} custom-call(bf16[2048,768]{1,0:T(8,128)(2,1)S(1)} %get-tuple-element.27.table, f32[2048,1]{1,0:T(8,128)S(1)} %get-tuple-element.28.half_norms, f32[256,896]{1,0:T(8,128)S(1)} %base_kernel.1.base, bf16[128,768]{1,0:T(8,128)(2,1)S(1)} %join.11.came, bf16[128,768]{1,0:T(8,128)(2,1)S(1)} %collective-permute-done.16.passed, ...), custom_call_target="tpu_custom_call" | custom-call | flops 268435456 | tf_op jit(solution)/shard_map/refit_kernel/pallas_call | solution.py:415
  (11 shorter events, 0.3 us)
Async XLA Ops:
  1.4 4.7 %collective-permute-start.3 = (bf16[64,768]{1,0:T(8,128)(2,1)S(1)}, bf16[64,768]{1,0:T(8,128)(2,1)S(1)}, u32[]{:S(2)}, u32[]{:S(2)}) collective-permute-start(bf16[64,768]{1,0:T(8,128)(2,1)S(1)} %get-tuple-element.23.refs_0_.near), channel_id=1, source_target_pairs={{0,1},{1,0},{2,3},{3,2},{4,5},{5,4},{6,7},{7,6},{8,9},{9,8},{10,11... | collective-permute-start | bytes 294920 | tf_op jit(solution)/shard_map/ppermute | solution.py:399
  2.0 9.8 %collective-permute-start = (bf16[64,768]{1,0:T(8,128)(2,1)S(1)}, bf16[64,768]{1,0:T(8,128)(2,1)S(1)}, u32[]{:S(2)}, u32[]{:S(2)}) collective-permute-start(bf16[64,768]{1,0:T(8,128)(2,1)S(1)} %get-tuple-element.24), channel_id=1, source_target_pairs={{0,24},{8,16},{16,8},{24,0},{1,25},{9,17},{17,9},{25,1},{2,26},{10... | collective-permute-start | bytes 294920 | tf_op jit(solution)/shard_map/ppermute | solution.py:435
  5.5 6.3 %collective-permute-start.1 = (bf16[64,768]{1,0:T(8,128)(2,1)S(1)}, bf16[64,768]{1,0:T(8,128)(2,1)S(1)}, u32[]{:S(2)}, u32[]{:S(2)}) collective-permute-start(bf16[64,768]{1,0:T(8,128)(2,1)S(1)} %get-tuple-element.25), channel_id=1, source_target_pairs={{0,16},{8,24},{16,0},{24,8},{1,17},{9,25},{17,1},{25,9},{2,18},{10... | collective-permute-start | bytes 294920 | tf_op jit(solution)/shard_map/ppermute | solution.py:435
  6.0 5.8 %collective-permute-start.2 = (bf16[64,768]{1,0:T(8,128)(2,1)S(1)}, bf16[64,768]{1,0:T(8,128)(2,1)S(1)}, u32[]{:S(2)}, u32[]{:S(2)}) collective-permute-start(bf16[64,768]{1,0:T(8,128)(2,1)S(1)} %get-tuple-element.26), channel_id=1, source_target_pairs={{0,8},{8,0},{16,24},{24,16},{1,9},{9,1},{17,25},{25,17},{2,10},{10... | collective-permute-start | bytes 294920 | tf_op jit(solution)/shard_map/ppermute | solution.py:435
  6.1 14.5 %collective-permute-start.5 = (bf16[128,768]{1,0:T(8,128)(2,1)S(1)}, bf16[128,768]{1,0:T(8,128)(2,1)S(1)}, u32[]{:S(2)}, u32[]{:S(2)}) collective-permute-start(bf16[128,768]{1,0:T(8,128)(2,1)S(1)} %join.8.own), channel_id=1, source_target_pairs={{0,4},{4,6},{7,3},{3,1},{8,12},{12,14},{15,11},{11,9},{16,20},{20,... | collective-permute-start | bytes 589832 | tf_op jit(solution)/shard_map/ppermute | solution.py:404
  11.1 9.6 %collective-permute-start.4 = (bf16[128,768]{1,0:T(8,128)(2,1)S(1)}, bf16[128,768]{1,0:T(8,128)(2,1)S(1)}, u32[]{:S(2)}, u32[]{:S(2)}) collective-permute-start(bf16[128,768]{1,0:T(8,128)(2,1)S(1)} %join.8.own), channel_id=1, source_target_pairs={{2,6},{5,1},{10,14},{13,9},{18,22},{21,17},{26,30},{29,25}} | collective-permute-start | bytes 589832 | tf_op jit(solution)/shard_map/ppermute | solution.py:404
  11.8 4.6 %collective-permute-start.7 = (bf16[96,768]{1,0:T(8,128)(2,1)S(1)}, bf16[96,768]{1,0:T(8,128)(2,1)S(1)}, u32[]{:S(2)}, u32[]{:S(2)}) collective-permute-start(bf16[96,768]{1,0:T(8,128)(2,1)S(1)} %get-tuple-element.31), channel_id=1, source_target_pairs={{0,1},{1,0},{2,3},{3,2},{4,5},{5,4},{6,7},{7,6},{8,9},{9,8},{10,11... | collective-permute-start | bytes 442376 | tf_op jit(solution)/shard_map/ppermute | solution.py:399
  11.9 4.5 %collective-permute-start.8 = (bf16[96,768]{1,0:T(8,128)(2,1)S(1)}, bf16[96,768]{1,0:T(8,128)(2,1)S(1)}, u32[]{:S(2)}, u32[]{:S(2)}) collective-permute-start(bf16[96,768]{1,0:T(8,128)(2,1)S(1)} %get-tuple-element.32), channel_id=1, source_target_pairs={{0,1},{1,0},{2,3},{3,2},{4,5},{5,4},{6,7},{7,6},{8,9},{9,8},{10,11... | collective-permute-start | bytes 442376 | tf_op jit(solution)/shard_map/ppermute | solution.py:399
  12.4 10.6 %collective-permute-start.6 = (bf16[192,768]{1,0:T(8,128)(2,1)S(1)}, bf16[192,768]{1,0:T(8,128)(2,1)S(1)}, u32[]{:S(2)}, u32[]{:S(2)}) collective-permute-start(bf16[192,768]{1,0:T(8,128)(2,1)S(1)} %join.7.far.whole.refs_0_.own), channel_id=1, source_target_pairs={{0,4},{4,6},{7,3},{3,1},{8,12},{12,14},{15,11},{11,9},{16,20},{20,... | collective-permute-start | bytes 884744 | tf_op jit(solution)/shard_map/ppermute | solution.py:404
  16.4 8.5 %collective-permute-start.9 = (bf16[192,768]{1,0:T(8,128)(2,1)S(1)}, bf16[192,768]{1,0:T(8,128)(2,1)S(1)}, u32[]{:S(2)}, u32[]{:S(2)}) collective-permute-start(bf16[192,768]{1,0:T(8,128)(2,1)S(1)} %join.9.refs_1_.own.refs_0_), channel_id=1, source_target_pairs={{0,4},{4,6},{7,3},{3,1},{8,12},{12,14},{15,11},{11,9},{16,20},{20,... | collective-permute-start | bytes 884744 | tf_op jit(solution)/shard_map/ppermute | solution.py:404
  20.0 15.8 %collective-permute-start.10 = (bf16[256,768]{1,0:T(8,128)(2,1)S(1)}, bf16[256,768]{1,0:T(8,128)(2,1)S(1)}, u32[]{:S(2)}, u32[]{:S(2)}) collective-permute-start(bf16[256,768]{1,0:T(8,128)(2,1)S(1)} %join.10), channel_id=1, source_target_pairs={{2,6},{5,1},{10,14},{13,9},{18,22},{21,17},{26,30},{29,25}} | collective-permute-start | bytes 1179656 | tf_op jit(solution)/shard_map/ppermute | solution.py:404
  23.0 13.0 %collective-permute-start.11 = (bf16[192,768]{1,0:T(8,128)(2,1)S(1)}, bf16[192,768]{1,0:T(8,128)(2,1)S(1)}, u32[]{:S(2)}, u32[]{:S(2)}) collective-permute-start(bf16[192,768]{1,0:T(8,128)(2,1)S(1)} %pick.3), channel_id=1, source_target_pairs={{0,2},{2,4},{4,6},{7,5},{5,3},{3,1},{8,10},{10,12},{12,14},{15,13}... | collective-permute-start | bytes 884744 | tf_op jit(solution)/shard_map/ppermute | solution.py:404
  25.0 11.2 %collective-permute-start.12 = (bf16[192,768]{1,0:T(8,128)(2,1)S(1)}, bf16[192,768]{1,0:T(8,128)(2,1)S(1)}, u32[]{:S(2)}, u32[]{:S(2)}) collective-permute-start(bf16[192,768]{1,0:T(8,128)(2,1)S(1)} %pick.4), channel_id=1, source_target_pairs={{0,2},{2,4},{4,6},{7,5},{5,3},{3,1},{8,10},{10,12},{12,14},{15,13}... | collective-permute-start | bytes 884744 | tf_op jit(solution)/shard_map/ppermute | solution.py:404
  28.5 9.6 %collective-permute-start.17 = (bf16[128,768]{1,0:T(8,128)(2,1)S(1)}, bf16[128,768]{1,0:T(8,128)(2,1)S(1)}, u32[]{:S(2)}, u32[]{:S(2)}) collective-permute-start(bf16[128,768]{1,0:T(8,128)(2,1)S(1)} %join.12), channel_id=1, source_target_pairs={{2,6},{5,1},{10,14},{13,9},{18,22},{21,17},{26,30},{29,25}} | collective-permute-start | bytes 589832 | tf_op jit(solution)/shard_map/ppermute | solution.py:404
  29.2 9.4 %collective-permute-start.15 = (bf16[128,768]{1,0:T(8,128)(2,1)S(1)}, bf16[128,768]{1,0:T(8,128)(2,1)S(1)}, u32[]{:S(2)}, u32[]{:S(2)}) collective-permute-start(bf16[128,768]{1,0:T(8,128)(2,1)S(1)} %pick.5), channel_id=1, source_target_pairs={{0,2},{2,4},{4,6},{7,5},{5,3},{3,1},{8,10},{10,12},{12,14},{15,13}... | collective-permute-start | bytes 589832 | tf_op jit(solution)/shard_map/ppermute | solution.py:404
  36.6 3.9 %collective-permute-start.13 = (f32[128,896]{1,0:T(8,128)S(1)}, f32[128,896]{1,0:T(8,128)S(1)}, u32[]{:S(2)}, u32[]{:S(2)}) collective-permute-start(f32[128,896]{1,0:T(8,128)S(1)} %get-tuple-element.42), channel_id=1, source_target_pairs={{0,1},{1,0},{2,3},{3,2},{4,5},{5,4},{6,7},{7,6},{8,9},{9,8},{10,11... | collective-permute-start | bytes 1376264 | tf_op jit(solution)/shard_map/ppermute | solution.py:399
  38.0 2.5 %collective-permute-start.14 = (f32[128,896]{1,0:T(8,128)S(1)}, f32[128,896]{1,0:T(8,128)S(1)}, u32[]{:S(2)}, u32[]{:S(2)}) collective-permute-start(f32[128,896]{1,0:T(8,128)S(1)} %get-tuple-element.41), channel_id=1, source_target_pairs={{0,1},{1,0},{2,3},{3,2},{4,5},{5,4},{6,7},{7,6},{8,9},{9,8},{10,11... | collective-permute-start | bytes 1376264 | tf_op jit(solution)/shard_map/ppermute | solution.py:399
  38.1 2.5 %collective-permute-start.18 = (bf16[128,768]{1,0:T(8,128)(2,1)S(1)}, bf16[128,768]{1,0:T(8,128)(2,1)S(1)}, u32[]{:S(2)}, u32[]{:S(2)}) collective-permute-start(bf16[128,768]{1,0:T(8,128)(2,1)S(1)} %join.13.refs_0_), channel_id=1, source_target_pairs={{0,1},{1,0},{2,3},{3,2},{4,5},{5,4},{6,7},{7,6},{8,9},{9,8},{10,11... | collective-permute-start | bytes 589832 | tf_op jit(solution)/shard_map/ppermute | solution.py:399
  38.6 2.9 %collective-permute-start.16 = (bf16[128,768]{1,0:T(8,128)(2,1)S(1)}, bf16[128,768]{1,0:T(8,128)(2,1)S(1)}, u32[]{:S(2)}, u32[]{:S(2)}) collective-permute-start(bf16[128,768]{1,0:T(8,128)(2,1)S(1)} %join.11.came), channel_id=1, source_target_pairs={{0,1},{1,0},{2,3},{3,2},{4,5},{5,4},{6,7},{7,6},{8,9},{9,8},{10,11... | collective-permute-start | bytes 589832 | tf_op jit(solution)/shard_map/ppermute | solution.py:399

commit v7 on v6

--- a/solution.py
+++ b/solution.py
@@ -295,7 +295,7 @@
         add_rows(table, half_norms, parts, rows, scores, ((mine, keep), (other, give)), tile)
 
 
-def own_kernel(tile, depth, table, half_norms, keep_in, give_in, near, far, apart_near, *refs):
+def own_kernel(tile, depth, table, half_norms, keep_in, give_in, near, far, over_near, *refs):
     came, (keep, give, rows, scores) = refs[:-4], refs[-4:]
     keep[...] = keep_in[...]
     give[...] = give_in[...]
@@ -312,7 +312,7 @@
 
     @pl.when(here & jnp.logical_not(end))
     def _():
-        add(near, far, apart_near, *came)
+        add(near, far, over_near, *came)
 
     @pl.when(jnp.logical_not(here))
     def _():
@@ -436,7 +436,7 @@
         for k in reversed(range(1, group_count))
     ]
     near = join([packed[0], swap(packed[0])])
-    apart_near, over_near = along(near, apart), along(near, over)
+    apart_near, over_near = along(near, apart[1:]), along(near, over + apart[:1])
     first = join(fetched)
     slot_rows, far_rows = packed[0].shape[0], first.shape[0]
     apart_first = along(first, apart)
@@ -475,10 +475,10 @@
 
     beside_first = along(pick(depth, first, apart_first, keep, pick_flops), beside)
     beside_second = along(pick(depth, second, apart_second, keep), beside)
-    beside_near = along(pick(depth, near, apart_near, keep), beside)
+    beside_near = along(pick(depth, near, over_near, keep), beside)
     over_second = along(join([second], spans=[(slot_rows, far_rows)]), over)
     own_body = functools.partial(own_kernel, tile, depth)
-    keep, give = add(own_body, keep, give, packed[0], first, apart_near, apart_first, apart_second)
+    keep, give = add(own_body, keep, give, packed[0], first, over_near, apart_first, apart_second)
     over_body = functools.partial(step_kernel, tile, depth, last)
     keep, give = add(over_body, keep, give, over_first)
     beside_body = functools.partial(step_kernel, tile, depth, 1)

time: 44.1 us -> 43.5 us (0.986)
  starting transfers between devices: 33.4 us -> 32.8 us
    ppermute x7, starting transfers between devices: 4.92 us -> 3.83 us  [swap(): return lax.ppermute(x, 'member', [(i, i ^ 1) for i in range(member_count)])]
    ppermute x9, starting transfers between devices: 24.3 us -> 24.8 us  [along(): return lax.ppermute(x, 'member', up + down)]
where the time goes in v7:
time: 43.5 us; the launch traced here: 43.2 us
  starting transfers between devices  32.8 us (75%)
  Pallas kernels  8.89 us (20%)
  waiting for transfers between devices  0.99 us (2%)
  between operations  0.49 us (1%)
    ppermute x9, starting transfers between devices, along(): return lax.ppermute(x, 'member', up + down)  24.8 us
    pallas_call x7, Pallas kernels, kernel(): pl.pallas_call(body, out_shape=out_shape, in_specs=list(specs) + [vmem()]...  7.2 us
    ppermute x3, starting transfers between devices, handoff(): lax.ppermute(packed[k], 'group', [(i, i ^ k) for i in range(group_count)])  4.16 us
    ppermute x7, starting transfers between devices, swap(): return lax.ppermute(x, 'member', [(i, i ^ 1) for i in range(member_count)])  3.83 us
    pallas_call x1, Pallas kernels, pack(): pl.pallas_call(pack_kernel, out_shape=[jax.ShapeDtypeStruct((capacity, fe...  1.43 us
    ppermute x7, waiting for transfers between devices, swap(): return lax.ppermute(x, 'member', [(i, i ^ 1) for i in range(member_count)])  0.96 us
  transfers between devices with their start and end apart: 19, of which 1 were waited for; matrix products, arithmetic and copies ran while one was open for 0% of the time, Pallas kernels for 12%

profile of v7, /device:TPU:0, one launch (start us, length us, event | category | flops | bytes accessed | tf_op | source)
XLA Modules:
  0.0 43.2 jit_solution(686601859450187536)
XLA Ops:
  0.0 1.4 %pack.1 = (bf16[64,768]{1,0:T(8,128)(2,1)S(1)}, bf16[64,768]{1,0:T(8,128)(2,1)S(1)}, bf16[64,768]{1,0:T(8,128)(2,1)S(1)}, bf16[64,768]{1,0:T(8,128)(2,1)S(1)}) custom-call(s32[1,256]{1,0:T(1,128)} %bitcast.1, bf16[256,768]{1,0:T(8,128)(2,1)} %points.1), custom_call_target="tpu_custom_call" | custom-call | flops 1048576 | tf_op jit(solution)/shard_map/pack/pallas_call | solution.py:190
  1.4 0.5 %collective-permute-start.3 = (bf16[64,768]{1,0:T(8,128)(2,1)S(1)}, bf16[64,768]{1,0:T(8,128)(2,1)S(1)}, u32[]{:S(2)}, u32[]{:S(2)}) collective-permute-start(bf16[64,768]{1,0:T(8,128)(2,1)S(1)} %get-tuple-element.23.refs_0_.near), channel_id=1, source_target_pairs={{0,1},{1,0},{2,3},{3,2},{4,5},{5,4},{6,7},{7,6},{8,9},{9,8},{10,11... | collective-permute-start | bytes 294920 | tf_op jit(solution)/shard_map/ppermute | solution.py:399
  2.0 3.5 %collective-permute-start = (bf16[64,768]{1,0:T(8,128)(2,1)S(1)}, bf16[64,768]{1,0:T(8,128)(2,1)S(1)}, u32[]{:S(2)}, u32[]{:S(2)}) collective-permute-start(bf16[64,768]{1,0:T(8,128)(2,1)S(1)} %get-tuple-element.24), channel_id=1, source_target_pairs={{0,24},{8,16},{16,8},{24,0},{1,25},{9,17},{17,9},{25,1},{2,26},{10... | collective-permute-start | bytes 294920 | tf_op jit(solution)/shard_map/ppermute | solution.py:435
  5.5 0.5 %collective-permute-start.1 = (bf16[64,768]{1,0:T(8,128)(2,1)S(1)}, bf16[64,768]{1,0:T(8,128)(2,1)S(1)}, u32[]{:S(2)}, u32[]{:S(2)}) collective-permute-start(bf16[64,768]{1,0:T(8,128)(2,1)S(1)} %get-tuple-element.25), channel_id=1, source_target_pairs={{0,16},{8,24},{16,0},{24,8},{1,17},{9,25},{17,1},{25,9},{2,18},{10... | collective-permute-start | bytes 294920 | tf_op jit(solution)/shard_map/ppermute | solution.py:435
  6.0 0.1 collective-permute-start.2
  6.1 0.0 collective-permute-done.3.refs_1_
  6.1 4.9 %collective-permute-start.4 = (bf16[128,768]{1,0:T(8,128)(2,1)S(1)}, bf16[128,768]{1,0:T(8,128)(2,1)S(1)}, u32[]{:S(2)}, u32[]{:S(2)}) collective-permute-start(bf16[128,768]{1,0:T(8,128)(2,1)S(1)} %join.8.own), channel_id=1, source_target_pairs={{2,6},{0,4},{5,1},{7,3},{10,14},{8,12},{13,9},{15,11},{18,22},{16,... | collective-permute-start | bytes 589832 | tf_op jit(solution)/shard_map/ppermute | solution.py:404
  11.1 0.7 %collective-permute-start.5 = (bf16[128,768]{1,0:T(8,128)(2,1)S(1)}, bf16[128,768]{1,0:T(8,128)(2,1)S(1)}, u32[]{:S(2)}, u32[]{:S(2)}) collective-permute-start(bf16[128,768]{1,0:T(8,128)(2,1)S(1)} %join.8.own), channel_id=1, source_target_pairs={{4,6},{3,1},{12,14},{11,9},{20,22},{19,17},{28,30},{27,25}} | collective-permute-start | bytes 589832 | tf_op jit(solution)/shard_map/ppermute | solution.py:404
  11.7 0.0 collective-permute-done.refs_0_
  11.7 0.0 collective-permute-done.1.refs_1_
  11.8 0.0 collective-permute-done.2.refs_2_
  11.8 0.1 collective-permute-start.7
  11.9 0.5 %collective-permute-start.8 = (bf16[96,768]{1,0:T(8,128)(2,1)S(1)}, bf16[96,768]{1,0:T(8,128)(2,1)S(1)}, u32[]{:S(2)}, u32[]{:S(2)}) collective-permute-start(bf16[96,768]{1,0:T(8,128)(2,1)S(1)} %get-tuple-element.32), channel_id=1, source_target_pairs={{0,1},{1,0},{2,3},{3,2},{4,5},{5,4},{6,7},{7,6},{8,9},{9,8},{10,11... | collective-permute-start | bytes 442376 | tf_op jit(solution)/shard_map/ppermute | solution.py:399
  12.4 4.1 %collective-permute-start.6 = (bf16[192,768]{1,0:T(8,128)(2,1)S(1)}, bf16[192,768]{1,0:T(8,128)(2,1)S(1)}, u32[]{:S(2)}, u32[]{:S(2)}) collective-permute-start(bf16[192,768]{1,0:T(8,128)(2,1)S(1)} %join.7.far.whole.refs_0_.own), channel_id=1, source_target_pairs={{0,4},{4,6},{7,3},{3,1},{8,12},{12,14},{15,11},{11,9},{16,20},{20,... | collective-permute-start | bytes 884744 | tf_op jit(solution)/shard_map/ppermute | solution.py:404
  16.5 0.0 collective-permute-done.7.refs_0_
  16.5 0.0 collective-permute-done.8.refs_1_
  16.6 3.3 %collective-permute-start.9 = (bf16[192,768]{1,0:T(8,128)(2,1)S(1)}, bf16[192,768]{1,0:T(8,128)(2,1)S(1)}, u32[]{:S(2)}, u32[]{:S(2)}) collective-permute-start(bf16[192,768]{1,0:T(8,128)(2,1)S(1)} %join.9.refs_1_.own.refs_0_), channel_id=1, source_target_pairs={{0,4},{4,6},{7,3},{3,1},{8,12},{12,14},{15,11},{11,9},{16,20},{20,... | collective-permute-start | bytes 884744 | tf_op jit(solution)/shard_map/ppermute | solution.py:404
  20.0 0.7 %collective-permute-start.10 = (bf16[256,768]{1,0:T(8,128)(2,1)S(1)}, bf16[256,768]{1,0:T(8,128)(2,1)S(1)}, u32[]{:S(2)}, u32[]{:S(2)}) collective-permute-start(bf16[256,768]{1,0:T(8,128)(2,1)S(1)} %join.10), channel_id=1, source_target_pairs={{2,6},{5,1},{10,14},{13,9},{18,22},{21,17},{26,30},{29,25}} | collective-permute-start | bytes 1179656 | tf_op jit(solution)/shard_map/ppermute | solution.py:404
  20.6 0.0 collective-permute-done.4.over.over_near.came
  20.7 0.0 collective-permute-done.5.apart
  20.7 2.3 %first_kernel.1 = (bf16[2048,768]{1,0:T(8,128)(2,1)S(1)}, f32[256,896]{1,0:T(8,128)S(1)}, f32[256,896]{1,0:T(8,128)S(1)}, f32[2048,1]{1,0:T(8,128)S(1)}) custom-call(bf16[2048,768]{1,0:T(8,128)(2,1)} %table_from.1, bf16[64,768]{1,0:T(8,128)(2,1)S(1)} %get-tuple-element.23.refs_0_.near, bf16[192,768]{1,0:T(8,128)(2,1)S(1)} %join.7.far.whole.refs_0_.own, ...), custom_call_target="tpu_custom_call" | custom-call | flops 2147483648 | tf_op jit(solution)/shard_map/first_kernel/pallas_call | solution.py:415
  23.0 0.0 collective-permute-done.6.refs_0_.came
  23.0 1.9 %collective-permute-start.11 = (bf16[192,768]{1,0:T(8,128)(2,1)S(1)}, bf16[192,768]{1,0:T(8,128)(2,1)S(1)}, u32[]{:S(2)}, u32[]{:S(2)}) collective-permute-start(bf16[192,768]{1,0:T(8,128)(2,1)S(1)} %pick.3), channel_id=1, source_target_pairs={{0,2},{2,4},{4,6},{7,5},{5,3},{3,1},{8,10},{10,12},{12,14},{15,13}... | collective-permute-start | bytes 884744 | tf_op jit(solution)/shard_map/ppermute | solution.py:404
  25.0 0.0 collective-permute-done.9.refs_1_.came
  25.0 3.6 %collective-permute-start.12 = (bf16[192,768]{1,0:T(8,128)(2,1)S(1)}, bf16[192,768]{1,0:T(8,128)(2,1)S(1)}, u32[]{:S(2)}, u32[]{:S(2)}) collective-permute-start(bf16[192,768]{1,0:T(8,128)(2,1)S(1)} %pick.4), channel_id=1, source_target_pairs={{0,2},{2,4},{4,6},{7,5},{5,3},{3,1},{8,10},{10,12},{12,14},{15,13}... | collective-permute-start | bytes 884744 | tf_op jit(solution)/shard_map/ppermute | solution.py:404
  28.7 0.7 %collective-permute-start.17 = (bf16[128,768]{1,0:T(8,128)(2,1)S(1)}, bf16[128,768]{1,0:T(8,128)(2,1)S(1)}, u32[]{:S(2)}, u32[]{:S(2)}) collective-permute-start(bf16[128,768]{1,0:T(8,128)(2,1)S(1)} %join.12), channel_id=1, source_target_pairs={{2,6},{5,1},{10,14},{13,9},{18,22},{21,17},{26,30},{29,25}} | collective-permute-start | bytes 589832 | tf_op jit(solution)/shard_map/ppermute | solution.py:404
  29.4 4.9 %collective-permute-start.15 = (bf16[128,768]{1,0:T(8,128)(2,1)S(1)}, bf16[128,768]{1,0:T(8,128)(2,1)S(1)}, u32[]{:S(2)}, u32[]{:S(2)}) collective-permute-start(bf16[128,768]{1,0:T(8,128)(2,1)S(1)} %pick.5), channel_id=1, source_target_pairs={{0,2},{2,4},{4,6},{7,5},{5,3},{3,1},{8,10},{10,12},{12,14},{15,13}... | collective-permute-start | bytes 589832 | tf_op jit(solution)/shard_map/ppermute | solution.py:404
  34.3 1.9 %own_kernel.1 = (f32[256,896]{1,0:T(8,128)S(1)}, f32[256,896]{1,0:T(8,128)S(1)}) custom-call(bf16[2048,768]{1,0:T(8,128)(2,1)S(1)} %get-tuple-element.27.table, f32[2048,1]{1,0:T(8,128)S(1)} %get-tuple-element.28.half_norms, f32[256,896]{1,0:T(8,128)S(1)} %get-tuple-element.29.keep_in.after, ...), custom_call_target="tpu_custom_call", output_to_operand_aliasing={{0}: (2, {}), {1}: (3, {})} | custom-call | flops 268435456 | tf_op jit(solution)/shard_map/own_kernel/pallas_call | solution.py:415
  36.2 0.0 collective-permute-done.10.refs_0_
  36.2 0.2 step_kernel.3
  36.5 0.0 collective-permute-done.11.refs_0_
  36.5 0.2 step_kernel.4
  36.7 0.0 collective-permute-done.12.refs_0_
  36.7 0.2 step_kernel.5
  37.0 0.1 fusion
  37.1 0.3 collective-permute-start.13
  37.4 0.2 collective-permute-start.14
  37.6 0.0 collective-permute-done.17.refs_1_
  37.7 0.3 collective-permute-start.18
  38.0 0.0 collective-permute-done.15.refs_1_
  38.0 1.8 %collective-permute-start.16 = (bf16[128,768]{1,0:T(8,128)(2,1)S(1)}, bf16[128,768]{1,0:T(8,128)(2,1)S(1)}, u32[]{:S(2)}, u32[]{:S(2)}) collective-permute-start(bf16[128,768]{1,0:T(8,128)(2,1)S(1)} %join.11.came), channel_id=1, source_target_pairs={{0,1},{1,0},{2,3},{3,2},{4,5},{5,4},{6,7},{7,6},{8,9},{9,8},{10,11... | collective-permute-start | bytes 589832 | tf_op jit(solution)/shard_map/ppermute | solution.py:399
  39.8 0.0 collective-permute-done.13.refs_0_
  39.8 0.0 collective-permute-done.14.refs_1_
  39.8 0.1 base_kernel.1.base
  40.0 0.0 collective-permute-done.18.refs_1_
  40.0 0.9 %collective-permute-done.16.passed = bf16[128,768]{1,0:T(8,128)(2,1)S(1)} collective-permute-done((bf16[128,768]{1,0:T(8,128)(2,1)S(1)}, bf16[128,768]{1,0:T(8,128)(2,1)S(1)}, u32[]{:S(2)}, u32[]{:S(2)}) %collective-permute-start.16) | collective-permute-done | bytes 196640 | tf_op jit(solution)/shard_map/ppermute | solution.py:399
  40.9 2.1 %refit_kernel.1 = bf16[256,768]{1,0:T(8,128)(2,1)} custom-call(bf16[2048,768]{1,0:T(8,128)(2,1)S(1)} %get-tuple-element.27.table, f32[2048,1]{1,0:T(8,128)S(1)} %get-tuple-element.28.half_norms, f32[256,896]{1,0:T(8,128)S(1)} %base_kernel.1.base, bf16[128,768]{1,0:T(8,128)(2,1)S(1)} %join.11.came, bf16[128,768]{1,0:T(8,128)(2,1)S(1)} %collective-permute-done.16.passed, ...), custom_call_target="tpu_custom_call" | custom-call | flops 268435456 | tf_op jit(solution)/shard_map/refit_kernel/pallas_call | solution.py:415
  (11 shorter events, 0.3 us)
Async XLA Ops:
  1.4 4.7 %collective-permute-start.3 = (bf16[64,768]{1,0:T(8,128)(2,1)S(1)}, bf16[64,768]{1,0:T(8,128)(2,1)S(1)}, u32[]{:S(2)}, u32[]{:S(2)}) collective-permute-start(bf16[64,768]{1,0:T(8,128)(2,1)S(1)} %get-tuple-element.23.refs_0_.near), channel_id=1, source_target_pairs={{0,1},{1,0},{2,3},{3,2},{4,5},{5,4},{6,7},{7,6},{8,9},{9,8},{10,11... | collective-permute-start | bytes 294920 | tf_op jit(solution)/shard_map/ppermute | solution.py:399
  2.0 9.8 %collective-permute-start = (bf16[64,768]{1,0:T(8,128)(2,1)S(1)}, bf16[64,768]{1,0:T(8,128)(2,1)S(1)}, u32[]{:S(2)}, u32[]{:S(2)}) collective-permute-start(bf16[64,768]{1,0:T(8,128)(2,1)S(1)} %get-tuple-element.24), channel_id=1, source_target_pairs={{0,24},{8,16},{16,8},{24,0},{1,25},{9,17},{17,9},{25,1},{2,26},{10... | collective-permute-start | bytes 294920 | tf_op jit(solution)/shard_map/ppermute | solution.py:435
  5.5 6.3 %collective-permute-start.1 = (bf16[64,768]{1,0:T(8,128)(2,1)S(1)}, bf16[64,768]{1,0:T(8,128)(2,1)S(1)}, u32[]{:S(2)}, u32[]{:S(2)}) collective-permute-start(bf16[64,768]{1,0:T(8,128)(2,1)S(1)} %get-tuple-element.25), channel_id=1, source_target_pairs={{0,16},{8,24},{16,0},{24,8},{1,17},{9,25},{17,1},{25,9},{2,18},{10... | collective-permute-start | bytes 294920 | tf_op jit(solution)/shard_map/ppermute | solution.py:435
  6.0 5.8 %collective-permute-start.2 = (bf16[64,768]{1,0:T(8,128)(2,1)S(1)}, bf16[64,768]{1,0:T(8,128)(2,1)S(1)}, u32[]{:S(2)}, u32[]{:S(2)}) collective-permute-start(bf16[64,768]{1,0:T(8,128)(2,1)S(1)} %get-tuple-element.26), channel_id=1, source_target_pairs={{0,8},{8,0},{16,24},{24,16},{1,9},{9,1},{17,25},{25,17},{2,10},{10... | collective-permute-start | bytes 294920 | tf_op jit(solution)/shard_map/ppermute | solution.py:435
  6.1 14.5 %collective-permute-start.4 = (bf16[128,768]{1,0:T(8,128)(2,1)S(1)}, bf16[128,768]{1,0:T(8,128)(2,1)S(1)}, u32[]{:S(2)}, u32[]{:S(2)}) collective-permute-start(bf16[128,768]{1,0:T(8,128)(2,1)S(1)} %join.8.own), channel_id=1, source_target_pairs={{2,6},{0,4},{5,1},{7,3},{10,14},{8,12},{13,9},{15,11},{18,22},{16,... | collective-permute-start | bytes 589832 | tf_op jit(solution)/shard_map/ppermute | solution.py:404
  11.1 9.6 %collective-permute-start.5 = (bf16[128,768]{1,0:T(8,128)(2,1)S(1)}, bf16[128,768]{1,0:T(8,128)(2,1)S(1)}, u32[]{:S(2)}, u32[]{:S(2)}) collective-permute-start(bf16[128,768]{1,0:T(8,128)(2,1)S(1)} %join.8.own), channel_id=1, source_target_pairs={{4,6},{3,1},{12,14},{11,9},{20,22},{19,17},{28,30},{27,25}} | collective-permute-start | bytes 589832 | tf_op jit(solution)/shard_map/ppermute | solution.py:404
  11.8 4.7 %collective-permute-start.7 = (bf16[96,768]{1,0:T(8,128)(2,1)S(1)}, bf16[96,768]{1,0:T(8,128)(2,1)S(1)}, u32[]{:S(2)}, u32[]{:S(2)}) collective-permute-start(bf16[96,768]{1,0:T(8,128)(2,1)S(1)} %get-tuple-element.31), channel_id=1, source_target_pairs={{0,1},{1,0},{2,3},{3,2},{4,5},{5,4},{6,7},{7,6},{8,9},{9,8},{10,11... | collective-permute-start | bytes 442376 | tf_op jit(solution)/shard_map/ppermute | solution.py:399
  11.9 4.6 %collective-permute-start.8 = (bf16[96,768]{1,0:T(8,128)(2,1)S(1)}, bf16[96,768]{1,0:T(8,128)(2,1)S(1)}, u32[]{:S(2)}, u32[]{:S(2)}) collective-permute-start(bf16[96,768]{1,0:T(8,128)(2,1)S(1)} %get-tuple-element.32), channel_id=1, source_target_pairs={{0,1},{1,0},{2,3},{3,2},{4,5},{5,4},{6,7},{7,6},{8,9},{9,8},{10,11... | collective-permute-start | bytes 442376 | tf_op jit(solution)/shard_map/ppermute | solution.py:399
  12.4 10.6 %collective-permute-start.6 = (bf16[192,768]{1,0:T(8,128)(2,1)S(1)}, bf16[192,768]{1,0:T(8,128)(2,1)S(1)}, u32[]{:S(2)}, u32[]{:S(2)}) collective-permute-start(bf16[192,768]{1,0:T(8,128)(2,1)S(1)} %join.7.far.whole.refs_0_.own), channel_id=1, source_target_pairs={{0,4},{4,6},{7,3},{3,1},{8,12},{12,14},{15,11},{11,9},{16,20},{20,... | collective-permute-start | bytes 884744 | tf_op jit(solution)/shard_map/ppermute | solution.py:404
  16.6 8.4 %collective-permute-start.9 = (bf16[192,768]{1,0:T(8,128)(2,1)S(1)}, bf16[192,768]{1,0:T(8,128)(2,1)S(1)}, u32[]{:S(2)}, u32[]{:S(2)}) collective-permute-start(bf16[192,768]{1,0:T(8,128)(2,1)S(1)} %join.9.refs_1_.own.refs_0_), channel_id=1, source_target_pairs={{0,4},{4,6},{7,3},{3,1},{8,12},{12,14},{15,11},{11,9},{16,20},{20,... | collective-permute-start | bytes 884744 | tf_op jit(solution)/shard_map/ppermute | solution.py:404
  20.0 16.3 %collective-permute-start.10 = (bf16[256,768]{1,0:T(8,128)(2,1)S(1)}, bf16[256,768]{1,0:T(8,128)(2,1)S(1)}, u32[]{:S(2)}, u32[]{:S(2)}) collective-permute-start(bf16[256,768]{1,0:T(8,128)(2,1)S(1)} %join.10), channel_id=1, source_target_pairs={{2,6},{5,1},{10,14},{13,9},{18,22},{21,17},{26,30},{29,25}} | collective-permute-start | bytes 1179656 | tf_op jit(solution)/shard_map/ppermute | solution.py:404
  23.0 13.4 %collective-permute-start.11 = (bf16[192,768]{1,0:T(8,128)(2,1)S(1)}, bf16[192,768]{1,0:T(8,128)(2,1)S(1)}, u32[]{:S(2)}, u32[]{:S(2)}) collective-permute-start(bf16[192,768]{1,0:T(8,128)(2,1)S(1)} %pick.3), channel_id=1, source_target_pairs={{0,2},{2,4},{4,6},{7,5},{5,3},{3,1},{8,10},{10,12},{12,14},{15,13}... | collective-permute-start | bytes 884744 | tf_op jit(solution)/shard_map/ppermute | solution.py:404
  25.0 11.7 %collective-permute-start.12 = (bf16[192,768]{1,0:T(8,128)(2,1)S(1)}, bf16[192,768]{1,0:T(8,128)(2,1)S(1)}, u32[]{:S(2)}, u32[]{:S(2)}) collective-permute-start(bf16[192,768]{1,0:T(8,128)(2,1)S(1)} %pick.4), channel_id=1, source_target_pairs={{0,2},{2,4},{4,6},{7,5},{5,3},{3,1},{8,10},{10,12},{12,14},{15,13}... | collective-permute-start | bytes 884744 | tf_op jit(solution)/shard_map/ppermute | solution.py:404
  28.7 9.0 %collective-permute-start.17 = (bf16[128,768]{1,0:T(8,128)(2,1)S(1)}, bf16[128,768]{1,0:T(8,128)(2,1)S(1)}, u32[]{:S(2)}, u32[]{:S(2)}) collective-permute-start(bf16[128,768]{1,0:T(8,128)(2,1)S(1)} %join.12), channel_id=1, source_target_pairs={{2,6},{5,1},{10,14},{13,9},{18,22},{21,17},{26,30},{29,25}} | collective-permute-start | bytes 589832 | tf_op jit(solution)/shard_map/ppermute | solution.py:404
  29.4 8.6 %collective-permute-start.15 = (bf16[128,768]{1,0:T(8,128)(2,1)S(1)}, bf16[128,768]{1,0:T(8,128)(2,1)S(1)}, u32[]{:S(2)}, u32[]{:S(2)}) collective-permute-start(bf16[128,768]{1,0:T(8,128)(2,1)S(1)} %pick.5), channel_id=1, source_target_pairs={{0,2},{2,4},{4,6},{7,5},{5,3},{3,1},{8,10},{10,12},{12,14},{15,13}... | collective-permute-start | bytes 589832 | tf_op jit(solution)/shard_map/ppermute | solution.py:404
  37.1 2.8 %collective-permute-start.13 = (f32[128,896]{1,0:T(8,128)S(1)}, f32[128,896]{1,0:T(8,128)S(1)}, u32[]{:S(2)}, u32[]{:S(2)}) collective-permute-start(f32[128,896]{1,0:T(8,128)S(1)} %get-tuple-element.42), channel_id=1, source_target_pairs={{0,1},{1,0},{2,3},{3,2},{4,5},{5,4},{6,7},{7,6},{8,9},{9,8},{10,11... | collective-permute-start | bytes 1376264 | tf_op jit(solution)/shard_map/ppermute | solution.py:399
  37.4 2.5 %collective-permute-start.14 = (f32[128,896]{1,0:T(8,128)S(1)}, f32[128,896]{1,0:T(8,128)S(1)}, u32[]{:S(2)}, u32[]{:S(2)}) collective-permute-start(f32[128,896]{1,0:T(8,128)S(1)} %get-tuple-element.41), channel_id=1, source_target_pairs={{0,1},{1,0},{2,3},{3,2},{4,5},{5,4},{6,7},{7,6},{8,9},{9,8},{10,11... | collective-permute-start | bytes 1376264 | tf_op jit(solution)/shard_map/ppermute | solution.py:399
  37.7 2.3 %collective-permute-start.18 = (bf16[128,768]{1,0:T(8,128)(2,1)S(1)}, bf16[128,768]{1,0:T(8,128)(2,1)S(1)}, u32[]{:S(2)}, u32[]{:S(2)}) collective-permute-start(bf16[128,768]{1,0:T(8,128)(2,1)S(1)} %join.13.refs_0_), channel_id=1, source_target_pairs={{0,1},{1,0},{2,3},{3,2},{4,5},{5,4},{6,7},{7,6},{8,9},{9,8},{10,11... | collective-permute-start | bytes 589832 | tf_op jit(solution)/shard_map/ppermute | solution.py:399
  38.0 2.9 %collective-permute-start.16 = (bf16[128,768]{1,0:T(8,128)(2,1)S(1)}, bf16[128,768]{1,0:T(8,128)(2,1)S(1)}, u32[]{:S(2)}, u32[]{:S(2)}) collective-permute-start(bf16[128,768]{1,0:T(8,128)(2,1)S(1)} %join.11.came), channel_id=1, source_target_pairs={{0,1},{1,0},{2,3},{3,2},{4,5},{5,4},{6,7},{7,6},{8,9},{9,8},{10,11... | collective-permute-start | bytes 589832 | tf_op jit(solution)/shard_map/ppermute | solution.py:399

commit v8 on v7

--- a/solution.py
+++ b/solution.py
@@ -354,21 +354,26 @@
     feature_dim = table.shape[1]
     mine = chip_place()[2]
     end, here = end_chip(depth), came_to(1, depth)
+    used = came.shape[0] + over_came.shape[0]
 
     @pl.when(end & here)
     def _():
         gather_rows((came, over_came), rows)
+        rows[used:, :] = jnp.zeros_like(rows[used:, :])
 
     @pl.when(end & jnp.logical_not(here))
     def _():
         gather_rows((passed, over_passed), rows)
+        rows[used:, :] = jnp.zeros_like(rows[used:, :])
 
     @pl.when(jnp.logical_not(end))
     def _():
         gather_rows((came, passed), rows)
 
     all_rows = rows[...]
-    terms = softmax_terms(table, half_norms, all_rows, scores, tile)
+    top, inverse = softmax_terms(table, half_norms, all_rows, scores, tile)
+    lane = lax.broadcasted_iota(jnp.int32, inverse.shape, 1)
+    terms = top, jnp.where(jnp.logical_not(end) | (lane < used), inverse, 0.0)
     half = tile // sent.shape[0]
     copies = []
     for index in range(sent.shape[0]):
@@ -444,7 +449,7 @@
     swapped = [swap(half) for half in halves]
     second = join(swapped)
     apart_second = along(second, apart)
-    over_first = along(join([first, second], spans=[(0, far_rows), (0, slot_rows)]), over)
+    over_first = along(join([first, second], spans=[(0, far_rows), (0, 2 * slot_rows)]), over)
     two_sums = [sums_shape, sums_shape]
     table, keep, give, half_norms = kernel(
         functools.partial(first_kernel, tile, depth),
@@ -476,7 +481,7 @@
     beside_first = along(pick(depth, first, apart_first, keep, pick_flops), beside)
     beside_second = along(pick(depth, second, apart_second, keep), beside)
     beside_near = along(pick(depth, near, over_near, keep), beside)
-    over_second = along(join([second], spans=[(slot_rows, far_rows)]), over)
+    over_second = along(join([second], spans=[(2 * slot_rows, far_rows)]), over)
     own_body = functools.partial(own_kernel, tile, depth)
     keep, give = add(own_body, keep, give, packed[0], first, over_near, apart_first, apart_second)
     over_body = functools.partial(step_kernel, tile, depth, last)

time: 43.5 us -> 44.1 us (1.014)
  waiting for transfers between devices: 0.99 us -> 1.58 us
    ppermute x7, starting transfers between devices: 3.83 us -> 4.52 us  [swap(): return lax.ppermute(x, 'member', [(i, i ^ 1) for i in range(member_count)])]
    ppermute x9, starting transfers between devices: 24.8 us -> 24.2 us  [along(): return lax.ppermute(x, 'member', up + down)]
    ppermute x7, waiting for transfers between devices: 0.96 us -> 1.55 us  [swap(): return lax.ppermute(x, 'member', [(i, i ^ 1) for i in range(member_count)])]
  transfers between devices with their start and end apart: 19 -> 19, of which waited for: 1 -> 2; matrix products, arithmetic and copies ran while one was open for 0% -> 0% of each run, Pallas kernels for 12% -> 12%
where the time goes in v8:
time: 44.1 us; the launch traced here: 43.8 us
  starting transfers between devices  32.8 us (74%)
  Pallas kernels  8.87 us (20%)
  waiting for transfers between devices  1.58 us (4%)
  between operations  0.48 us (1%)
    ppermute x9, starting transfers between devices, along(): return lax.ppermute(x, 'member', up + down)  24.2 us
    pallas_call x7, Pallas kernels, kernel(): pl.pallas_call(body, out_shape=out_shape, in_specs=list(specs) + [vmem()]...  7.18 us
    ppermute x7, starting transfers between devices, swap(): return lax.ppermute(x, 'member', [(i, i ^ 1) for i in range(member_count)])  4.52 us
    ppermute x3, starting transfers between devices, handoff(): lax.ppermute(packed[k], 'group', [(i, i ^ k) for i in range(group_count)])  4.16 us
    ppermute x7, waiting for transfers between devices, swap(): return lax.ppermute(x, 'member', [(i, i ^ 1) for i in range(member_count)])  1.55 us
    pallas_call x1, Pallas kernels, pack(): pl.pallas_call(pack_kernel, out_shape=[jax.ShapeDtypeStruct((capacity, fe...  1.43 us
  transfers between devices with their start and end apart: 19, of which 2 were waited for; matrix products, arithmetic and copies ran while one was open for 0% of the time, Pallas kernels for 12%

profile of v8, /device:TPU:0, one launch (start us, length us, event | category | flops | bytes accessed | tf_op | source)
XLA Modules:
  0.0 43.8 jit_solution(8574786551898959856)
XLA Ops:
  0.0 1.4 %pack.1 = (bf16[64,768]{1,0:T(8,128)(2,1)S(1)}, bf16[64,768]{1,0:T(8,128)(2,1)S(1)}, bf16[64,768]{1,0:T(8,128)(2,1)S(1)}, bf16[64,768]{1,0:T(8,128)(2,1)S(1)}) custom-call(s32[1,256]{1,0:T(1,128)} %bitcast.1, bf16[256,768]{1,0:T(8,128)(2,1)} %points.1), custom_call_target="tpu_custom_call" | custom-call | flops 1048576 | tf_op jit(solution)/shard_map/pack/pallas_call | solution.py:190
  1.4 0.5 %collective-permute-start.3 = (bf16[64,768]{1,0:T(8,128)(2,1)S(1)}, bf16[64,768]{1,0:T(8,128)(2,1)S(1)}, u32[]{:S(2)}, u32[]{:S(2)}) collective-permute-start(bf16[64,768]{1,0:T(8,128)(2,1)S(1)} %get-tuple-element.23.refs_0_.near), channel_id=1, source_target_pairs={{0,1},{1,0},{2,3},{3,2},{4,5},{5,4},{6,7},{7,6},{8,9},{9,8},{10,11... | collective-permute-start | bytes 294920 | tf_op jit(solution)/shard_map/ppermute | solution.py:404
  2.0 3.5 %collective-permute-start = (bf16[64,768]{1,0:T(8,128)(2,1)S(1)}, bf16[64,768]{1,0:T(8,128)(2,1)S(1)}, u32[]{:S(2)}, u32[]{:S(2)}) collective-permute-start(bf16[64,768]{1,0:T(8,128)(2,1)S(1)} %get-tuple-element.24), channel_id=1, source_target_pairs={{0,24},{8,16},{16,8},{24,0},{1,25},{9,17},{17,9},{25,1},{2,26},{10... | collective-permute-start | bytes 294920 | tf_op jit(solution)/shard_map/ppermute | solution.py:440
  5.5 0.5 %collective-permute-start.1 = (bf16[64,768]{1,0:T(8,128)(2,1)S(1)}, bf16[64,768]{1,0:T(8,128)(2,1)S(1)}, u32[]{:S(2)}, u32[]{:S(2)}) collective-permute-start(bf16[64,768]{1,0:T(8,128)(2,1)S(1)} %get-tuple-element.25), channel_id=1, source_target_pairs={{0,16},{8,24},{16,0},{24,8},{1,17},{9,25},{17,1},{25,9},{2,18},{10... | collective-permute-start | bytes 294920 | tf_op jit(solution)/shard_map/ppermute | solution.py:440
  6.0 0.1 collective-permute-start.2
  6.1 0.0 collective-permute-done.3.refs_1_
  6.1 4.9 %collective-permute-start.4 = (bf16[128,768]{1,0:T(8,128)(2,1)S(1)}, bf16[128,768]{1,0:T(8,128)(2,1)S(1)}, u32[]{:S(2)}, u32[]{:S(2)}) collective-permute-start(bf16[128,768]{1,0:T(8,128)(2,1)S(1)} %join.8.own), channel_id=1, source_target_pairs={{2,6},{0,4},{5,1},{7,3},{10,14},{8,12},{13,9},{15,11},{18,22},{16,... | collective-permute-start | bytes 589832 | tf_op jit(solution)/shard_map/ppermute | solution.py:409
  11.1 0.7 %collective-permute-start.5 = (bf16[128,768]{1,0:T(8,128)(2,1)S(1)}, bf16[128,768]{1,0:T(8,128)(2,1)S(1)}, u32[]{:S(2)}, u32[]{:S(2)}) collective-permute-start(bf16[128,768]{1,0:T(8,128)(2,1)S(1)} %join.8.own), channel_id=1, source_target_pairs={{4,6},{3,1},{12,14},{11,9},{20,22},{19,17},{28,30},{27,25}} | collective-permute-start | bytes 589832 | tf_op jit(solution)/shard_map/ppermute | solution.py:409
  11.7 0.0 collective-permute-done.refs_0_
  11.7 0.0 collective-permute-done.1.refs_1_
  11.8 0.0 collective-permute-done.2.refs_2_
  11.8 0.1 collective-permute-start.7
  11.9 0.5 %collective-permute-start.8 = (bf16[96,768]{1,0:T(8,128)(2,1)S(1)}, bf16[96,768]{1,0:T(8,128)(2,1)S(1)}, u32[]{:S(2)}, u32[]{:S(2)}) collective-permute-start(bf16[96,768]{1,0:T(8,128)(2,1)S(1)} %get-tuple-element.32), channel_id=1, source_target_pairs={{0,1},{1,0},{2,3},{3,2},{4,5},{5,4},{6,7},{7,6},{8,9},{9,8},{10,11... | collective-permute-start | bytes 442376 | tf_op jit(solution)/shard_map/ppermute | solution.py:404
  12.4 4.1 %collective-permute-start.6 = (bf16[192,768]{1,0:T(8,128)(2,1)S(1)}, bf16[192,768]{1,0:T(8,128)(2,1)S(1)}, u32[]{:S(2)}, u32[]{:S(2)}) collective-permute-start(bf16[192,768]{1,0:T(8,128)(2,1)S(1)} %join.7.far.whole.refs_0_.own), channel_id=1, source_target_pairs={{0,4},{4,6},{7,3},{3,1},{8,12},{12,14},{15,11},{11,9},{16,20},{20,... | collective-permute-start | bytes 884744 | tf_op jit(solution)/shard_map/ppermute | solution.py:409
  16.5 0.0 collective-permute-done.7.refs_0_
  16.5 0.0 collective-permute-done.8.refs_1_
  16.6 3.3 %collective-permute-start.9 = (bf16[192,768]{1,0:T(8,128)(2,1)S(1)}, bf16[192,768]{1,0:T(8,128)(2,1)S(1)}, u32[]{:S(2)}, u32[]{:S(2)}) collective-permute-start(bf16[192,768]{1,0:T(8,128)(2,1)S(1)} %join.9.refs_1_.own.refs_0_), channel_id=1, source_target_pairs={{0,4},{4,6},{7,3},{3,1},{8,12},{12,14},{15,11},{11,9},{16,20},{20,... | collective-permute-start | bytes 884744 | tf_op jit(solution)/shard_map/ppermute | solution.py:409
  20.0 0.7 %collective-permute-start.10 = (bf16[320,768]{1,0:T(8,128)(2,1)S(1)}, bf16[320,768]{1,0:T(8,128)(2,1)S(1)}, u32[]{:S(2)}, u32[]{:S(2)}) collective-permute-start(bf16[320,768]{1,0:T(8,128)(2,1)S(1)} %join.10), channel_id=1, source_target_pairs={{2,6},{5,1},{10,14},{13,9},{18,22},{21,17},{26,30},{29,25}} | collective-permute-start | bytes 1474568 | tf_op jit(solution)/shard_map/ppermute | solution.py:409
  20.7 0.0 collective-permute-done.4.over.over_near.came
  20.7 0.0 collective-permute-done.5.apart
  20.7 2.3 %first_kernel.1 = (bf16[2048,768]{1,0:T(8,128)(2,1)S(1)}, f32[256,896]{1,0:T(8,128)S(1)}, f32[256,896]{1,0:T(8,128)S(1)}, f32[2048,1]{1,0:T(8,128)S(1)}) custom-call(bf16[2048,768]{1,0:T(8,128)(2,1)} %table_from.1, bf16[64,768]{1,0:T(8,128)(2,1)S(1)} %get-tuple-element.23.refs_0_.near, bf16[192,768]{1,0:T(8,128)(2,1)S(1)} %join.7.far.whole.refs_0_.own, ...), custom_call_target="tpu_custom_call" | custom-call | flops 2147483648 | tf_op jit(solution)/shard_map/first_kernel/pallas_call | solution.py:420
  23.0 0.0 collective-permute-done.6.refs_0_.came
  23.0 1.9 %collective-permute-start.11 = (bf16[192,768]{1,0:T(8,128)(2,1)S(1)}, bf16[192,768]{1,0:T(8,128)(2,1)S(1)}, u32[]{:S(2)}, u32[]{:S(2)}) collective-permute-start(bf16[192,768]{1,0:T(8,128)(2,1)S(1)} %pick.3), channel_id=1, source_target_pairs={{0,2},{2,4},{4,6},{7,5},{5,3},{3,1},{8,10},{10,12},{12,14},{15,13}... | collective-permute-start | bytes 884744 | tf_op jit(solution)/shard_map/ppermute | solution.py:409
  25.0 0.0 collective-permute-done.9.refs_1_.came
  25.0 3.6 %collective-permute-start.12 = (bf16[192,768]{1,0:T(8,128)(2,1)S(1)}, bf16[192,768]{1,0:T(8,128)(2,1)S(1)}, u32[]{:S(2)}, u32[]{:S(2)}) collective-permute-start(bf16[192,768]{1,0:T(8,128)(2,1)S(1)} %pick.4), channel_id=1, source_target_pairs={{0,2},{2,4},{4,6},{7,5},{5,3},{3,1},{8,10},{10,12},{12,14},{15,13}... | collective-permute-start | bytes 884744 | tf_op jit(solution)/shard_map/ppermute | solution.py:409
  28.7 4.2 %collective-permute-start.15 = (bf16[128,768]{1,0:T(8,128)(2,1)S(1)}, bf16[128,768]{1,0:T(8,128)(2,1)S(1)}, u32[]{:S(2)}, u32[]{:S(2)}) collective-permute-start(bf16[128,768]{1,0:T(8,128)(2,1)S(1)} %pick.5), channel_id=1, source_target_pairs={{0,2},{2,4},{4,6},{7,5},{5,3},{3,1},{8,10},{10,12},{12,14},{15,13}... | collective-permute-start | bytes 589832 | tf_op jit(solution)/shard_map/ppermute | solution.py:409
  33.0 0.7 %collective-permute-start.17 = (bf16[64,768]{1,0:T(8,128)(2,1)S(1)}, bf16[64,768]{1,0:T(8,128)(2,1)S(1)}, u32[]{:S(2)}, u32[]{:S(2)}) collective-permute-start(bf16[64,768]{1,0:T(8,128)(2,1)S(1)} %join.12), channel_id=1, source_target_pairs={{2,6},{5,1},{10,14},{13,9},{18,22},{21,17},{26,30},{29,25}} | collective-permute-start | bytes 294920 | tf_op jit(solution)/shard_map/ppermute | solution.py:409
  33.6 1.9 %own_kernel.1 = (f32[256,896]{1,0:T(8,128)S(1)}, f32[256,896]{1,0:T(8,128)S(1)}) custom-call(bf16[2048,768]{1,0:T(8,128)(2,1)S(1)} %get-tuple-element.27.table, f32[2048,1]{1,0:T(8,128)S(1)} %get-tuple-element.28.half_norms, f32[256,896]{1,0:T(8,128)S(1)} %get-tuple-element.29.keep_in.after, ...), custom_call_target="tpu_custom_call", output_to_operand_aliasing={{0}: (2, {}), {1}: (3, {})} | custom-call | flops 268435456 | tf_op jit(solution)/shard_map/own_kernel/pallas_call | solution.py:420
  35.6 0.0 collective-permute-done.10.refs_0_
  35.6 0.2 step_kernel.3
  35.8 0.0 collective-permute-done.11.refs_0_
  35.8 0.2 step_kernel.4
  36.1 0.0 collective-permute-done.12.refs_0_
  36.1 0.2 step_kernel.5
  36.3 0.0 collective-permute-done.15.refs_1_
  36.4 2.4 %collective-permute-start.16 = (bf16[128,768]{1,0:T(8,128)(2,1)S(1)}, bf16[128,768]{1,0:T(8,128)(2,1)S(1)}, u32[]{:S(2)}, u32[]{:S(2)}) collective-permute-start(bf16[128,768]{1,0:T(8,128)(2,1)S(1)} %join.11.came), channel_id=1, source_target_pairs={{0,1},{1,0},{2,3},{3,2},{4,5},{5,4},{6,7},{7,6},{8,9},{9,8},{10,11... | collective-permute-start | bytes 589832 | tf_op jit(solution)/shard_map/ppermute | solution.py:404
  38.8 0.1 fusion
  38.8 0.1 collective-permute-start.13
  38.9 0.5 %collective-permute-start.14 = (f32[128,896]{1,0:T(8,128)S(1)}, f32[128,896]{1,0:T(8,128)S(1)}, u32[]{:S(2)}, u32[]{:S(2)}) collective-permute-start(f32[128,896]{1,0:T(8,128)S(1)} %get-tuple-element.41), channel_id=1, source_target_pairs={{0,1},{1,0},{2,3},{3,2},{4,5},{5,4},{6,7},{7,6},{8,9},{9,8},{10,11... | collective-permute-start | bytes 1376264 | tf_op jit(solution)/shard_map/ppermute | solution.py:404
  39.4 0.0 collective-permute-done.17.refs_1_
  39.4 0.4 collective-permute-start.18
  39.9 0.9 %collective-permute-done.13.refs_0_ = f32[128,896]{1,0:T(8,128)S(1)} collective-permute-done((f32[128,896]{1,0:T(8,128)S(1)}, f32[128,896]{1,0:T(8,128)S(1)}, u32[]{:S(2)}, u32[]{:S(2)}) %collective-permute-start.13) | collective-permute-done | bytes 458784 | tf_op jit(solution)/shard_map/ppermute | solution.py:404
  40.7 0.7 %collective-permute-done.14.refs_1_ = f32[128,896]{1,0:T(8,128)S(1)} collective-permute-done((f32[128,896]{1,0:T(8,128)S(1)}, f32[128,896]{1,0:T(8,128)S(1)}, u32[]{:S(2)}, u32[]{:S(2)}) %collective-permute-start.14) | collective-permute-done | bytes 458784 | tf_op jit(solution)/shard_map/ppermute | solution.py:404
  41.4 0.1 base_kernel.1.base
  41.5 0.0 collective-permute-done.18.refs_1_
  41.5 0.0 collective-permute-done.16.passed
  41.5 2.1 %refit_kernel.1 = bf16[256,768]{1,0:T(8,128)(2,1)} custom-call(bf16[2048,768]{1,0:T(8,128)(2,1)S(1)} %get-tuple-element.27.table, f32[2048,1]{1,0:T(8,128)S(1)} %get-tuple-element.28.half_norms, f32[256,896]{1,0:T(8,128)S(1)} %base_kernel.1.base, bf16[128,768]{1,0:T(8,128)(2,1)S(1)} %join.11.came, bf16[128,768]{1,0:T(8,128)(2,1)S(1)} %collective-permute-done.16.passed, ...), custom_call_target="tpu_custom_call" | custom-call | flops 268435456 | tf_op jit(solution)/shard_map/refit_kernel/pallas_call | solution.py:420
  (11 shorter events, 0.3 us)
Async XLA Ops:
  1.4 4.7 %collective-permute-start.3 = (bf16[64,768]{1,0:T(8,128)(2,1)S(1)}, bf16[64,768]{1,0:T(8,128)(2,1)S(1)}, u32[]{:S(2)}, u32[]{:S(2)}) collective-permute-start(bf16[64,768]{1,0:T(8,128)(2,1)S(1)} %get-tuple-element.23.refs_0_.near), channel_id=1, source_target_pairs={{0,1},{1,0},{2,3},{3,2},{4,5},{5,4},{6,7},{7,6},{8,9},{9,8},{10,11... | collective-permute-start | bytes 294920 | tf_op jit(solution)/shard_map/ppermute | solution.py:404
  2.0 9.8 %collective-permute-start = (bf16[64,768]{1,0:T(8,128)(2,1)S(1)}, bf16[64,768]{1,0:T(8,128)(2,1)S(1)}, u32[]{:S(2)}, u32[]{:S(2)}) collective-permute-start(bf16[64,768]{1,0:T(8,128)(2,1)S(1)} %get-tuple-element.24), channel_id=1, source_target_pairs={{0,24},{8,16},{16,8},{24,0},{1,25},{9,17},{17,9},{25,1},{2,26},{10... | collective-permute-start | bytes 294920 | tf_op jit(solution)/shard_map/ppermute | solution.py:440
  5.5 6.3 %collective-permute-start.1 = (bf16[64,768]{1,0:T(8,128)(2,1)S(1)}, bf16[64,768]{1,0:T(8,128)(2,1)S(1)}, u32[]{:S(2)}, u32[]{:S(2)}) collective-permute-start(bf16[64,768]{1,0:T(8,128)(2,1)S(1)} %get-tuple-element.25), channel_id=1, source_target_pairs={{0,16},{8,24},{16,0},{24,8},{1,17},{9,25},{17,1},{25,9},{2,18},{10... | collective-permute-start | bytes 294920 | tf_op jit(solution)/shard_map/ppermute | solution.py:440
  6.0 5.8 %collective-permute-start.2 = (bf16[64,768]{1,0:T(8,128)(2,1)S(1)}, bf16[64,768]{1,0:T(8,128)(2,1)S(1)}, u32[]{:S(2)}, u32[]{:S(2)}) collective-permute-start(bf16[64,768]{1,0:T(8,128)(2,1)S(1)} %get-tuple-element.26), channel_id=1, source_target_pairs={{0,8},{8,0},{16,24},{24,16},{1,9},{9,1},{17,25},{25,17},{2,10},{10... | collective-permute-start | bytes 294920 | tf_op jit(solution)/shard_map/ppermute | solution.py:440
  6.1 14.5 %collective-permute-start.4 = (bf16[128,768]{1,0:T(8,128)(2,1)S(1)}, bf16[128,768]{1,0:T(8,128)(2,1)S(1)}, u32[]{:S(2)}, u32[]{:S(2)}) collective-permute-start(bf16[128,768]{1,0:T(8,128)(2,1)S(1)} %join.8.own), channel_id=1, source_target_pairs={{2,6},{0,4},{5,1},{7,3},{10,14},{8,12},{13,9},{15,11},{18,22},{16,... | collective-permute-start | bytes 589832 | tf_op jit(solution)/shard_map/ppermute | solution.py:409
  11.1 9.6 %collective-permute-start.5 = (bf16[128,768]{1,0:T(8,128)(2,1)S(1)}, bf16[128,768]{1,0:T(8,128)(2,1)S(1)}, u32[]{:S(2)}, u32[]{:S(2)}) collective-permute-start(bf16[128,768]{1,0:T(8,128)(2,1)S(1)} %join.8.own), channel_id=1, source_target_pairs={{4,6},{3,1},{12,14},{11,9},{20,22},{19,17},{28,30},{27,25}} | collective-permute-start | bytes 589832 | tf_op jit(solution)/shard_map/ppermute | solution.py:409
  11.8 4.7 %collective-permute-start.7 = (bf16[96,768]{1,0:T(8,128)(2,1)S(1)}, bf16[96,768]{1,0:T(8,128)(2,1)S(1)}, u32[]{:S(2)}, u32[]{:S(2)}) collective-permute-start(bf16[96,768]{1,0:T(8,128)(2,1)S(1)} %get-tuple-element.31), channel_id=1, source_target_pairs={{0,1},{1,0},{2,3},{3,2},{4,5},{5,4},{6,7},{7,6},{8,9},{9,8},{10,11... | collective-permute-start | bytes 442376 | tf_op jit(solution)/shard_map/ppermute | solution.py:404
  11.9 4.6 %collective-permute-start.8 = (bf16[96,768]{1,0:T(8,128)(2,1)S(1)}, bf16[96,768]{1,0:T(8,128)(2,1)S(1)}, u32[]{:S(2)}, u32[]{:S(2)}) collective-permute-start(bf16[96,768]{1,0:T(8,128)(2,1)S(1)} %get-tuple-element.32), channel_id=1, source_target_pairs={{0,1},{1,0},{2,3},{3,2},{4,5},{5,4},{6,7},{7,6},{8,9},{9,8},{10,11... | collective-permute-start | bytes 442376 | tf_op jit(solution)/shard_map/ppermute | solution.py:404
  12.4 10.6 %collective-permute-start.6 = (bf16[192,768]{1,0:T(8,128)(2,1)S(1)}, bf16[192,768]{1,0:T(8,128)(2,1)S(1)}, u32[]{:S(2)}, u32[]{:S(2)}) collective-permute-start(bf16[192,768]{1,0:T(8,128)(2,1)S(1)} %join.7.far.whole.refs_0_.own), channel_id=1, source_target_pairs={{0,4},{4,6},{7,3},{3,1},{8,12},{12,14},{15,11},{11,9},{16,20},{20,... | collective-permute-start | bytes 884744 | tf_op jit(solution)/shard_map/ppermute | solution.py:409
  16.6 8.4 %collective-permute-start.9 = (bf16[192,768]{1,0:T(8,128)(2,1)S(1)}, bf16[192,768]{1,0:T(8,128)(2,1)S(1)}, u32[]{:S(2)}, u32[]{:S(2)}) collective-permute-start(bf16[192,768]{1,0:T(8,128)(2,1)S(1)} %join.9.refs_1_.own.refs_0_), channel_id=1, source_target_pairs={{0,4},{4,6},{7,3},{3,1},{8,12},{12,14},{15,11},{11,9},{16,20},{20,... | collective-permute-start | bytes 884744 | tf_op jit(solution)/shard_map/ppermute | solution.py:409
  20.0 15.6 %collective-permute-start.10 = (bf16[320,768]{1,0:T(8,128)(2,1)S(1)}, bf16[320,768]{1,0:T(8,128)(2,1)S(1)}, u32[]{:S(2)}, u32[]{:S(2)}) collective-permute-start(bf16[320,768]{1,0:T(8,128)(2,1)S(1)} %join.10), channel_id=1, source_target_pairs={{2,6},{5,1},{10,14},{13,9},{18,22},{21,17},{26,30},{29,25}} | collective-permute-start | bytes 1474568 | tf_op jit(solution)/shard_map/ppermute | solution.py:409
  23.0 12.8 %collective-permute-start.11 = (bf16[192,768]{1,0:T(8,128)(2,1)S(1)}, bf16[192,768]{1,0:T(8,128)(2,1)S(1)}, u32[]{:S(2)}, u32[]{:S(2)}) collective-permute-start(bf16[192,768]{1,0:T(8,128)(2,1)S(1)} %pick.3), channel_id=1, source_target_pairs={{0,2},{2,4},{4,6},{7,5},{5,3},{3,1},{8,10},{10,12},{12,14},{15,13}... | collective-permute-start | bytes 884744 | tf_op jit(solution)/shard_map/ppermute | solution.py:409
  25.0 11.0 %collective-permute-start.12 = (bf16[192,768]{1,0:T(8,128)(2,1)S(1)}, bf16[192,768]{1,0:T(8,128)(2,1)S(1)}, u32[]{:S(2)}, u32[]{:S(2)}) collective-permute-start(bf16[192,768]{1,0:T(8,128)(2,1)S(1)} %pick.4), channel_id=1, source_target_pairs={{0,2},{2,4},{4,6},{7,5},{5,3},{3,1},{8,10},{10,12},{12,14},{15,13}... | collective-permute-start | bytes 884744 | tf_op jit(solution)/shard_map/ppermute | solution.py:409
  28.7 7.6 %collective-permute-start.15 = (bf16[128,768]{1,0:T(8,128)(2,1)S(1)}, bf16[128,768]{1,0:T(8,128)(2,1)S(1)}, u32[]{:S(2)}, u32[]{:S(2)}) collective-permute-start(bf16[128,768]{1,0:T(8,128)(2,1)S(1)} %pick.5), channel_id=1, source_target_pairs={{0,2},{2,4},{4,6},{7,5},{5,3},{3,1},{8,10},{10,12},{12,14},{15,13}... | collective-permute-start | bytes 589832 | tf_op jit(solution)/shard_map/ppermute | solution.py:409
  33.0 6.5 %collective-permute-start.17 = (bf16[64,768]{1,0:T(8,128)(2,1)S(1)}, bf16[64,768]{1,0:T(8,128)(2,1)S(1)}, u32[]{:S(2)}, u32[]{:S(2)}) collective-permute-start(bf16[64,768]{1,0:T(8,128)(2,1)S(1)} %join.12), channel_id=1, source_target_pairs={{2,6},{5,1},{10,14},{13,9},{18,22},{21,17},{26,30},{29,25}} | collective-permute-start | bytes 294920 | tf_op jit(solution)/shard_map/ppermute | solution.py:409
  36.4 5.2 %collective-permute-start.16 = (bf16[128,768]{1,0:T(8,128)(2,1)S(1)}, bf16[128,768]{1,0:T(8,128)(2,1)S(1)}, u32[]{:S(2)}, u32[]{:S(2)}) collective-permute-start(bf16[128,768]{1,0:T(8,128)(2,1)S(1)} %join.11.came), channel_id=1, source_target_pairs={{0,1},{1,0},{2,3},{3,2},{4,5},{5,4},{6,7},{7,6},{8,9},{9,8},{10,11... | collective-permute-start | bytes 589832 | tf_op jit(solution)/shard_map/ppermute | solution.py:404
  38.8 1.9 %collective-permute-start.13 = (f32[128,896]{1,0:T(8,128)S(1)}, f32[128,896]{1,0:T(8,128)S(1)}, u32[]{:S(2)}, u32[]{:S(2)}) collective-permute-start(f32[128,896]{1,0:T(8,128)S(1)} %get-tuple-element.42), channel_id=1, source_target_pairs={{0,1},{1,0},{2,3},{3,2},{4,5},{5,4},{6,7},{7,6},{8,9},{9,8},{10,11... | collective-permute-start | bytes 1376264 | tf_op jit(solution)/shard_map/ppermute | solution.py:404
  38.9 2.5 %collective-permute-start.14 = (f32[128,896]{1,0:T(8,128)S(1)}, f32[128,896]{1,0:T(8,128)S(1)}, u32[]{:S(2)}, u32[]{:S(2)}) collective-permute-start(f32[128,896]{1,0:T(8,128)S(1)} %get-tuple-element.41), channel_id=1, source_target_pairs={{0,1},{1,0},{2,3},{3,2},{4,5},{5,4},{6,7},{7,6},{8,9},{9,8},{10,11... | collective-permute-start | bytes 1376264 | tf_op jit(solution)/shard_map/ppermute | solution.py:404
  39.4 2.1 %collective-permute-start.18 = (bf16[64,768]{1,0:T(8,128)(2,1)S(1)}, bf16[64,768]{1,0:T(8,128)(2,1)S(1)}, u32[]{:S(2)}, u32[]{:S(2)}) collective-permute-start(bf16[64,768]{1,0:T(8,128)(2,1)S(1)} %join.13.refs_0_), channel_id=1, source_target_pairs={{0,1},{1,0},{2,3},{3,2},{4,5},{5,4},{6,7},{7,6},{8,9},{9,8},{10,11... | collective-permute-start | bytes 294920 | tf_op jit(solution)/shard_map/ppermute | solution.py:404

commit v9 on v7

--- a/solution.py
+++ b/solution.py
@@ -159,9 +159,9 @@
 def pack_kernel(dest_from, points, *refs):
     packed, (dest, rows, dest_arrival, arrival) = refs[:-4], refs[-4:]
     dest_copy = pltpu.make_async_copy(dest_from, dest, dest_arrival)
-    dest_copy.start()
     copy = pltpu.make_async_copy(points, rows, arrival)
     copy.start()
+    dest_copy.start()
     count = len(packed)
     row_count = rows.shape[0]
     capacity = row_count // count

time: 43.5 us -> 43.5 us (level)
  no operation moved by 1% of the time
where the time goes in v9:
time: 43.5 us; the launch traced here: 43.2 us
  starting transfers between devices  32.8 us (75%)
  Pallas kernels  8.87 us (20%)
  waiting for transfers between devices  0.99 us (2%)
  between operations  0.49 us (1%)
    ppermute x9, starting transfers between devices, along(): return lax.ppermute(x, 'member', up + down)  24.8 us
    pallas_call x7, Pallas kernels, kernel(): pl.pallas_call(body, out_shape=out_shape, in_specs=list(specs) + [vmem()]...  7.19 us
    ppermute x3, starting transfers between devices, handoff(): lax.ppermute(packed[k], 'group', [(i, i ^ k) for i in range(group_count)])  4.16 us
    ppermute x7, starting transfers between devices, swap(): return lax.ppermute(x, 'member', [(i, i ^ 1) for i in range(member_count)])  3.83 us
    pallas_call x1, Pallas kernels, pack(): pl.pallas_call(pack_kernel, out_shape=[jax.ShapeDtypeStruct((capacity, fe...  1.41 us
    ppermute x7, waiting for transfers between devices, swap(): return lax.ppermute(x, 'member', [(i, i ^ 1) for i in range(member_count)])  0.96 us
  transfers between devices with their start and end apart: 19, of which 1 were waited for; matrix products, arithmetic and copies ran while one was open for 0% of the time, Pallas kernels for 12%

profile of v9, /device:TPU:0, one launch (start us, length us, event | category | flops | bytes accessed | tf_op | source)
XLA Modules:
  0.0 43.2 jit_solution(352786642932407014)
XLA Ops:
  0.0 1.4 %pack.1 = (bf16[64,768]{1,0:T(8,128)(2,1)S(1)}, bf16[64,768]{1,0:T(8,128)(2,1)S(1)}, bf16[64,768]{1,0:T(8,128)(2,1)S(1)}, bf16[64,768]{1,0:T(8,128)(2,1)S(1)}) custom-call(s32[1,256]{1,0:T(1,128)} %bitcast.1, bf16[256,768]{1,0:T(8,128)(2,1)} %points.1), custom_call_target="tpu_custom_call" | custom-call | flops 1048576 | tf_op jit(solution)/shard_map/pack/pallas_call | solution.py:190
  1.4 0.5 %collective-permute-start.3 = (bf16[64,768]{1,0:T(8,128)(2,1)S(1)}, bf16[64,768]{1,0:T(8,128)(2,1)S(1)}, u32[]{:S(2)}, u32[]{:S(2)}) collective-permute-start(bf16[64,768]{1,0:T(8,128)(2,1)S(1)} %get-tuple-element.23.refs_0_.near), channel_id=1, source_target_pairs={{0,1},{1,0},{2,3},{3,2},{4,5},{5,4},{6,7},{7,6},{8,9},{9,8},{10,11... | collective-permute-start | bytes 294920 | tf_op jit(solution)/shard_map/ppermute | solution.py:399
  1.9 3.5 %collective-permute-start = (bf16[64,768]{1,0:T(8,128)(2,1)S(1)}, bf16[64,768]{1,0:T(8,128)(2,1)S(1)}, u32[]{:S(2)}, u32[]{:S(2)}) collective-permute-start(bf16[64,768]{1,0:T(8,128)(2,1)S(1)} %get-tuple-element.24), channel_id=1, source_target_pairs={{0,24},{8,16},{16,8},{24,0},{1,25},{9,17},{17,9},{25,1},{2,26},{10... | collective-permute-start | bytes 294920 | tf_op jit(solution)/shard_map/ppermute | solution.py:435
  5.5 0.5 %collective-permute-start.1 = (bf16[64,768]{1,0:T(8,128)(2,1)S(1)}, bf16[64,768]{1,0:T(8,128)(2,1)S(1)}, u32[]{:S(2)}, u32[]{:S(2)}) collective-permute-start(bf16[64,768]{1,0:T(8,128)(2,1)S(1)} %get-tuple-element.25), channel_id=1, source_target_pairs={{0,16},{8,24},{16,0},{24,8},{1,17},{9,25},{17,1},{25,9},{2,18},{10... | collective-permute-start | bytes 294920 | tf_op jit(solution)/shard_map/ppermute | solution.py:435
  6.0 0.1 collective-permute-start.2
  6.1 0.0 collective-permute-done.3.refs_1_
  6.1 4.9 %collective-permute-start.4 = (bf16[128,768]{1,0:T(8,128)(2,1)S(1)}, bf16[128,768]{1,0:T(8,128)(2,1)S(1)}, u32[]{:S(2)}, u32[]{:S(2)}) collective-permute-start(bf16[128,768]{1,0:T(8,128)(2,1)S(1)} %join.8.own), channel_id=1, source_target_pairs={{2,6},{0,4},{5,1},{7,3},{10,14},{8,12},{13,9},{15,11},{18,22},{16,... | collective-permute-start | bytes 589832 | tf_op jit(solution)/shard_map/ppermute | solution.py:404
  11.0 0.7 %collective-permute-start.5 = (bf16[128,768]{1,0:T(8,128)(2,1)S(1)}, bf16[128,768]{1,0:T(8,128)(2,1)S(1)}, u32[]{:S(2)}, u32[]{:S(2)}) collective-permute-start(bf16[128,768]{1,0:T(8,128)(2,1)S(1)} %join.8.own), channel_id=1, source_target_pairs={{4,6},{3,1},{12,14},{11,9},{20,22},{19,17},{28,30},{27,25}} | collective-permute-start | bytes 589832 | tf_op jit(solution)/shard_map/ppermute | solution.py:404
  11.7 0.0 collective-permute-done.refs_0_
  11.7 0.0 collective-permute-done.1.refs_1_
  11.7 0.0 collective-permute-done.2.refs_2_
  11.8 0.1 collective-permute-start.7
  11.9 0.5 %collective-permute-start.8 = (bf16[96,768]{1,0:T(8,128)(2,1)S(1)}, bf16[96,768]{1,0:T(8,128)(2,1)S(1)}, u32[]{:S(2)}, u32[]{:S(2)}) collective-permute-start(bf16[96,768]{1,0:T(8,128)(2,1)S(1)} %get-tuple-element.32), channel_id=1, source_target_pairs={{0,1},{1,0},{2,3},{3,2},{4,5},{5,4},{6,7},{7,6},{8,9},{9,8},{10,11... | collective-permute-start | bytes 442376 | tf_op jit(solution)/shard_map/ppermute | solution.py:399
  12.4 4.1 %collective-permute-start.6 = (bf16[192,768]{1,0:T(8,128)(2,1)S(1)}, bf16[192,768]{1,0:T(8,128)(2,1)S(1)}, u32[]{:S(2)}, u32[]{:S(2)}) collective-permute-start(bf16[192,768]{1,0:T(8,128)(2,1)S(1)} %join.7.far.whole.refs_0_.own), channel_id=1, source_target_pairs={{0,4},{4,6},{7,3},{3,1},{8,12},{12,14},{15,11},{11,9},{16,20},{20,... | collective-permute-start | bytes 884744 | tf_op jit(solution)/shard_map/ppermute | solution.py:404
  16.5 0.0 collective-permute-done.7.refs_0_
  16.5 0.0 collective-permute-done.8.refs_1_
  16.5 3.3 %collective-permute-start.9 = (bf16[192,768]{1,0:T(8,128)(2,1)S(1)}, bf16[192,768]{1,0:T(8,128)(2,1)S(1)}, u32[]{:S(2)}, u32[]{:S(2)}) collective-permute-start(bf16[192,768]{1,0:T(8,128)(2,1)S(1)} %join.9.refs_1_.own.refs_0_), channel_id=1, source_target_pairs={{0,4},{4,6},{7,3},{3,1},{8,12},{12,14},{15,11},{11,9},{16,20},{20,... | collective-permute-start | bytes 884744 | tf_op jit(solution)/shard_map/ppermute | solution.py:404
  19.9 0.7 %collective-permute-start.10 = (bf16[256,768]{1,0:T(8,128)(2,1)S(1)}, bf16[256,768]{1,0:T(8,128)(2,1)S(1)}, u32[]{:S(2)}, u32[]{:S(2)}) collective-permute-start(bf16[256,768]{1,0:T(8,128)(2,1)S(1)} %join.10), channel_id=1, source_target_pairs={{2,6},{5,1},{10,14},{13,9},{18,22},{21,17},{26,30},{29,25}} | collective-permute-start | bytes 1179656 | tf_op jit(solution)/shard_map/ppermute | solution.py:404
  20.6 0.0 collective-permute-done.4.over.over_near.came
  20.6 0.0 collective-permute-done.5.apart
  20.7 2.3 %first_kernel.1 = (bf16[2048,768]{1,0:T(8,128)(2,1)S(1)}, f32[256,896]{1,0:T(8,128)S(1)}, f32[256,896]{1,0:T(8,128)S(1)}, f32[2048,1]{1,0:T(8,128)S(1)}) custom-call(bf16[2048,768]{1,0:T(8,128)(2,1)} %table_from.1, bf16[64,768]{1,0:T(8,128)(2,1)S(1)} %get-tuple-element.23.refs_0_.near, bf16[192,768]{1,0:T(8,128)(2,1)S(1)} %join.7.far.whole.refs_0_.own, ...), custom_call_target="tpu_custom_call" | custom-call | flops 2147483648 | tf_op jit(solution)/shard_map/first_kernel/pallas_call | solution.py:415
  23.0 0.0 collective-permute-done.6.refs_0_.came
  23.0 1.9 %collective-permute-start.11 = (bf16[192,768]{1,0:T(8,128)(2,1)S(1)}, bf16[192,768]{1,0:T(8,128)(2,1)S(1)}, u32[]{:S(2)}, u32[]{:S(2)}) collective-permute-start(bf16[192,768]{1,0:T(8,128)(2,1)S(1)} %pick.3), channel_id=1, source_target_pairs={{0,2},{2,4},{4,6},{7,5},{5,3},{3,1},{8,10},{10,12},{12,14},{15,13}... | collective-permute-start | bytes 884744 | tf_op jit(solution)/shard_map/ppermute | solution.py:404
  24.9 0.0 collective-permute-done.9.refs_1_.came
  25.0 3.6 %collective-permute-start.12 = (bf16[192,768]{1,0:T(8,128)(2,1)S(1)}, bf16[192,768]{1,0:T(8,128)(2,1)S(1)}, u32[]{:S(2)}, u32[]{:S(2)}) collective-permute-start(bf16[192,768]{1,0:T(8,128)(2,1)S(1)} %pick.4), channel_id=1, source_target_pairs={{0,2},{2,4},{4,6},{7,5},{5,3},{3,1},{8,10},{10,12},{12,14},{15,13}... | collective-permute-start | bytes 884744 | tf_op jit(solution)/shard_map/ppermute | solution.py:404
  28.7 0.7 %collective-permute-start.17 = (bf16[128,768]{1,0:T(8,128)(2,1)S(1)}, bf16[128,768]{1,0:T(8,128)(2,1)S(1)}, u32[]{:S(2)}, u32[]{:S(2)}) collective-permute-start(bf16[128,768]{1,0:T(8,128)(2,1)S(1)} %join.12), channel_id=1, source_target_pairs={{2,6},{5,1},{10,14},{13,9},{18,22},{21,17},{26,30},{29,25}} | collective-permute-start | bytes 589832 | tf_op jit(solution)/shard_map/ppermute | solution.py:404
  29.4 4.9 %collective-permute-start.15 = (bf16[128,768]{1,0:T(8,128)(2,1)S(1)}, bf16[128,768]{1,0:T(8,128)(2,1)S(1)}, u32[]{:S(2)}, u32[]{:S(2)}) collective-permute-start(bf16[128,768]{1,0:T(8,128)(2,1)S(1)} %pick.5), channel_id=1, source_target_pairs={{0,2},{2,4},{4,6},{7,5},{5,3},{3,1},{8,10},{10,12},{12,14},{15,13}... | collective-permute-start | bytes 589832 | tf_op jit(solution)/shard_map/ppermute | solution.py:404
  34.3 1.9 %own_kernel.1 = (f32[256,896]{1,0:T(8,128)S(1)}, f32[256,896]{1,0:T(8,128)S(1)}) custom-call(bf16[2048,768]{1,0:T(8,128)(2,1)S(1)} %get-tuple-element.27.table, f32[2048,1]{1,0:T(8,128)S(1)} %get-tuple-element.28.half_norms, f32[256,896]{1,0:T(8,128)S(1)} %get-tuple-element.29.keep_in.after, ...), custom_call_target="tpu_custom_call", output_to_operand_aliasing={{0}: (2, {}), {1}: (3, {})} | custom-call | flops 268435456 | tf_op jit(solution)/shard_map/own_kernel/pallas_call | solution.py:415
  36.2 0.0 collective-permute-done.10.refs_0_
  36.2 0.2 step_kernel.3
  36.4 0.0 collective-permute-done.11.refs_0_
  36.4 0.2 step_kernel.4
  36.7 0.0 collective-permute-done.12.refs_0_
  36.7 0.2 step_kernel.5
  37.0 0.1 fusion
  37.0 0.3 collective-permute-start.13
  37.4 0.2 collective-permute-start.14
  37.6 0.0 collective-permute-done.17.refs_1_
  37.6 0.3 collective-permute-start.18
  38.0 0.0 collective-permute-done.15.refs_1_
  38.0 1.8 %collective-permute-start.16 = (bf16[128,768]{1,0:T(8,128)(2,1)S(1)}, bf16[128,768]{1,0:T(8,128)(2,1)S(1)}, u32[]{:S(2)}, u32[]{:S(2)}) collective-permute-start(bf16[128,768]{1,0:T(8,128)(2,1)S(1)} %join.11.came), channel_id=1, source_target_pairs={{0,1},{1,0},{2,3},{3,2},{4,5},{5,4},{6,7},{7,6},{8,9},{9,8},{10,11... | collective-permute-start | bytes 589832 | tf_op jit(solution)/shard_map/ppermute | solution.py:399
  39.8 0.0 collective-permute-done.13.refs_0_
  39.8 0.0 collective-permute-done.14.refs_1_
  39.8 0.1 base_kernel.1.base
  39.9 0.0 collective-permute-done.18.refs_1_
  39.9 0.9 %collective-permute-done.16.passed = bf16[128,768]{1,0:T(8,128)(2,1)S(1)} collective-permute-done((bf16[128,768]{1,0:T(8,128)(2,1)S(1)}, bf16[128,768]{1,0:T(8,128)(2,1)S(1)}, u32[]{:S(2)}, u32[]{:S(2)}) %collective-permute-start.16) | collective-permute-done | bytes 196640 | tf_op jit(solution)/shard_map/ppermute | solution.py:399
  40.9 2.2 %refit_kernel.1 = bf16[256,768]{1,0:T(8,128)(2,1)} custom-call(bf16[2048,768]{1,0:T(8,128)(2,1)S(1)} %get-tuple-element.27.table, f32[2048,1]{1,0:T(8,128)S(1)} %get-tuple-element.28.half_norms, f32[256,896]{1,0:T(8,128)S(1)} %base_kernel.1.base, bf16[128,768]{1,0:T(8,128)(2,1)S(1)} %join.11.came, bf16[128,768]{1,0:T(8,128)(2,1)S(1)} %collective-permute-done.16.passed, ...), custom_call_target="tpu_custom_call" | custom-call | flops 268435456 | tf_op jit(solution)/shard_map/refit_kernel/pallas_call | solution.py:415
  (11 shorter events, 0.3 us)
Async XLA Ops:
  1.4 4.7 %collective-permute-start.3 = (bf16[64,768]{1,0:T(8,128)(2,1)S(1)}, bf16[64,768]{1,0:T(8,128)(2,1)S(1)}, u32[]{:S(2)}, u32[]{:S(2)}) collective-permute-start(bf16[64,768]{1,0:T(8,128)(2,1)S(1)} %get-tuple-element.23.refs_0_.near), channel_id=1, source_target_pairs={{0,1},{1,0},{2,3},{3,2},{4,5},{5,4},{6,7},{7,6},{8,9},{9,8},{10,11... | collective-permute-start | bytes 294920 | tf_op jit(solution)/shard_map/ppermute | solution.py:399
  1.9 9.8 %collective-permute-start = (bf16[64,768]{1,0:T(8,128)(2,1)S(1)}, bf16[64,768]{1,0:T(8,128)(2,1)S(1)}, u32[]{:S(2)}, u32[]{:S(2)}) collective-permute-start(bf16[64,768]{1,0:T(8,128)(2,1)S(1)} %get-tuple-element.24), channel_id=1, source_target_pairs={{0,24},{8,16},{16,8},{24,0},{1,25},{9,17},{17,9},{25,1},{2,26},{10... | collective-permute-start | bytes 294920 | tf_op jit(solution)/shard_map/ppermute | solution.py:435
  5.5 6.3 %collective-permute-start.1 = (bf16[64,768]{1,0:T(8,128)(2,1)S(1)}, bf16[64,768]{1,0:T(8,128)(2,1)S(1)}, u32[]{:S(2)}, u32[]{:S(2)}) collective-permute-start(bf16[64,768]{1,0:T(8,128)(2,1)S(1)} %get-tuple-element.25), channel_id=1, source_target_pairs={{0,16},{8,24},{16,0},{24,8},{1,17},{9,25},{17,1},{25,9},{2,18},{10... | collective-permute-start | bytes 294920 | tf_op jit(solution)/shard_map/ppermute | solution.py:435
  6.0 5.8 %collective-permute-start.2 = (bf16[64,768]{1,0:T(8,128)(2,1)S(1)}, bf16[64,768]{1,0:T(8,128)(2,1)S(1)}, u32[]{:S(2)}, u32[]{:S(2)}) collective-permute-start(bf16[64,768]{1,0:T(8,128)(2,1)S(1)} %get-tuple-element.26), channel_id=1, source_target_pairs={{0,8},{8,0},{16,24},{24,16},{1,9},{9,1},{17,25},{25,17},{2,10},{10... | collective-permute-start | bytes 294920 | tf_op jit(solution)/shard_map/ppermute | solution.py:435
  6.1 14.5 %collective-permute-start.4 = (bf16[128,768]{1,0:T(8,128)(2,1)S(1)}, bf16[128,768]{1,0:T(8,128)(2,1)S(1)}, u32[]{:S(2)}, u32[]{:S(2)}) collective-permute-start(bf16[128,768]{1,0:T(8,128)(2,1)S(1)} %join.8.own), channel_id=1, source_target_pairs={{2,6},{0,4},{5,1},{7,3},{10,14},{8,12},{13,9},{15,11},{18,22},{16,... | collective-permute-start | bytes 589832 | tf_op jit(solution)/shard_map/ppermute | solution.py:404
  11.0 9.6 %collective-permute-start.5 = (bf16[128,768]{1,0:T(8,128)(2,1)S(1)}, bf16[128,768]{1,0:T(8,128)(2,1)S(1)}, u32[]{:S(2)}, u32[]{:S(2)}) collective-permute-start(bf16[128,768]{1,0:T(8,128)(2,1)S(1)} %join.8.own), channel_id=1, source_target_pairs={{4,6},{3,1},{12,14},{11,9},{20,22},{19,17},{28,30},{27,25}} | collective-permute-start | bytes 589832 | tf_op jit(solution)/shard_map/ppermute | solution.py:404
  11.8 4.7 %collective-permute-start.7 = (bf16[96,768]{1,0:T(8,128)(2,1)S(1)}, bf16[96,768]{1,0:T(8,128)(2,1)S(1)}, u32[]{:S(2)}, u32[]{:S(2)}) collective-permute-start(bf16[96,768]{1,0:T(8,128)(2,1)S(1)} %get-tuple-element.31), channel_id=1, source_target_pairs={{0,1},{1,0},{2,3},{3,2},{4,5},{5,4},{6,7},{7,6},{8,9},{9,8},{10,11... | collective-permute-start | bytes 442376 | tf_op jit(solution)/shard_map/ppermute | solution.py:399
  11.9 4.6 %collective-permute-start.8 = (bf16[96,768]{1,0:T(8,128)(2,1)S(1)}, bf16[96,768]{1,0:T(8,128)(2,1)S(1)}, u32[]{:S(2)}, u32[]{:S(2)}) collective-permute-start(bf16[96,768]{1,0:T(8,128)(2,1)S(1)} %get-tuple-element.32), channel_id=1, source_target_pairs={{0,1},{1,0},{2,3},{3,2},{4,5},{5,4},{6,7},{7,6},{8,9},{9,8},{10,11... | collective-permute-start | bytes 442376 | tf_op jit(solution)/shard_map/ppermute | solution.py:399
  12.4 10.6 %collective-permute-start.6 = (bf16[192,768]{1,0:T(8,128)(2,1)S(1)}, bf16[192,768]{1,0:T(8,128)(2,1)S(1)}, u32[]{:S(2)}, u32[]{:S(2)}) collective-permute-start(bf16[192,768]{1,0:T(8,128)(2,1)S(1)} %join.7.far.whole.refs_0_.own), channel_id=1, source_target_pairs={{0,4},{4,6},{7,3},{3,1},{8,12},{12,14},{15,11},{11,9},{16,20},{20,... | collective-permute-start | bytes 884744 | tf_op jit(solution)/shard_map/ppermute | solution.py:404
  16.5 8.4 %collective-permute-start.9 = (bf16[192,768]{1,0:T(8,128)(2,1)S(1)}, bf16[192,768]{1,0:T(8,128)(2,1)S(1)}, u32[]{:S(2)}, u32[]{:S(2)}) collective-permute-start(bf16[192,768]{1,0:T(8,128)(2,1)S(1)} %join.9.refs_1_.own.refs_0_), channel_id=1, source_target_pairs={{0,4},{4,6},{7,3},{3,1},{8,12},{12,14},{15,11},{11,9},{16,20},{20,... | collective-permute-start | bytes 884744 | tf_op jit(solution)/shard_map/ppermute | solution.py:404
  19.9 16.2 %collective-permute-start.10 = (bf16[256,768]{1,0:T(8,128)(2,1)S(1)}, bf16[256,768]{1,0:T(8,128)(2,1)S(1)}, u32[]{:S(2)}, u32[]{:S(2)}) collective-permute-start(bf16[256,768]{1,0:T(8,128)(2,1)S(1)} %join.10), channel_id=1, source_target_pairs={{2,6},{5,1},{10,14},{13,9},{18,22},{21,17},{26,30},{29,25}} | collective-permute-start | bytes 1179656 | tf_op jit(solution)/shard_map/ppermute | solution.py:404
  23.0 13.4 %collective-permute-start.11 = (bf16[192,768]{1,0:T(8,128)(2,1)S(1)}, bf16[192,768]{1,0:T(8,128)(2,1)S(1)}, u32[]{:S(2)}, u32[]{:S(2)}) collective-permute-start(bf16[192,768]{1,0:T(8,128)(2,1)S(1)} %pick.3), channel_id=1, source_target_pairs={{0,2},{2,4},{4,6},{7,5},{5,3},{3,1},{8,10},{10,12},{12,14},{15,13}... | collective-permute-start | bytes 884744 | tf_op jit(solution)/shard_map/ppermute | solution.py:404
  25.0 11.7 %collective-permute-start.12 = (bf16[192,768]{1,0:T(8,128)(2,1)S(1)}, bf16[192,768]{1,0:T(8,128)(2,1)S(1)}, u32[]{:S(2)}, u32[]{:S(2)}) collective-permute-start(bf16[192,768]{1,0:T(8,128)(2,1)S(1)} %pick.4), channel_id=1, source_target_pairs={{0,2},{2,4},{4,6},{7,5},{5,3},{3,1},{8,10},{10,12},{12,14},{15,13}... | collective-permute-start | bytes 884744 | tf_op jit(solution)/shard_map/ppermute | solution.py:404
  28.7 9.0 %collective-permute-start.17 = (bf16[128,768]{1,0:T(8,128)(2,1)S(1)}, bf16[128,768]{1,0:T(8,128)(2,1)S(1)}, u32[]{:S(2)}, u32[]{:S(2)}) collective-permute-start(bf16[128,768]{1,0:T(8,128)(2,1)S(1)} %join.12), channel_id=1, source_target_pairs={{2,6},{5,1},{10,14},{13,9},{18,22},{21,17},{26,30},{29,25}} | collective-permute-start | bytes 589832 | tf_op jit(solution)/shard_map/ppermute | solution.py:404
  29.4 8.6 %collective-permute-start.15 = (bf16[128,768]{1,0:T(8,128)(2,1)S(1)}, bf16[128,768]{1,0:T(8,128)(2,1)S(1)}, u32[]{:S(2)}, u32[]{:S(2)}) collective-permute-start(bf16[128,768]{1,0:T(8,128)(2,1)S(1)} %pick.5), channel_id=1, source_target_pairs={{0,2},{2,4},{4,6},{7,5},{5,3},{3,1},{8,10},{10,12},{12,14},{15,13}... | collective-permute-start | bytes 589832 | tf_op jit(solution)/shard_map/ppermute | solution.py:404
  37.0 2.8 %collective-permute-start.13 = (f32[128,896]{1,0:T(8,128)S(1)}, f32[128,896]{1,0:T(8,128)S(1)}, u32[]{:S(2)}, u32[]{:S(2)}) collective-permute-start(f32[128,896]{1,0:T(8,128)S(1)} %get-tuple-element.42), channel_id=1, source_target_pairs={{0,1},{1,0},{2,3},{3,2},{4,5},{5,4},{6,7},{7,6},{8,9},{9,8},{10,11... | collective-permute-start | bytes 1376264 | tf_op jit(solution)/shard_map/ppermute | solution.py:399
  37.4 2.5 %collective-permute-start.14 = (f32[128,896]{1,0:T(8,128)S(1)}, f32[128,896]{1,0:T(8,128)S(1)}, u32[]{:S(2)}, u32[]{:S(2)}) collective-permute-start(f32[128,896]{1,0:T(8,128)S(1)} %get-tuple-element.41), channel_id=1, source_target_pairs={{0,1},{1,0},{2,3},{3,2},{4,5},{5,4},{6,7},{7,6},{8,9},{9,8},{10,11... | collective-permute-start | bytes 1376264 | tf_op jit(solution)/shard_map/ppermute | solution.py:399
  37.6 2.3 %collective-permute-start.18 = (bf16[128,768]{1,0:T(8,128)(2,1)S(1)}, bf16[128,768]{1,0:T(8,128)(2,1)S(1)}, u32[]{:S(2)}, u32[]{:S(2)}) collective-permute-start(bf16[128,768]{1,0:T(8,128)(2,1)S(1)} %join.13.refs_0_), channel_id=1, source_target_pairs={{0,1},{1,0},{2,3},{3,2},{4,5},{5,4},{6,7},{7,6},{8,9},{9,8},{10,11... | collective-permute-start | bytes 589832 | tf_op jit(solution)/shard_map/ppermute | solution.py:399
  38.0 2.9 %collective-permute-start.16 = (bf16[128,768]{1,0:T(8,128)(2,1)S(1)}, bf16[128,768]{1,0:T(8,128)(2,1)S(1)}, u32[]{:S(2)}, u32[]{:S(2)}) collective-permute-start(bf16[128,768]{1,0:T(8,128)(2,1)S(1)} %join.11.came), channel_id=1, source_target_pairs={{0,1},{1,0},{2,3},{3,2},{4,5},{5,4},{6,7},{7,6},{8,9},{9,8},{10,11... | collective-permute-start | bytes 589832 | tf_op jit(solution)/shard_map/ppermute | solution.py:399
